TPU v7x, 32 devices: a whole 2x2x4 slice. The times are simulated.
32 devices in a mesh: batch: 4 (over y, x), head: 8 (over z, core).
Axes of the slice: x: 2, y: 2, z: 4, core: 2. Of those that a mesh axis runs over, the one named last changes fastest.
Arguments:
- layer_source: bfloat16 [16384, 2048], P(('batch', 'head')), may hold values from -6 to 6
- piecewise_opening_memory: float32 [4, 32, 64, 64], P('batch', 'head'), may hold values from -18 to 18
- upstream_adjoint: bfloat16 [16384, 2048], P(('batch', 'head')), may hold values from -6 to 6
- earlier_layernorm_scale: float32 [2048], replicated, may hold values from 0.25 to 1.75
- earlier_layernorm_shift: float32 [2048], replicated, may hold values from -1.8 to 1.8
- accept_blend: float32 [2048], replicated, may hold values from 0 to 1
- lookup_blend: float32 [2048], replicated, may hold values from 0 to 1
- payload_blend: float32 [2048], replicated, may hold values from 0 to 1
- valve_blend: float32 [2048], replicated, may hold values from 0 to 1
- accept_weights: bfloat16 [2048, 2048], P('batch', 'head'), may hold values from -0.125 to 0.125
- lookup_weights: bfloat16 [2048, 2048], P('batch', 'head'), may hold values from -0.125 to 0.125
- payload_weights: bfloat16 [2048, 2048], P('batch', 'head'), may hold values from -0.125 to 0.125
- valve_weights: bfloat16 [2048, 2048], P('batch', 'head'), may hold values from -0.125 to 0.125
- forgetting_loglog: float32 [32, 64], P('head'), may hold values from -8 to -3.4
- diagonal_boost: float32 [32, 64], P('head'), may hold values from 0 to 1.5
- groupwise_scale: float32 [2048], P('head'), may hold values from 0.25 to 1.75
- groupwise_shift: float32 [2048], P('head'), may hold values from -1.8 to 1.8
- emission_weights: bfloat16 [2048, 2048], P('head', 'batch'), may hold values from -0.25 to 0.25
- later_layernorm_scale: float32 [2048], replicated, may hold values from 0.25 to 1.75
- later_layernorm_shift: float32 [2048], replicated, may hold values from -1.8 to 1.8
- feedforward_lookup_blend: float32 [2048], replicated, may hold values from 0 to 1
- feedforward_accept_blend: float32 [2048], replicated, may hold values from 0 to 1
- feedforward_lookup_weights: bfloat16 [2048, 7168], P('batch', 'head'), may hold values from -0.125 to 0.125
- feedforward_payload_weights: bfloat16 [7168, 2048], P('head', 'batch'), may hold values from -0.0625 to 0.0625
- feedforward_accept_weights: bfloat16 [2048, 2048], P('batch', 'head'), may hold values from -0.125 to 0.125
Outputs:
- block_out: bfloat16 [16384, 2048], P(('batch', 'head'))
- in_grad: float32 [16384, 2048], P(('batch', 'head'))
- initial_state_gradient: float32 [4, 32, 64, 64], P('batch', 'head')
- ln1_gain_grad: float32 [2048], replicated
- ln1_bias_grad: float32 [2048], replicated
- mix_r_grad: float32 [2048], replicated
- mix_k_grad: float32 [2048], replicated
- mix_v_grad: float32 [2048], replicated
- mix_g_grad: float32 [2048], replicated
- weight_r_grad: float32 [2048, 2048], P('batch', 'head')
- weight_k_grad: float32 [2048, 2048], P('batch', 'head')
- weight_v_grad: float32 [2048, 2048], P('batch', 'head')
- weight_g_grad: float32 [2048, 2048], P('batch', 'head')
- decay_grad: float32 [32, 64], P('head')
- diagonal_boost_deriv: float32 [32, 64], P('head')
- group_gain_grad: float32 [2048], P('head')
- group_bias_grad: float32 [2048], P('head')
- weight_o_grad: float32 [2048, 2048], P('head', 'batch')
- ln2_gain_grad: float32 [2048], replicated
- ln2_bias_grad: float32 [2048], replicated
- chan_mix_k_grad: float32 [2048], replicated
- chan_mix_r_grad: float32 [2048], replicated
- chan_key_grad: float32 [2048, 7168], P('batch', 'head')
- chan_value_grad: float32 [7168, 2048], P('head', 'batch')
- chan_recept_grad: float32 [2048, 2048], P('batch', 'head')
All inputs are finite; a program needn't handle non-finite values.
Results may differ from a plain program's by a relative error of at most 0.03.
Values may be sent and summed in bfloat16 or wider, within the bound.
A program may use at most 512 MiB of HBM per device.

v0:
```python
import jax
import jax.numpy as jnp
from jax import lax
from jax.sharding import PartitionSpec as P

ATTN_NUMBER = 32
ATTN_WIDTH = 64


ln_eps = 1e-05
gn_eps = 0.00064
highest = lax.Precision.HIGHEST


def plain_prod(left, right):
    return jnp.dot(left, right, preferred_element_type=jnp.float32)


def outer_grad(left, right):
    return lax.dot_general(
        left, right, (((0,), (0,)), ((), ())), preferred_element_type=jnp.float32
    )


def back_prod(left, right):
    return lax.dot_general(
        left, right, (((1,), (1,)), ((), ())), preferred_element_type=jnp.float32
    )


def layer_norm(payload_lines, gain, bias):
    center = payload_lines - jnp.mean(payload_lines, -1, keepdims=True)
    inv_scale = lax.rsqrt(jnp.mean(center * center, -1, keepdims=True) + ln_eps)
    normed = center * inv_scale
    return (normed * gain + bias, normed, inv_scale)


def norm_back(upstream_deriv, normed, inv_scale, gain):
    scaled = upstream_deriv * gain
    return inv_scale * (
        scaled
        - jnp.mean(scaled, -1, keepdims=True)
        - normed * jnp.mean(scaled * normed, -1, keepdims=True)
    )


def shift_down(payload_lines):
    return jnp.concatenate([jnp.zeros_like(payload_lines[:1]), payload_lines[:-1]], 0)


def shift_up(payload_lines):
    return jnp.concatenate([payload_lines[1:], jnp.zeros_like(payload_lines[:1])], 0)


def token_mix(current, earlier, weight):
    return (
        current.astype(jnp.float32) * weight + earlier.astype(jnp.float32) * (1.0 - weight)
    ).astype(jnp.bfloat16)


def make_mixes(current, earlier, accept_blend, lookup_blend, payload_blend, valve_blend):
    return (
        token_mix(current, earlier, accept_blend),
        token_mix(current, earlier, lookup_blend),
        token_mix(current, earlier, payload_blend),
        token_mix(current, earlier, valve_blend),
    )


def wkv_setup(forgetting_loglog, block_len):
    logarithm_retain = -jnp.exp(forgetting_loglog)
    positions = jnp.arange(block_len, dtype=jnp.float32)[:, None, None]
    attenuation_toward = jnp.exp(logarithm_retain * positions)
    attenuation_away = jnp.exp(-logarithm_retain * (positions + 1.0))
    fade_all = jnp.exp(logarithm_retain * block_len)
    return (logarithm_retain, positions, attenuation_toward, attenuation_away, fade_all)


def attention_recurrence_pieces(
    accept_lines, lookup_lines, payload_lines, forgetting_loglog, diagonal_boost
):
    block_len = accept_lines.shape[1]
    logarithm_retain, positions, attenuation_toward, attenuation_away, fade_all = wkv_setup(
        forgetting_loglog, block_len
    )
    queries = accept_lines * attenuation_toward
    keys_scaled = lookup_lines * attenuation_away
    causal_mask = (jnp.arange(block_len)[:, None] > jnp.arange(block_len)[None, :]).astype(
        jnp.float32
    )
    scores = jnp.einsum("cthi,cshi->chts", queries, keys_scaled, precision=highest) * causal_mask
    diagonal_addend = jnp.sum(accept_lines * diagonal_boost * lookup_lines, -1, keepdims=True)
    span_kv = jnp.einsum("cshi,cshj->chij", keys_scaled, payload_lines, precision=highest)
    return (
        logarithm_retain,
        positions,
        attenuation_toward,
        attenuation_away,
        fade_all,
        queries,
        keys_scaled,
        causal_mask,
        scores,
        diagonal_addend,
        span_kv,
    )


def weighted_key_value_forward(
    accept_lines, lookup_lines, payload_lines, forgetting_loglog, diagonal_boost, attn_memory
):
    (
        logarithm_retain,
        positions,
        attenuation_toward,
        attenuation_away,
        fade_all,
        queries,
        keys_scaled,
        causal_mask,
        scores,
        diagonal_addend,
        span_kv,
    ) = attention_recurrence_pieces(
        accept_lines, lookup_lines, payload_lines, forgetting_loglog, diagonal_boost
    )

    def advance(carried_memory, addition):
        return (fade_all[:, :, None] * (carried_memory + addition), carried_memory)

    final_state, beginning_locations = lax.scan(advance, attn_memory, span_kv)
    ultimate_answer = (
        jnp.einsum("chts,cshj->cthj", scores, payload_lines, precision=highest)
        + diagonal_addend * payload_lines
        + jnp.einsum("cthi,chij->cthj", queries, beginning_locations, precision=highest)
    )
    return (ultimate_answer, beginning_locations)


def weighted_key_value_backward(
    accept_lines,
    lookup_lines,
    payload_lines,
    forgetting_loglog,
    diagonal_boost,
    beginning_locations,
    upstream_deriv,
):
    (
        logarithm_retain,
        positions,
        attenuation_toward,
        attenuation_away,
        fade_all,
        queries,
        keys_scaled,
        causal_mask,
        scores,
        diagonal_addend,
        span_kv,
    ) = attention_recurrence_pieces(
        accept_lines, lookup_lines, payload_lines, forgetting_loglog, diagonal_boost
    )
    block_len = accept_lines.shape[1]
    state_terms = jnp.einsum("cthi,cthj->chij", queries, upstream_deriv, precision=highest)

    def retreat(carried_memory, addition):
        passed = fade_all[:, :, None] * carried_memory
        return (addition + passed, passed)

    initial_state_gradient, passes = lax.scan(
        retreat, jnp.zeros_like(beginning_locations[0]), state_terms, reverse=True
    )
    pairs = (
        jnp.einsum("cthj,cshj->chts", upstream_deriv, payload_lines, precision=highest)
        * causal_mask
    )
    accept_deriv_lines = jnp.einsum(
        "cthj,chij->cthi", upstream_deriv, beginning_locations, precision=highest
    ) + jnp.einsum("chts,cshi->cthi", pairs, keys_scaled, precision=highest)
    multiplied_deriv = jnp.einsum(
        "chts,cthi->cshi", pairs, queries, precision=highest
    ) + jnp.einsum("cshj,chij->cshi", payload_lines, passes, precision=highest)
    payload_deriv_lines = (
        jnp.einsum("chts,cthj->cshj", scores, upstream_deriv, precision=highest)
        + diagonal_addend * upstream_deriv
        + jnp.einsum("cshi,chij->cshj", keys_scaled, passes, precision=highest)
    )
    inner_pairings = jnp.sum(upstream_deriv * payload_lines, -1, keepdims=True)
    accept_deriv = (
        accept_deriv_lines * attenuation_toward + inner_pairings * diagonal_boost * lookup_lines
    )
    lookup_deriv_lines = (
        multiplied_deriv * attenuation_away + inner_pairings * diagonal_boost * accept_lines
    )
    diagonal_deriv_piece = jnp.sum(inner_pairings * accept_lines * lookup_lines, (0, 1))
    rate_gradient = (
        jnp.sum(positions * accept_deriv_lines * queries, (0, 1))
        - jnp.sum((positions + 1.0) * multiplied_deriv * keys_scaled, (0, 1))
        + block_len * jnp.sum(passes * (beginning_locations + span_kv), (0, 3))
    )
    return (
        accept_deriv,
        lookup_deriv_lines,
        payload_deriv_lines,
        rate_gradient * logarithm_retain,
        diagonal_deriv_piece,
        initial_state_gradient,
    )


def proj_back(mixed_now, grad_now, full_now, mix_now, spread, direct, delayed):
    weight_part = outer_grad(mixed_now, grad_now)
    grad_in = back_prod(grad_now, full_now)
    return (
        weight_part,
        direct + grad_in * mix_now,
        delayed + grad_in * (1.0 - mix_now),
        jnp.sum(grad_in * spread, 0),
    )


def location_share(part, total, offset):
    return lax.dynamic_update_slice_in_dim(
        jnp.zeros((total,) + part.shape[1:], jnp.float32), part, offset, 0
    )


def on_device(
    layer_source,
    piecewise_opening_memory,
    upstream_adjoint,
    earlier_layernorm_scale,
    earlier_layernorm_shift,
    accept_blend,
    lookup_blend,
    payload_blend,
    valve_blend,
    accept_weights,
    lookup_weights,
    payload_weights,
    valve_weights,
    forgetting_loglog,
    diagonal_boost,
    groupwise_scale,
    groupwise_shift,
    emission_weights,
    later_layernorm_scale,
    later_layernorm_shift,
    feedforward_lookup_blend,
    feedforward_accept_blend,
    feedforward_lookup_weights,
    feedforward_payload_weights,
    feedforward_accept_weights,
):
    full_r, full_k, full_v, full_g, full_o, full_ck, full_cv, full_cr = (
        lax.all_gather(accept_weights, "batch", axis=0, tiled=True),
        lax.all_gather(lookup_weights, "batch", axis=0, tiled=True),
        lax.all_gather(payload_weights, "batch", axis=0, tiled=True),
        lax.all_gather(valve_weights, "batch", axis=0, tiled=True),
        lax.all_gather(emission_weights, "batch", axis=1, tiled=True),
        lax.all_gather(feedforward_lookup_weights, "batch", axis=0, tiled=True),
        lax.all_gather(feedforward_payload_weights, "batch", axis=1, tiled=True),
        lax.all_gather(feedforward_accept_weights, "batch", axis=0, tiled=True),
    )
    residual = layer_source.astype(jnp.float32)
    normed1, hat1, inv1 = layer_norm(residual, earlier_layernorm_scale, earlier_layernorm_shift)
    local_x1 = normed1.astype(jnp.bfloat16)
    seq_x1 = lax.all_gather(local_x1, "head", axis=0, tiled=True)
    sequence_length = seq_x1.shape[0]
    prev_x1 = shift_down(seq_x1)
    mixed_r, mixed_k, mixed_v, mixed_g = make_mixes(
        seq_x1, prev_x1, accept_blend, lookup_blend, payload_blend, valve_blend
    )
    accept_lines = plain_prod(mixed_r, full_r).astype(jnp.bfloat16)
    key_projection = plain_prod(mixed_k, full_k).astype(jnp.bfloat16)
    value_projection = plain_prod(mixed_v, full_v).astype(jnp.bfloat16)
    gate_pre = plain_prod(mixed_g, full_g)
    gate = jax.nn.silu(gate_pre)
    resident_attns = accept_lines.shape[1] // ATTN_WIDTH
    block_len = min(64, sequence_length)
    block_count = sequence_length // block_len

    def block_list(tensor_entry):
        return tensor_entry.astype(jnp.float32).reshape(
            block_count, block_len, resident_attns, ATTN_WIDTH
        )

    wkv_out, beginning_locations = weighted_key_value_forward(
        block_list(accept_lines),
        block_list(key_projection),
        block_list(value_projection),
        forgetting_loglog,
        diagonal_boost,
        piecewise_opening_memory[0],
    )
    head_view = wkv_out.reshape(sequence_length, resident_attns, ATTN_WIDTH)
    center = head_view - jnp.mean(head_view, -1, keepdims=True)
    inv_group = lax.rsqrt(jnp.mean(center * center, -1, keepdims=True) + gn_eps)
    normed_heads = center * inv_group
    normed_flat = normed_heads.reshape(sequence_length, -1)
    grouped = normed_flat * groupwise_scale + groupwise_shift
    mixed_z = (grouped * gate).astype(jnp.bfloat16)
    whole_o = lax.all_gather(full_o, "head", axis=0, tiled=True)
    z_rows = lax.all_to_all(mixed_z, "head", split_axis=0, concat_axis=1, tiled=True)
    mixer = plain_prod(z_rows, whole_o)
    middle = residual + mixer
    normed2, hat2, inv2 = layer_norm(middle, later_layernorm_scale, later_layernorm_shift)
    seq_x2 = lax.all_gather(normed2.astype(jnp.bfloat16), "head", axis=0, tiled=True)
    prev_x2 = shift_down(seq_x2)
    mixed_ck = token_mix(seq_x2, prev_x2, feedforward_lookup_blend)
    mixed_cr = token_mix(seq_x2, prev_x2, feedforward_accept_blend)
    key_pre = plain_prod(mixed_ck, full_ck)
    key_sq = jnp.square(jax.nn.relu(key_pre)).astype(jnp.bfloat16)
    value_cols = lax.psum_scatter(
        plain_prod(key_sq, full_cv).astype(jnp.bfloat16), "head", scatter_dimension=1, tiled=True
    ).astype(jnp.float32)
    recept2 = plain_prod(mixed_cr, full_cr)
    sig_two = jax.nn.sigmoid(recept2)
    channel = lax.all_to_all(
        (sig_two * value_cols).astype(jnp.bfloat16), "head", split_axis=0, concat_axis=1, tiled=True
    ).astype(jnp.float32)
    block_out = (middle + channel).astype(jnp.bfloat16)
    cot_cols = lax.all_to_all(
        upstream_adjoint, "head", split_axis=1, concat_axis=0, tiled=True
    ).astype(jnp.float32)
    grad_value = (cot_cols * sig_two).astype(jnp.bfloat16)
    grad_r2 = (cot_cols * value_cols * sig_two * (1.0 - sig_two)).astype(jnp.bfloat16)
    width_full = full_cv.shape[1]
    piece = lax.all_gather(grad_value, "head", axis=1, tiled=True)
    acc_key = back_prod(piece, full_cv)
    acc_weight = outer_grad(key_sq, piece)
    grad_key_pre = (acc_key * 2.0 * jax.nn.relu(key_pre)).astype(jnp.bfloat16)
    chan_key_part = outer_grad(mixed_ck, grad_key_pre)
    chan_recept_part = outer_grad(mixed_cr, grad_r2)
    spread_two = seq_x2.astype(jnp.float32) - prev_x2.astype(jnp.float32)
    grad_ck = back_prod(grad_key_pre, full_ck)
    grad_cr = back_prod(grad_r2, full_cr)
    chan_mix_k_part = jnp.sum(grad_ck * spread_two, 0)
    chan_mix_r_part = jnp.sum(grad_cr * spread_two, 0)
    direct_two = grad_ck * feedforward_lookup_blend + grad_cr * feedforward_accept_blend
    delayed_two = grad_ck * (1.0 - feedforward_lookup_blend) + grad_cr * (
        1.0 - feedforward_accept_blend
    )
    grad_x2 = lax.psum_scatter(
        (direct_two + shift_up(delayed_two)).astype(jnp.bfloat16),
        "head",
        scatter_dimension=0,
        tiled=True,
    ).astype(jnp.float32)
    ln2_gain_part = jnp.sum(grad_x2 * hat2, 0)
    ln2_bias_part = jnp.sum(grad_x2, 0)
    grad_middle = upstream_adjoint.astype(jnp.float32) + norm_back(
        grad_x2, hat2, inv2, later_layernorm_scale
    )
    piece = lax.all_gather(grad_middle.astype(jnp.bfloat16), "head", axis=0, tiled=True)
    acc_z = back_prod(piece, full_o)
    acc_o = outer_grad(mixed_z, piece)
    grad_grouped = acc_z * gate
    sig_gate = jax.nn.sigmoid(gate_pre)
    grad_gate_pre = (acc_z * grouped * sig_gate * (1.0 + gate_pre * (1.0 - sig_gate))).astype(
        jnp.bfloat16
    )
    group_gain_part = jnp.sum(grad_grouped * normed_flat, 0)
    group_bias_part = jnp.sum(grad_grouped, 0)
    scaled_heads = (grad_grouped * groupwise_scale).reshape(
        sequence_length, resident_attns, ATTN_WIDTH
    )
    grad_wkv = inv_group * (
        scaled_heads
        - jnp.mean(scaled_heads, -1, keepdims=True)
        - normed_heads * jnp.mean(scaled_heads * normed_heads, -1, keepdims=True)
    )
    (
        accept_diag_deriv,
        lookup_diag_deriv,
        payload_diag_deriv,
        decay_portion,
        diagonal_boost_share,
        state_portion,
    ) = weighted_key_value_backward(
        block_list(accept_lines),
        block_list(key_projection),
        block_list(value_projection),
        forgetting_loglog,
        diagonal_boost,
        beginning_locations,
        grad_wkv.reshape(block_count, block_len, resident_attns, ATTN_WIDTH),
    )
    accept_deriv = accept_diag_deriv.reshape(sequence_length, -1).astype(jnp.bfloat16)
    lookup_deriv_lines = lookup_diag_deriv.reshape(sequence_length, -1).astype(jnp.bfloat16)
    payload_deriv_lines = payload_diag_deriv.reshape(sequence_length, -1).astype(jnp.bfloat16)
    back_r, back_k, back_v, back_g = (mixed_r, mixed_k, mixed_v, mixed_g)
    spread_one = seq_x1.astype(jnp.float32) - prev_x1.astype(jnp.float32)
    direct_one = jnp.zeros((sequence_length, width_full), jnp.float32)
    delayed_one = jnp.zeros((sequence_length, width_full), jnp.float32)
    weight_r_part, direct_one, delayed_one, mix_r_part = proj_back(
        back_r, accept_deriv, full_r, accept_blend, spread_one, direct_one, delayed_one
    )
    weight_k_part, direct_one, delayed_one, mix_k_part = proj_back(
        back_k, lookup_deriv_lines, full_k, lookup_blend, spread_one, direct_one, delayed_one
    )
    weight_v_part, direct_one, delayed_one, mix_v_part = proj_back(
        back_v, payload_deriv_lines, full_v, payload_blend, spread_one, direct_one, delayed_one
    )
    weight_g_part, direct_one, delayed_one, mix_g_part = proj_back(
        back_g, grad_gate_pre, full_g, valve_blend, spread_one, direct_one, delayed_one
    )
    grad_x1 = lax.psum_scatter(
        (direct_one + shift_up(delayed_one)).astype(jnp.bfloat16),
        "head",
        scatter_dimension=0,
        tiled=True,
    ).astype(jnp.float32)
    ln1_gain_part = jnp.sum(grad_x1 * hat1, 0)
    ln1_bias_part = jnp.sum(grad_x1, 0)
    in_grad = grad_middle + norm_back(grad_x1, hat1, inv1, earlier_layernorm_scale)
    (
        weight_r_grad,
        weight_k_grad,
        weight_v_grad,
        weight_g_grad,
        weight_o_grad,
        chan_key_grad,
        chan_value_grad,
        chan_recept_grad,
    ) = (
        lax.psum_scatter(
            weight_r_part.astype(jnp.bfloat16), "batch", scatter_dimension=0, tiled=True
        ).astype(jnp.float32),
        lax.psum_scatter(
            weight_k_part.astype(jnp.bfloat16), "batch", scatter_dimension=0, tiled=True
        ).astype(jnp.float32),
        lax.psum_scatter(
            weight_v_part.astype(jnp.bfloat16), "batch", scatter_dimension=0, tiled=True
        ).astype(jnp.float32),
        lax.psum_scatter(
            weight_g_part.astype(jnp.bfloat16), "batch", scatter_dimension=0, tiled=True
        ).astype(jnp.float32),
        lax.psum_scatter(
            acc_o.astype(jnp.bfloat16), "batch", scatter_dimension=1, tiled=True
        ).astype(jnp.float32),
        lax.psum_scatter(
            chan_key_part.astype(jnp.bfloat16), "batch", scatter_dimension=0, tiled=True
        ).astype(jnp.float32),
        lax.psum_scatter(
            acc_weight.astype(jnp.bfloat16), "batch", scatter_dimension=1, tiled=True
        ).astype(jnp.float32),
        lax.psum_scatter(
            chan_recept_part.astype(jnp.bfloat16), "batch", scatter_dimension=0, tiled=True
        ).astype(jnp.float32),
    )
    attn_slot_ordinal = lax.axis_index("head")
    width_here = groupwise_scale.shape[0]
    group_gain_full = location_share(group_gain_part, width_full, attn_slot_ordinal * width_here)
    group_bias_full = location_share(group_bias_part, width_full, attn_slot_ordinal * width_here)
    decay_full = location_share(decay_portion, ATTN_NUMBER, attn_slot_ordinal * resident_attns)
    diagonal_boost_full = location_share(
        diagonal_boost_share, ATTN_NUMBER, attn_slot_ordinal * resident_attns
    )
    (
        ln1_gain_grad,
        ln1_bias_grad,
        mix_r_grad,
        mix_k_grad,
        mix_v_grad,
        mix_g_grad,
        ln2_gain_grad,
        ln2_bias_grad,
        chan_mix_k_grad,
        chan_mix_r_grad,
        group_gain_sum,
        group_bias_sum,
        decay_sum,
        diagonal_boost_accum,
    ) = lax.psum(
        (
            ln1_gain_part,
            ln1_bias_part,
            mix_r_part,
            mix_k_part,
            mix_v_part,
            mix_g_part,
            ln2_gain_part,
            ln2_bias_part,
            chan_mix_k_part,
            chan_mix_r_part,
            group_gain_full,
            group_bias_full,
            decay_full,
            diagonal_boost_full,
        ),
        ("batch", "head"),
    )
    group_gain_grad = lax.dynamic_slice_in_dim(
        group_gain_sum, attn_slot_ordinal * width_here, width_here, 0
    )
    group_bias_grad = lax.dynamic_slice_in_dim(
        group_bias_sum, attn_slot_ordinal * width_here, width_here, 0
    )
    decay_grad = lax.dynamic_slice_in_dim(
        decay_sum, attn_slot_ordinal * resident_attns, resident_attns, 0
    )
    diagonal_boost_deriv = lax.dynamic_slice_in_dim(
        diagonal_boost_accum, attn_slot_ordinal * resident_attns, resident_attns, 0
    )
    return (
        block_out,
        in_grad,
        state_portion[None],
        ln1_gain_grad,
        ln1_bias_grad,
        mix_r_grad,
        mix_k_grad,
        mix_v_grad,
        mix_g_grad,
        weight_r_grad,
        weight_k_grad,
        weight_v_grad,
        weight_g_grad,
        decay_grad,
        diagonal_boost_deriv,
        group_gain_grad,
        group_bias_grad,
        weight_o_grad,
        ln2_gain_grad,
        ln2_bias_grad,
        chan_mix_k_grad,
        chan_mix_r_grad,
        chan_key_grad,
        chan_value_grad,
        chan_recept_grad,
    )


def solution(mesh):
    in_specs = (
        P(("batch", "head"), None),
        P("batch", "head", None, None),
        P(("batch", "head"), None),
        P(),
        P(),
        P(),
        P(),
        P(),
        P(),
        P("batch", "head"),
        P("batch", "head"),
        P("batch", "head"),
        P("batch", "head"),
        P("head", None),
        P("head", None),
        P("head"),
        P("head"),
        P("head", "batch"),
        P(),
        P(),
        P(),
        P(),
        P("batch", "head"),
        P("head", "batch"),
        P("batch", "head"),
    )
    out_specs = (
        P(("batch", "head"), None),
        P(("batch", "head"), None),
        P("batch", "head", None, None),
        P(),
        P(),
        P(),
        P(),
        P(),
        P(),
        P("batch", "head"),
        P("batch", "head"),
        P("batch", "head"),
        P("batch", "head"),
        P("head", None),
        P("head", None),
        P("head"),
        P("head"),
        P("head", "batch"),
        P(),
        P(),
        P(),
        P(),
        P("batch", "head"),
        P("head", "batch"),
        P("batch", "head"),
    )
    return jax.shard_map(
        on_device, mesh=mesh, in_specs=in_specs, out_specs=out_specs, check_vma=False
    )
```

profile of v0, /device:TPU:0, one launch (start us, length us, event | category | flops | bytes accessed | tf_op | source)
XLA Modules:
  0.0 2743.9 jit_solution(6763591294279218783)
XLA Ops:
  19.7 19.4 all-gather.24.cloned.1.call-done
  39.2 28.5 %all-gather.16.cloned.1.call-done = bf16[2048,256]{1,0:T(8,128)(2,1)} async-done(((bf16[512,256]{1,0:T(8,128)(2,1)}), bf16[2048,256]{1,0:T(8,128)(2,1)}) %all-gather.16.cloned.1.call-update) | async-done | bytes 1048592 | tf_op jit(solution)/shard_map/all_gather | solution.py:259
  67.7 153.3 %all-gather.14.cloned.1.call-done = bf16[4096,2048]{1,0:T(8,128)(2,1)} async-done(((bf16[512,2048]{1,0:T(8,128)(2,1)}), bf16[4096,2048]{1,0:T(8,128)(2,1)}) %all-gather.14.cloned.1.call-update) | async-done | bytes 16777232 | tf_op jit(solution)/shard_map/all_gather | solution.py:269
  221.0 21.5 convolution_convert_fusion.3
  253.0 22.9 fusion.44
  301.5 116.8 %while.29 = (s32[]{:T(128)}, f32[4,64,64]{2,1,0:T(8,128)S(1)}, f32[64,4,64,64]{3,2,1,0:T(8,128)}, f32[4,64]{1,0:T(4,128)S(1)}, f32[64,4,64,64]{2,3,1,0:T(8,128)}, /*index=5*/s32[]{:T(128)}) while((s32[]{:T(128)}, f32[4,64,64]{2,1,0:T(8,128)S(1)}, f32[64,4,64,64]{3,2,1,0:T(8,128)}, f32[4,64]{1,0:T(4,128)S(1)}, f32[64,4,64,64]{2,3,1,0:T(8,128)}, ...), condition=%wide.region_4.5_spmd, body=%wide.region_3.4_spmd.sunk | while | flops 32770 | bytes 656469 | solution.py:131
  418.4 23.4 fusion.45
  460.2 17.5 fusion.53
  477.6 16.6 fusion.54
  494.3 19.3 fusion.127
  555.1 25.0 multiply_convert_fusion.3
  589.4 48.2 %all-to-all-done = bf16[8,512,256]{1,2,0:T(8,128)(2,1)} async-done(((bf16[8,512,256]{1,2,0:T(8,128)(2,1)}), bf16[8,512,256]{1,2,0:T(8,128)(2,1)}, u32[]{:S(2)}, u32[]{:S(2)}) %all-to-all-start) | async-done | bytes 2097184 | tf_op jit(solution)/shard_map/all_to_all | solution.py:305
  651.5 148.7 %all-gather.28.cloned.1.call-done = bf16[4096,2048]{1,0:T(8,128)(2,1)} async-done(((bf16[512,2048]{1,0:T(8,128)(2,1)}), bf16[4096,2048]{1,0:T(8,128)(2,1)}) %all-gather.28.cloned.1.call-update) | async-done | bytes 16777232 | tf_op jit(solution)/shard_map/all_gather | solution.py:309
  800.2 29.8 %fusion.95 = f32[4096,896]{1,0:T(8,128)} fusion(bf16[2048,896]{1,0:T(8,128)(2,1)} %all-gather.32.cloned.1.call-done, bf16[4096,2048]{1,0:T(8,128)(2,1)} %all-gather.28.cloned.1.call-done, f32[2048]{0:T(1024)S(1)} %broadcast_subtract_fusion, f32[2048]{0:T(1024)S(1)} %copy-done.59, bf16[4095,2048]{1,0:T(8,128)(2,1)} %bitcast.162), kind=kOutput, calls=%fused_computation.183 | convolution fusion | flops 15082717184 | bytes 51916800 | tf_op jit(solution)/shard_map/dot_general | solution.py:16
  830.0 18.4 all-gather.34.cloned.1.call-done
  848.4 23.9 convolution_convert_fusion
  880.0 79.8 %all-to-all-done.2 = bf16[512,8,256]{2,0,1:T(8,128)(2,1)S(1)} async-done(((bf16[512,8,256]{2,0,1:T(8,128)(2,1)}), bf16[512,8,256]{2,0,1:T(8,128)(2,1)S(1)}, u32[]{:S(2)}, u32[]{:S(2)}) %all-to-all-start.2) | async-done | bytes 2097184 | tf_op jit(solution)/shard_map/all_to_all | solution.py:324
  961.2 114.5 %reduce-scatter.12.cloned.1.call-done = bf16[4096,256]{1,0:T(8,128)(2,1)} async-done(((bf16[4096,2048]{1,0:T(8,128)(2,1)}), bf16[4096,256]{1,0:T(8,128)(2,1)}) %reduce-scatter.12.cloned.1.call-update) | async-done | bytes 2097168 | tf_op jit(solution)/shard_map/reduce_scatter | solution.py:315
  1075.7 24.9 fusion.77
  1114.2 147.4 %all-gather.36.cloned.1.call-done = bf16[4096,2048]{1,0:T(8,128)(2,1)} async-done(((bf16[4096,256]{1,0:T(8,128)(2,1)}), bf16[4096,2048]{1,0:T(8,128)(2,1)}) %all-gather.36.cloned.1.call-update) | async-done | bytes 16777232 | tf_op jit(solution)/shard_map/all_gather | solution.py:330
  1261.6 23.6 multiply_convert_fusion
  1288.2 21.5 fusion.129
  1309.7 33.8 %fusion.16 = f32[4095,2048]{1,0:T(8,128)} fusion(f32[4096,2048]{1,0:T(8,128)} %fusion.130, f32[4096,2048]{1,0:T(8,128)} %fusion.129, f32[2048]{0:T(1024)S(1)} %broadcast_subtract_fusion.1, f32[2048]{0:T(1024)S(1)} %broadcast_subtract_fusion), kind=kLoop, calls=%fused_computation.41 | loop fusion | flops 25159680 | bytes 100655104 | tf_op jit(solution)/shard_map/add | solution.py:342
  1343.5 49.4 %multiply_reduce_fusion = (f32[2048]{0:T(1024)}, f32[2048]{0:T(1024)}, bf16[4096,2048]{1,0:T(8,128)(2,1)}) fusion(f32[4096,2048]{1,0:T(8,128)} %fusion.130, bf16[4096,2048]{1,0:T(8,128)(2,1)} %all-gather.28.cloned.1.call-done, bf16[4095,2048]{1,0:T(8,128)(2,1)} %bitcast.164, f32[4096,2048]{1,0:T(8,128)} %fusion.129, f32[4095,2048]{1,0:T(8,128)} %fusion.16, ...), kind=kLoop, calls=%fused_computation.43 | loop fusion | flops 100659200 | bytes 151015424 | tf_op jit(solution)/shard_map/reduce_sum | solution.py:340
  1394.5 86.1 %all_to_all.45 = bf16[8,512,256]{2,1,0:T(8,128)(2,1)S(1)} all-to-all(bf16[8,512,256]{2,1,0:T(8,128)(2,1)S(1)} %bitcast.175), channel_id=1, replica_groups=mesh['batch'=4,'head'=8] {'head'}, dimensions={0} | all-to-all | bytes 4194304 | tf_op jit(solution)/shard_map/all_to_all | solution.py:320
  1483.6 108.8 %reduce-scatter.14.cloned.1.call-done = bf16[512,2048]{1,0:T(8,128)(2,1)} async-done(((bf16[4096,2048]{1,0:T(8,128)(2,1)}), bf16[512,2048]{1,0:T(8,128)(2,1)}) %reduce-scatter.14.cloned.1.call-update) | async-done | bytes 2097168 | tf_op jit(solution)/shard_map/reduce_scatter | solution.py:345
  1603.8 18.3 convolution_convert_fusion.6
  1622.2 25.2 convolution_convert_fusion.4
  1667.1 24.9 convolution_convert_fusion.5
  1692.1 72.5 %all-gather.38.cloned.1.call-done = bf16[4096,2048]{1,0:T(8,128)(2,1)} async-done(((bf16[512,2048]{1,0:T(8,128)(2,1)}), bf16[4096,2048]{1,0:T(8,128)(2,1)}) %all-gather.38.cloned.1.call-update) | async-done | bytes 16777232 | tf_op jit(solution)/shard_map/all_gather | solution.py:356
  1764.6 13.9 fusion.123
  1819.6 19.6 fusion.52
  1843.6 115.2 %while.30 = (s32[]{:T(128)}, f32[4,64,64]{2,1,0:T(8,128)S(1)}, f32[64,4,64,64]{3,2,1,0:T(8,128)}, f32[64,4,64,64]{3,2,1,0:T(8,128)}, f32[4,64]{1,0:T(4,128)S(1)}, /*index=5*/s32[]{:T(128)}, s32[]{:T(128)}, s32[]{:T(128)}) while((s32[]{:T(128)}, f32[4,64,64]{2,1,0:T(8,128)S(1)}, f32[64,4,64,64]{3,2,1,0:T(8,128)}, ...), condition=%wide.region_17.18_spmd.clone, body=%wide.region_16.17_spmd.clone.sunk | while | flops 81924 | bytes 395388 | solution.py:171
  1959.4 20.2 fusion.55
  1979.6 21.5 fusion.24
  2012.8 14.7 fusion.131
  2039.2 19.9 fusion.29
  2070.8 30.9 %fusion.28 = (f32[4,64]{1,0:T(4,128)}, bf16[64,64,4,64]{3,1,2,0:T(8,128)(2,1)}, bf16[64,64,4,64]{3,1,2,0:T(8,128)(2,1)}, f32[4,64]{1,0:T(4,128)}) fusion(f32[64,64,4,64]{3,2,1,0:T(4,128)} %reshape.249, f32[64,4,64]{2,0,1:T(8,128)S(1)} %copy-done.18, f32[64,4,64,64]{2,3,1,0:T(8,128)} %fusion.31, f32[64,64,4,64]{3,2,1,0:T(4,128)} %reshape.250, ...), kind=kOutput, calls=%fused_computation.75 | convolution fusion | flops 825228800 | bytes 33754368 | tf_op jit(solution)/shard_map/cthj,chij->cthi/dot_general | solution.py:178
  2137.7 19.2 convolution_convert_fusion.8
  2157.0 18.1 convolution_convert_fusion.9
  2175.2 19.0 convolution_convert_fusion.11
  2194.3 18.6 convolution_convert_fusion.10
  2213.0 15.3 fusion.134
  2228.3 13.7 fusion.132
  2268.7 55.2 %fusion.13 = f32[4095,2048]{1,0:T(8,128)} fusion(f32[4096,2048]{1,0:T(8,128)} %fusion.136, f32[4096,2048]{1,0:T(8,128)} %fusion.135, f32[4096,2048]{1,0:T(8,128)} %fusion.134, f32[4096,2048]{1,0:T(8,128)} %fusion.132, f32[2048]{0:T(1024)S(1)} %copy-done.75, f32[2048]{0:T(1024)S(1)} %copy-done.73, f32[2048]{0:T(1024)S(1)} %copy-done.77, f32[2048]{0:T(1024)S(1)} %copy-done.71), kind=kLoop, calls=%fused_computation.34 | loop fusion | flops 58705920 | bytes 167763968 | tf_op jit(solution)/shard_map/add | solution.py:218
  2323.9 70.0 %multiply_reduce_fusion.2 = (f32[2048]{0:T(1024)}, f32[2048]{0:T(1024)}, f32[2048]{0:T(1024)}, f32[2048]{0:T(1024)}, bf16[4096,2048]{1,0:T(8,128)(2,1)}) fusion(f32[4096,2048]{1,0:T(8,128)} %fusion.136, bf16[4096,2048]{1,0:T(8,128)(2,1)} %all-gather.14.cloned.1.call-done, bf16[4095,2048]{1,0:T(8,128)(2,1)} %bitcast.161, f32[4096,2048]{1,0:T(8,128)} %fusion.134, ...), kind=kLoop, calls=%fused_computation.45 | loop fusion | flops 167763968 | bytes 218157056 | tf_op jit(solution)/shard_map/reduce_sum | solution.py:219
  2462.2 98.5 %reduce-scatter.16.cloned.1.call-done = bf16[512,2048]{1,0:T(8,128)(2,1)} async-done(((bf16[4096,2048]{1,0:T(8,128)(2,1)}), bf16[512,2048]{1,0:T(8,128)(2,1)}) %reduce-scatter.16.cloned.1.call-update) | async-done | bytes 2097168 | tf_op jit(solution)/shard_map/reduce_scatter | solution.py:409
  2569.8 149.0 %all-reduce.7.cloned.1.call-done = (f32[2048]{0:T(1024)}, f32[2048]{0:T(1024)}, f32[2048]{0:T(1024)}, f32[2048]{0:T(1024)}, f32[2048]{0:T(1024)}, /*index=5*/f32...) async-done(((f32[2048]{0:T(1024)}, f32[2048]{0:T(1024)}, ...) | async-done | bytes 114704 | tf_op jit(solution)/shard_map/psum | solution.py:476
  (770 shorter events, 660.2 us)
Async XLA Ops:
  7.3 31.9 %all-gather.24.cloned.1.call-start = ((), (), s32[]{:S(2)}) async-start(), calls=%async_computation.19 | async-start | bytes 1310720 | tf_op jit(solution)/shard_map/all_gather | solution.py:261
  8.0 59.7 %all-gather.16.cloned.1.call-start = ((), (), s32[]{:S(2)}) async-start(), calls=%async_computation.15 | async-start | bytes 1310720 | tf_op jit(solution)/shard_map/all_gather | solution.py:259
  8.7 212.2 %all-gather.14.cloned.1.call-start = ((), (), s32[]{:S(2)}) async-start(), calls=%async_computation.14 | async-start | bytes 18874368 | tf_op jit(solution)/shard_map/all_gather | solution.py:269
  17.4 235.5 %all-gather.20.cloned.1.call-start = ((), (), s32[]{:S(2)}) async-start(), calls=%async_computation.17 | async-start | bytes 1310720 | tf_op jit(solution)/shard_map/all_gather | solution.py:258
  18.0 400.4 %all-gather.18.cloned.1.call-start = ((), (), s32[]{:S(2)}) async-start(), calls=%async_computation.16 | async-start | bytes 1310720 | tf_op jit(solution)/shard_map/all_gather | solution.py:257
  18.6 536.6 %all-gather.22.cloned.1.call-start = ((), (), s32[]{:S(2)}) async-start(), calls=%async_computation.18 | async-start | bytes 1310720 | tf_op jit(solution)/shard_map/all_gather | solution.py:260
  19.2 570.2 %all-gather.26.cloned.1.call-start = ((), (), s32[]{:S(2)}) async-start(), calls=%async_computation.20 | async-start | bytes 9437184 | tf_op jit(solution)/shard_map/all_gather | solution.py:304
  19.4 223.0 %copy-start.87 = (f32[64]{0:T(128)}, f32[64]{0:T(128)S(1)}, u32[]{:S(2)}) copy-start(f32[64]{0:T(128)S(1)} %iota_add_fusion) | copy-start | bytes 772
  19.5 474.8 %copy-start.37 = (f32[64,64]{1,0:T(8,128)}, f32[64,64]{1,0:T(8,128)S(1)}, u32[]{:S(2)}) copy-start(f32[64,64]{1,0:T(8,128)S(1)} %fusion.108) | copy-start | bytes 49156
  19.5 222.9 %copy-start.72 = (f32[2048]{0:T(1024)}, f32[2048]{0:T(1024)S(1)}, u32[]{:S(2)}) copy-start(f32[2048]{0:T(1024)S(1)} %get-tuple-element.277) | copy-start | bytes 24580
  19.5 398.9 %copy-start.70 = (f32[2048]{0:T(1024)}, f32[2048]{0:T(1024)S(1)}, u32[]{:S(2)}) copy-start(f32[2048]{0:T(1024)S(1)} %get-tuple-element.276) | copy-start | bytes 24580
  19.6 233.4 %copy-start.76 = (f32[2048]{0:T(1024)}, f32[2048]{0:T(1024)S(1)}, u32[]{:S(2)}) copy-start(f32[2048]{0:T(1024)S(1)} %get-tuple-element.275) | copy-start | bytes 24580
  19.6 535.5 %copy-start.74 = (f32[2048]{0:T(1024)}, f32[2048]{0:T(1024)S(1)}, u32[]{:S(2)}) copy-start(f32[2048]{0:T(1024)S(1)} %get-tuple-element.274) | copy-start | bytes 24580
  19.7 457.9 %copy-start.15 = (f32[64,4,64]{2,0,1:T(8,128)}, f32[64,4,64]{2,0,1:T(8,128)S(1)}, u32[]{:S(2)}) copy-start(f32[64,4,64]{2,0,1:T(8,128)S(1)} %get-tuple-element.272) | copy-start | bytes 196612
  19.7 457.9 %copy-start.17 = (f32[64,4,64]{2,0,1:T(8,128)}, f32[64,4,64]{2,0,1:T(8,128)S(1)}, u32[]{:S(2)}) copy-start(f32[64,4,64]{2,0,1:T(8,128)S(1)} %get-tuple-element.273) | copy-start | bytes 196612
  584.2 53.4 %all-to-all-start = ((bf16[8,512,256]{1,2,0:T(8,128)(2,1)}), bf16[8,512,256]{1,2,0:T(8,128)(2,1)}, u32[]{:S(2)}, u32[]{:S(2)}) async-start(bf16[8,512,256]{1,2,0:T(8,128)(2,1)} %copy.133), calls=%async_computation | async-start | bytes 4194304 | tf_op jit(solution)/shard_map/all_to_all | solution.py:305
  588.6 62.9 %all-gather.32.cloned.1.call-start = ((), (), s32[]{:S(2)}) async-start(), calls=%async_computation.23 | async-start | bytes 4587520 | tf_op jit(solution)/shard_map/all_gather | solution.py:262
  589.3 210.9 %all-gather.28.cloned.1.call-start = ((), (), s32[]{:S(2)}) async-start(), calls=%async_computation.21 | async-start | bytes 18874368 | tf_op jit(solution)/shard_map/all_gather | solution.py:309
  650.1 198.3 %all-gather.34.cloned.1.call-start = ((), (), s32[]{:S(2)}) async-start(), calls=%async_computation.24 | async-start | bytes 4587520 | tf_op jit(solution)/shard_map/all_gather | solution.py:263
  650.7 229.4 %all-gather.30.cloned.1.call-start = ((), (), s32[]{:S(2)}) async-start(), calls=%async_computation.22 | async-start | bytes 1310720 | tf_op jit(solution)/shard_map/all_gather | solution.py:264
  651.4 424.2 %reduce-scatter.12.cloned.1.call-start = ((), (), s32[]{:S(2)}) async-start(), calls=%async_computation.25 | async-start | bytes 18874368 | tf_op jit(solution)/shard_map/reduce_scatter | solution.py:315
  875.3 84.5 %all-to-all-start.2 = ((bf16[512,8,256]{2,0,1:T(8,128)(2,1)}), bf16[512,8,256]{2,0,1:T(8,128)(2,1)S(1)}, u32[]{:S(2)}, u32[]{:S(2)}) async-start(bf16[512,8,256]{2,0,1:T(8,128)(2,1)} %bitcast.174), calls=%async_computation.3 | async-start | bytes 4194304 | tf_op jit(solution)/shard_map/all_to_all | solution.py:324
  879.9 381.7 %all-gather.36.cloned.1.call-start = ((), (), s32[]{:S(2)}) async-start(), calls=%async_computation.26 | async-start | bytes 18874368 | tf_op jit(solution)/shard_map/all_gather | solution.py:330
  880.0 220.6 %copy-start.35 = (bf16[2048,256]{1,0:T(8,128)(2,1)S(1)}, bf16[2048,256]{1,0:T(8,128)(2,1)}, u32[]{:S(2)}) copy-start(bf16[2048,256]{1,0:T(8,128)(2,1)} %all-gather.30.cloned.1.call-done) | copy-start | bytes 3145732
  1100.6 491.8 %reduce-scatter.14.cloned.1.call-start = ((), (), s32[]{:S(2)}) async-start(), calls=%async_computation.27 | async-start | bytes 18874368 | tf_op jit(solution)/shard_map/reduce_scatter | solution.py:345
  1392.9 371.6 %all-gather.38.cloned.1.call-start = ((), (), s32[]{:S(2)}) async-start(), calls=%async_computation.28 | async-start | bytes 18874368 | tf_op jit(solution)/shard_map/all_gather | solution.py:356
  1480.6 111.8 %copy-start.46 = (f32[2048]{0:T(1024)S(1)}, f32[2048]{0:T(1024)}, u32[]{:S(2)}) copy-start(f32[2048]{0:T(1024)} %param.47) | copy-start | bytes 24580
  1480.6 111.8 %copy-start.51 = (f32[512]{0:T(512)S(1)}, f32[512]{0:T(512)}, u32[]{:S(2)}) copy-start(f32[512]{0:T(512)} %copy-done.50) | copy-start | bytes 6148
  1480.6 111.8 %copy-start.57 = (f32[512]{0:T(512)S(1)}, f32[512]{0:T(512)}, u32[]{:S(2)}) copy-start(f32[512]{0:T(512)} %copy-done.56) | copy-start | bytes 6148
  1481.0 116.4 %copy-start.14 = (bf16[512,2048]{1,0:T(8,128)(2,1)S(1)}, bf16[512,2048]{1,0:T(8,128)(2,1)}, u32[]{:S(2)}) copy-start(bf16[512,2048]{1,0:T(8,128)(2,1)} %param.31) | copy-start | bytes 6291460
  1603.8 799.3 %reduce-scatter.32.cloned.1.call-start = ((), (), s32[]{:S(2)}) async-start(), calls=%async_computation.37 | async-start | bytes 1310720 | tf_op jit(solution)/shard_map/reduce_scatter | solution.py:449
  1622.2 782.7 %reduce-scatter.30.cloned.1.call-start = ((), (), s32[]{:S(2)}) async-start(), calls=%async_computation.36 | async-start | bytes 4587520 | tf_op jit(solution)/shard_map/reduce_scatter | solution.py:446
  1647.5 760.0 %reduce-scatter.28.cloned.1.call-start = ((), (), s32[]{:S(2)}) async-start(), calls=%async_computation.35 | async-start | bytes 4587520 | tf_op jit(solution)/shard_map/reduce_scatter | solution.py:443
  1667.1 97.5 %copy-start.95 = (f32[256]{0:T(256)S(1)}, f32[256]{0:T(256)}, u32[]{:S(2)}) copy-start(f32[256]{0:T(256)} %param.45) | copy-start | bytes 3076
  1692.0 761.2 %reduce-scatter.26.cloned.1.call-start = ((), (), s32[]{:S(2)}) async-start(), calls=%async_computation.34 | async-start | bytes 1310720 | tf_op jit(solution)/shard_map/reduce_scatter | solution.py:440
  1819.5 251.3 %copy-start.27 = (f32[64,64,4]{1,2,0:T(4,128)}, f32[64,64,4]{1,2,0:T(4,128)S(1)}, u32[]{:S(2)}) copy-start(f32[64,64,4]{1,2,0:T(4,128)S(1)} %get-tuple-element.245) | copy-start | bytes 196612
  1839.1 120.3 %copy-start.16 = (f32[64,4,64]{2,0,1:T(8,128)S(1)}, f32[64,4,64]{2,0,1:T(8,128)}, u32[]{:S(2)}) copy-start(f32[64,4,64]{2,0,1:T(8,128)} %copy-done.15) | copy-start | bytes 196612
  2137.6 317.5 %reduce-scatter.24.cloned.1.call-start = ((), (), s32[]{:S(2)}) async-start(), calls=%async_computation.33 | async-start | bytes 1310720 | tf_op jit(solution)/shard_map/reduce_scatter | solution.py:437
  2156.9 300.0 %reduce-scatter.22.cloned.1.call-start = ((), (), s32[]{:S(2)}) async-start(), calls=%async_computation.32 | async-start | bytes 1310720 | tf_op jit(solution)/shard_map/reduce_scatter | solution.py:434
  2175.1 283.5 %reduce-scatter.18.cloned.1.call-start = ((), (), s32[]{:S(2)}) async-start(), calls=%async_computation.30 | async-start | bytes 1310720 | tf_op jit(solution)/shard_map/reduce_scatter | solution.py:428
  2194.2 266.2 %reduce-scatter.20.cloned.1.call-start = ((), (), s32[]{:S(2)}) async-start(), calls=%async_computation.31 | async-start | bytes 1310720 | tf_op jit(solution)/shard_map/reduce_scatter | solution.py:431
  2212.9 347.8 %reduce-scatter.16.cloned.1.call-start = ((), (), s32[]{:S(2)}) async-start(), calls=%async_computation.29 | async-start | bytes 18874368 | tf_op jit(solution)/shard_map/reduce_scatter | solution.py:409
  2393.9 324.9 %all-reduce.7.cloned.1.call-start = ((), (), s32[]{:S(2)}) async-start(), calls=%async_computation.38 | async-start | bytes 262144 | tf_op jit(solution)/shard_map/psum | solution.py:476
  2441.6 119.1 %copy-start.7 = (bf16[512,2048]{1,0:T(8,128)(2,1)S(1)}, bf16[512,2048]{1,0:T(8,128)(2,1)}, u32[]{:S(2)}) copy-start(bf16[512,2048]{1,0:T(8,128)(2,1)} %param.29) | copy-start | bytes 6291460
  2441.6 119.1 %copy-start.47 = (f32[2048]{0:T(1024)S(1)}, f32[2048]{0:T(1024)}, u32[]{:S(2)}) copy-start(f32[2048]{0:T(1024)} %param.32) | copy-start | bytes 24580
  2441.6 119.1 %copy-start.53 = (f32[512]{0:T(512)S(1)}, f32[512]{0:T(512)}, u32[]{:S(2)}) copy-start(f32[512]{0:T(512)} %copy-done.52) | copy-start | bytes 6148
  2441.6 119.1 %copy-start.55 = (f32[512]{0:T(512)S(1)}, f32[512]{0:T(512)}, u32[]{:S(2)}) copy-start(f32[512]{0:T(512)} %copy-done.54) | copy-start | bytes 6148
  2453.2 111.5 %copy-start.48 = (f32[32,64]{1,0:T(8,128)}, f32[32,64]{1,0:T(8,128)S(1)}, u32[]{:S(2)}) copy-start(f32[32,64]{1,0:T(8,128)S(1)} %multiply_dynamic-update-slice_fusion) | copy-start | bytes 24580
  (80 other events, 1244.7 us)
Sparse Core Ops, SparseCore 0:
  9.9 29.1 all-gather.23
  41.0 26.6 all-gather.15
  69.8 151.0 all-gather.13
  222.7 24.8 all-gather.19
  249.2 26.6 all-gather.17
  277.6 26.6 all-gather.21
  305.9 82.0 all-gather.25
  591.3 49.6 all-gather.31
  650.2 149.9 all-gather.27
  801.9 46.4 all-gather.33
  850.2 26.6 all-gather.29
  879.1 196.5 reduce-scatter.11
  1100.7 160.8 all-gather.35
  1393.1 199.2 reduce-scatter.13
  1603.9 160.6 all-gather.37
  1767.9 25.9 reduce-scatter.31
  1797.0 48.3 reduce-scatter.29
  1848.5 48.2 reduce-scatter.27
  2137.7 26.0 reduce-scatter.25
  2166.6 27.7 reduce-scatter.23
  2197.5 27.6 reduce-scatter.21
  2228.1 27.7 reduce-scatter.17
  2259.1 27.7 reduce-scatter.19
  2394.0 166.6 reduce-scatter.15
  2568.8 149.9 all-reduce.6
where the time goes:
time: 2750 us; the launch traced here: 2740 us
  waiting for transfers between devices  1190 us (43%)
  matrix products  676 us (25%)
  other arithmetic  426 us (15%)
  local copies, waits for them, and re-layouts  333 us (12%)
  blocking collectives  86.1 us (3%)
    dot_general x8, matrix products, plain_prod(): return jnp.dot(left, right, preferred_element_type=jnp.float32)  179 us
    all_gather x1, waiting for transfers between devices, on_device(): seq_x1 = lax.all_gather(local_x1, 'head', axis=0, tiled=True)  153 us
    dot_general x8, matrix products, outer_grad(): lax.dot_general(left, right, (((0,), (0,)), ((), ())), preferred_element_...  153 us
    psum x1, waiting for transfers between devices, on_device(): lax.psum((ln1_gain_part, ln1_bias_part, mix_r_part, mix_k_part, mix_v_par...  149 us
    all_gather x1, waiting for transfers between devices, on_device(): lax.all_gather(normed2.astype(jnp.bfloat16), 'head', axis=0, tiled=True)  149 us
    all_gather x1, waiting for transfers between devices, on_device(): piece = lax.all_gather(grad_value, 'head', axis=1, tiled=True)  147 us
    dot_general x8, matrix products, back_prod(): lax.dot_general(left, right, (((1,), (1,)), ((), ())), preferred_element_...  128 us
    reduce_scatter x1, waiting for transfers between devices, on_device(): lax.psum_scatter(plain_prod(key_sq, full_cv).astype(jnp.bfloat16), 'head'...  114 us
  transfers between devices with their start and end apart: 27, of which 13 were waited for; matrix products, arithmetic and copies ran while one was open for 45% of the time, Pallas kernels for 0%

commit v1 on v0

v1 whole, which is shorter than its diff:
```python
import functools

import jax
import jax.numpy as jnp
from jax import lax
from jax.experimental import pallas as pl
from jax.experimental.pallas import tpu as pltpu
from jax.sharding import Mesh
from jax.sharding import PartitionSpec as P

ATTN_WIDTH = 64
QUAD = 256

ln_eps = 1e-05
gn_eps = 0.00064
f32 = jnp.float32
bf16 = jnp.bfloat16


def nn(left, right):
    return jnp.dot(left, right, preferred_element_type=f32)


def nt(left, right):
    return lax.dot_general(left, right, (((1,), (1,)), ((), ())), preferred_element_type=f32)


def tn(left, right):
    return lax.dot_general(left, right, (((0,), (0,)), ((), ())), preferred_element_type=f32)


def head_masks():
    lane_head = lax.broadcasted_iota(jnp.int32, (1, QUAD), 1) // ATTN_WIDTH
    return [lane_head == h for h in range(QUAD // ATTN_WIDTH)]


def block_mask():
    row_head = lax.broadcasted_iota(jnp.int32, (QUAD, QUAD), 0) // ATTN_WIDTH
    col_head = lax.broadcasted_iota(jnp.int32, (QUAD, QUAD), 1) // ATTN_WIDTH
    return row_head == col_head


def only(mask, lines):
    return jnp.where(mask, lines, jnp.zeros_like(lines))


def compress(square, masks):
    return sum(
        jnp.where(m, square[h * ATTN_WIDTH : (h + 1) * ATTN_WIDTH, :], 0.0)
        for h, m in enumerate(masks)
    )


def expand(packed, blocks):
    return jnp.where(blocks, jnp.concatenate([packed] * (QUAD // ATTN_WIDTH), 0), 0.0)


def head_sum(lines, ones):
    return nn(lines.astype(bf16), ones)


def head_sum_fine(lines, ones):
    coarse = lines.astype(bf16)
    return nn(coarse, ones) + nn((lines - coarse.astype(f32)).astype(bf16), ones)


def local_state_kernel(rate_ref, k_ref, v_ref, out_ref):
    length = k_ref.shape[1]
    rate = rate_ref[...]
    remaining = (length - 1) - lax.broadcasted_iota(jnp.int32, (length, 1), 0)
    faded = (k_ref[0].astype(f32) * jnp.exp(-rate * remaining.astype(f32))).astype(bf16)
    out_ref[0] = compress(tn(v_ref[0], faded), head_masks())


def group_norm_parts(y, ones):
    center = y - head_sum_fine(y, ones) * (1.0 / ATTN_WIDTH)
    inv = lax.rsqrt(head_sum(center * center, ones) * (1.0 / ATTN_WIDTH) + gn_eps)
    return center * inv, inv


def forward_kernel(
    rate_ref, boost_ref, gain_ref, bias_ref, s0_ref, r_ref, k_ref, v_ref, g_ref,
    z_ref, y_ref, begin_ref, state,
):
    span = r_ref.shape[1]
    masks = head_masks()
    blocks = block_mask()
    ones = jnp.where(blocks, 1.0, 0.0).astype(bf16)

    @pl.when(pl.program_id(2) == 0)
    def _():
        state[...] = expand(s0_ref[0], blocks)

    rate = rate_ref[...]
    pos = lax.broadcasted_iota(jnp.int32, (span, 1), 0).astype(f32)
    r = r_ref[0].astype(f32)
    k = k_ref[0].astype(f32)
    v = v_ref[0]
    qt = (r * jnp.exp(-rate * pos)).astype(bf16)
    kt = (k * jnp.exp(rate * (pos + 1.0))).astype(bf16)
    begin = state[...]
    begin_ref[0, 0] = compress(begin, masks)
    y = nt(qt, begin.astype(bf16))
    causal = lax.broadcasted_iota(jnp.int32, (span, span), 0) > lax.broadcasted_iota(
        jnp.int32, (span, span), 1
    )
    for m in masks:
        scores = jnp.where(causal, nt(only(m, qt), kt), 0.0).astype(bf16)
        y = y + nn(scores, only(m, v))
    y = y + head_sum(r * boost_ref[...] * k, ones) * v.astype(f32)
    state[...] = jnp.exp(-rate * span) * (begin + jnp.where(blocks, tn(v, kt), 0.0))
    y_ref[0] = y
    normed, _ = group_norm_parts(y, ones)
    g = g_ref[0]
    z_ref[0] = ((normed * gain_ref[...] + bias_ref[...]) * (g * jax.nn.sigmoid(g))).astype(bf16)


def gate_back_kernel(
    rate_ref, gain_ref, bias_ref, gz_ref, y_ref, g_ref, r_ref,
    gg_ref, gy_ref, end_ref, sums_ref, total,
):
    span = r_ref.shape[1]
    step = pl.program_id(2)
    blocks = block_mask()
    ones = jnp.where(blocks, 1.0, 0.0).astype(bf16)

    @pl.when(step == 0)
    def _():
        total[...] = jnp.zeros_like(total)
        sums_ref[...] = jnp.zeros_like(sums_ref)

    normed, inv = group_norm_parts(y_ref[0], ones)
    gain = gain_ref[...]
    g = g_ref[0]
    gz = gz_ref[0].astype(f32)
    sig = jax.nn.sigmoid(g)
    grad_grouped = gz * (g * sig)
    grouped = normed * gain + bias_ref[...]
    gg_ref[0] = (gz * grouped * sig * (1.0 + g * (1.0 - sig))).astype(bf16)
    sums_ref[0, 0, 0:1, :] += jnp.sum(grad_grouped * normed, 0, keepdims=True)
    sums_ref[0, 0, 1:2, :] += jnp.sum(grad_grouped, 0, keepdims=True)
    e = grad_grouped * gain
    gy = inv * (
        e
        - head_sum_fine(e, ones) * (1.0 / ATTN_WIDTH)
        - normed * (head_sum(e * normed, ones) * (1.0 / ATTN_WIDTH))
    )
    gy = gy.astype(bf16)
    gy_ref[0] = gy
    pos = (lax.broadcasted_iota(jnp.int32, (span, 1), 0) + step * span).astype(f32)
    faded = (r_ref[0].astype(f32) * jnp.exp(-rate_ref[...] * pos)).astype(bf16)
    total[...] += tn(gy, faded)
    end_ref[0] = compress(total[...], head_masks())


def backward_kernel(
    rate_ref, boost_ref, end_ref, begin_ref, r_ref, k_ref, v_ref, gy_ref,
    dr_ref, dk_ref, dv_ref, sums_ref, carry,
):
    span = r_ref.shape[1]
    masks = head_masks()
    blocks = block_mask()
    ones = jnp.where(blocks, 1.0, 0.0).astype(bf16)

    @pl.when(pl.program_id(2) == 0)
    def _():
        carry[...] = expand(end_ref[0], blocks)
        sums_ref[...] = jnp.zeros_like(sums_ref)

    rate = rate_ref[...]
    boost = boost_ref[...]
    pos = lax.broadcasted_iota(jnp.int32, (span, 1), 0).astype(f32)
    toward = jnp.exp(-rate * pos)
    away = jnp.exp(rate * (pos + 1.0))
    r = r_ref[0].astype(f32)
    k = k_ref[0].astype(f32)
    v = v_ref[0]
    gy = gy_ref[0]
    qt = (r * toward).astype(bf16)
    kt = (k * away).astype(bf16)
    passed = jnp.exp(-rate * span) * carry[...]
    passed_low = passed.astype(bf16)
    begin = expand(begin_ref[0, 0], blocks)
    rows = lax.broadcasted_iota(jnp.int32, (span, span), 0)
    cols = lax.broadcasted_iota(jnp.int32, (span, span), 1)
    dq = nn(gy, begin.astype(bf16))
    dk = nn(v, passed_low)
    dv = nt(kt, passed_low)
    for m in masks:
        v_h, gy_h, k_h, q_h = only(m, v), only(m, gy), only(m, kt), only(m, qt)
        pairs = jnp.where(rows > cols, nt(gy_h, v), 0.0).astype(bf16)
        dq = dq + nn(pairs, k_h)
        pairs_t = jnp.where(rows < cols, nt(v_h, gy), 0.0).astype(bf16)
        dk = dk + nn(pairs_t, q_h)
        scores_t = jnp.where(rows < cols, nt(k_h, qt), 0.0).astype(bf16)
        dv = dv + nn(scores_t, gy_h)
    vf = v.astype(f32)
    gyf = gy.astype(f32)
    inner = head_sum(gyf * vf, ones)
    dv = dv + head_sum(r * boost * k, ones) * gyf
    dr_ref[0] = (dq * toward + inner * boost * k).astype(bf16)
    dk_ref[0] = (dk * away + inner * boost * r).astype(bf16)
    dv_ref[0] = dv.astype(bf16)
    held = begin.astype(bf16).astype(f32) + jnp.where(blocks, tn(v, kt), 0.0)
    decay = (
        jnp.sum(pos * dq * qt.astype(f32), 0, keepdims=True)
        - jnp.sum((pos + 1.0) * dk * kt.astype(f32), 0, keepdims=True)
        + span * jnp.sum(passed_low.astype(f32) * held, 0, keepdims=True)
    )
    sums_ref[0, 0, 0:1, :] += decay * (-rate)
    sums_ref[0, 0, 1:2, :] += jnp.sum(inner * r * k, 0, keepdims=True)
    carry[...] = passed + jnp.where(blocks, tn(gy, qt), 0.0)


VMEM_LIMIT = 48 * 1024 * 1024


def vec_spec():
    return pl.BlockSpec((1, QUAD), lambda s, q, c: (0, q))


def state_spec():
    return pl.BlockSpec((1, ATTN_WIDTH, QUAD), lambda s, q, c: (s, 0, q))


def sums_spec():
    return pl.BlockSpec((1, 1, 2, QUAD), lambda s, q, c: (s, q, 0, 0))


def sds(shape, dtype):
    return jax.ShapeDtypeStruct(shape, dtype)


def local_state(rate, k, v):
    segs, length, width = k.shape
    block = pl.BlockSpec((1, length, QUAD), lambda s, q: (s, 0, q))
    return pl.pallas_call(
        local_state_kernel,
        grid=(segs, width // QUAD),
        in_specs=[pl.BlockSpec((1, QUAD), lambda s, q: (0, q)), block, block],
        out_specs=pl.BlockSpec((1, ATTN_WIDTH, QUAD), lambda s, q: (s, 0, q)),
        out_shape=sds((segs, ATTN_WIDTH, width), f32),
        compiler_params=pltpu.CompilerParams(vmem_limit_bytes=VMEM_LIMIT),
        name="local_state",
    )(rate, k, v)


def mix_forward(rate, boost, gain, bias, s0, r, k, v, g):
    segs, length, width = r.shape
    span = min(QUAD, length)
    count = length // span
    quads = width // QUAD
    block = pl.BlockSpec((1, span, QUAD), lambda s, q, c: (s, c, q))
    return pl.pallas_call(
        forward_kernel,
        grid=(segs, quads, count),
        in_specs=[vec_spec()] * 4 + [state_spec()] + [block] * 4,
        out_specs=[
            block,
            block,
            pl.BlockSpec((1, 1, ATTN_WIDTH, QUAD), lambda s, q, c: (s, c, 0, q)),
        ],
        out_shape=[
            sds((segs, length, width), bf16),
            sds((segs, length, width), f32),
            sds((segs, count, ATTN_WIDTH, width), f32),
        ],
        scratch_shapes=[pltpu.VMEM((QUAD, QUAD), f32)],
        compiler_params=pltpu.CompilerParams(vmem_limit_bytes=VMEM_LIMIT),
        name="mix_forward",
    )(rate, boost, gain, bias, s0, r, k, v, g)


def gate_back(rate, gain, bias, gz, y, g, r):
    segs, length, width = r.shape
    span = min(QUAD, length)
    quads = width // QUAD
    block = pl.BlockSpec((1, span, QUAD), lambda s, q, c: (s, c, q))
    return pl.pallas_call(
        gate_back_kernel,
        grid=(segs, quads, length // span),
        in_specs=[vec_spec()] * 3 + [block] * 4,
        out_specs=[block, block, state_spec(), sums_spec()],
        out_shape=[
            sds((segs, length, width), bf16),
            sds((segs, length, width), bf16),
            sds((segs, ATTN_WIDTH, width), f32),
            sds((segs, quads, 2, QUAD), f32),
        ],
        scratch_shapes=[pltpu.VMEM((QUAD, QUAD), f32)],
        compiler_params=pltpu.CompilerParams(vmem_limit_bytes=VMEM_LIMIT),
        name="gate_back",
    )(rate, gain, bias, gz, y, g, r)


def mix_backward(rate, boost, end, begin, r, k, v, gy):
    segs, length, width = r.shape
    span = min(QUAD, length)
    count = length // span
    quads = width // QUAD
    block = pl.BlockSpec((1, span, QUAD), lambda s, q, c: (s, count - 1 - c, q))
    return pl.pallas_call(
        backward_kernel,
        grid=(segs, quads, count),
        in_specs=[vec_spec()] * 2
        + [
            state_spec(),
            pl.BlockSpec((1, 1, ATTN_WIDTH, QUAD), lambda s, q, c: (s, count - 1 - c, 0, q)),
        ]
        + [block] * 4,
        out_specs=[block, block, block, sums_spec()],
        out_shape=[sds((segs, length, width), bf16)] * 3 + [sds((segs, quads, 2, QUAD), f32)],
        scratch_shapes=[pltpu.VMEM((QUAD, QUAD), f32)],
        compiler_params=pltpu.CompilerParams(vmem_limit_bytes=VMEM_LIMIT),
        name="mix_backward",
    )(rate, boost, end, begin, r, k, v, gy)


def swap(value, axis):
    return lax.ppermute(value, axis, [(0, 1), (1, 0)])


def send_far(value, team, distance):
    if distance == 1:
        return swap(value, team[-1])
    if distance == 2:
        return swap(value, team[0])
    return lax.ppermute(value, team, [(i, 3 - i) for i in range(4)])


def team_size(team):
    return 2 ** len(team)


def reorder(values, team):
    far = lax.axis_index(team[-1]) == 1
    if len(team) == 1:
        return jnp.where(far, jnp.stack([values[1], values[0]]), values)
    flipped = jnp.stack([values[1], values[0], values[3], values[2]])
    values = jnp.where(far, flipped, values)
    far = lax.axis_index(team[0]) == 1
    flipped = jnp.stack([values[2], values[3], values[0], values[1]])
    return jnp.where(far, flipped, values)


def team_exchange(values, team):
    return [values[0]] + [send_far(values[i], team, i) for i in range(1, team_size(team))]


def abs_exchange(values, team):
    by_distance = reorder(values, team)
    return reorder(jnp.stack(team_exchange(by_distance, team)), team)


def team_copies(value, team):
    if len(team) == 1:
        return [value, swap(value, team[0])]
    near = swap(value, team[1])
    side = swap(value, team[0])
    half = value.shape[0] // 2
    if half == 0:
        return [value, near, side, swap(near, team[0])]
    corner = jnp.concatenate([swap(near[:half], team[0]), swap(side[half:], team[1])], 0)
    return [value, near, side, corner]


def core_pair(value):
    other = swap(value, "c")
    first = lax.axis_index("c") == 0
    return jnp.where(
        first, jnp.concatenate([value, other], 0), jnp.concatenate([other, value], 0)
    )


def gather_tokens(value, team):
    return [core_pair(piece) for piece in team_copies(value, team)]


def core_reduce(part):
    tokens = part.shape[0] // 2
    core = lax.axis_index("c")
    mine = lax.dynamic_slice_in_dim(part, core * tokens, tokens, 0)
    other = lax.dynamic_slice_in_dim(part, (1 - core) * tokens, tokens, 0)
    return mine.astype(f32) + swap(other, "c").astype(f32)


def reduce_tokens(make_part, team):
    if len(team) == 1:
        away = core_reduce(make_part(1)).astype(bf16)
        got = swap(away, team[0])
        return core_reduce(make_part(0)) + got.astype(f32)
    corner = core_reduce(make_part(3)).astype(bf16)
    half = corner.shape[0] // 2
    to_near = swap(corner[:half], team[0])
    to_side = swap(corner[half:], team[1])
    near = core_reduce(make_part(1))
    near = jnp.concatenate([near[:half] + to_near.astype(f32), near[half:]], 0).astype(bf16)
    from_near = swap(near, team[1])
    side = core_reduce(make_part(2))
    side = jnp.concatenate([side[:half], side[half:] + to_side.astype(f32)], 0).astype(bf16)
    from_side = swap(side, team[0])
    return core_reduce(make_part(0)) + from_near.astype(f32) + from_side.astype(f32)


def gather_weights(shards, team, spread):
    n, rows, cols = shards.shape
    members = team_size(team)
    fine = rows // members
    blocks = shards.reshape(n, members, fine, cols).transpose(1, 0, 2, 3)
    mine = abs_exchange(blocks, team)
    whole = lax.all_gather(mine, spread, axis=0, tiled=False)
    nz = lax.axis_size("z")
    nd = whole.shape[0] // nz
    whole = whole.reshape(nd, nz, members, n, fine, cols)
    return whole.transpose(3, 1, 4, 0, 2, 5).reshape(n, nz * fine, nd * members * cols)


def scatter_weights(grads, team, spread):
    n, rows, width = grads.shape
    members = team_size(team)
    nz = lax.axis_size("z")
    nd = lax.axis_size("d")
    fine = rows // nz
    cols = width // (nd * members)
    blocks = grads.reshape(n, nz, fine, nd, members, cols).transpose(3, 1, 4, 0, 2, 5)
    blocks = blocks.reshape(nd * nz, members, n, fine, cols)
    mine = lax.psum_scatter(blocks, spread, scatter_dimension=0, tiled=False)
    mine = abs_exchange(mine, team)
    return mine.transpose(1, 0, 2, 3).reshape(n, members * fine, cols)


def layer_norm(payload_lines, gain, bias):
    center = payload_lines - jnp.mean(payload_lines, -1, keepdims=True)
    inv_scale = lax.rsqrt(jnp.mean(center * center, -1, keepdims=True) + ln_eps)
    normed = center * inv_scale
    return (normed * gain + bias, normed, inv_scale)


def norm_back(upstream_deriv, normed, inv_scale, gain):
    scaled = upstream_deriv * gain
    return inv_scale * (
        scaled
        - jnp.mean(scaled, -1, keepdims=True)
        - normed * jnp.mean(scaled * normed, -1, keepdims=True)
    )


def token_mix(current, earlier, weight):
    return (
        current.astype(f32) * weight + earlier.astype(f32) * (1.0 - weight)
    ).astype(bf16)


def on_device(
    team,
    layer_source,
    piecewise_opening_memory,
    upstream_adjoint,
    earlier_layernorm_scale,
    earlier_layernorm_shift,
    accept_blend,
    lookup_blend,
    payload_blend,
    valve_blend,
    accept_weights,
    lookup_weights,
    payload_weights,
    valve_weights,
    forgetting_loglog,
    diagonal_boost,
    groupwise_scale,
    groupwise_shift,
    emission_weights,
    later_layernorm_scale,
    later_layernorm_shift,
    feedforward_lookup_blend,
    feedforward_accept_blend,
    feedforward_lookup_weights,
    feedforward_payload_weights,
    feedforward_accept_weights,
):
    members = team_size(team)
    every = ("d",) + team + ("z", "c")
    spread = ("d", "z") if lax.axis_size("d") > 1 else "z"
    nz = lax.axis_size("z")
    nd = lax.axis_size("d")
    zi = lax.axis_index("z")
    ci = lax.axis_index("c")
    member = lax.axis_index(team)
    tokens, width = layer_source.shape
    heads_here = nz
    length = 2 * tokens
    line = [(i * 2 + j) for i in range(nz) for j in range(2)]
    down = [(i, i + 1) for i in line[:-1]]
    up = [(i + 1, i) for i in line[:-1]]

    mix_shards = jnp.stack(
        [w.T for w in (accept_weights, lookup_weights, payload_weights, valve_weights)]
    )
    mix_w = gather_weights(mix_shards, team, spread)
    vectors = jnp.stack(
        [
            forgetting_loglog,
            diagonal_boost,
            groupwise_scale.reshape(members, ATTN_WIDTH),
            groupwise_shift.reshape(members, ATTN_WIDTH),
        ]
    )
    vectors = lax.all_gather(vectors, "z", axis=0, tiled=False)
    vectors = lax.dynamic_index_in_dim(vectors, member, 2, keepdims=False)
    vectors = vectors.transpose(1, 0, 2).reshape(4, 1, heads_here * ATTN_WIDTH)
    rate, boost, gn_gain, gn_bias = jnp.exp(vectors[0]), vectors[1], vectors[2], vectors[3]

    residual = layer_source.astype(f32)
    normed1, hat1, inv1 = layer_norm(residual, earlier_layernorm_scale, earlier_layernorm_shift)
    local_x1 = normed1.astype(bf16)
    tail = lax.ppermute(layer_source[-1:], "z", [(i, i + 1) for i in range(nz - 1)])
    tail = jnp.where(ci == 1, tail, swap(tail, "c"))
    halo = layer_norm(tail.astype(f32), earlier_layernorm_scale, earlier_layernorm_shift)[0]
    halo = jnp.where(zi > 0, halo, 0.0).astype(bf16)
    halos = team_copies(halo, team)
    x1 = gather_tokens(local_x1, team)
    whole_x1 = jnp.stack(
        [
            jnp.concatenate([now, jnp.concatenate([edge, now[:-1]], 0)], 1)
            for now, edge in zip(x1, halos)
        ]
    )
    whole_x1 = whole_x1.reshape(members * length, 2 * width)

    nb_cols = emission_weights.shape[1]
    whole_o = lax.all_gather(emission_weights, every, axis=0, tiled=False)
    whole_o = whole_o.reshape(nd * members, nz, 2, members, ATTN_WIDTH, nb_cols)
    whole_o = whole_o.transpose(2, 3, 1, 4, 0, 5).reshape(width, width)
    lookup_t = gather_weights(feedforward_lookup_weights.T[None], team, spread)[0]
    payload_w = gather_weights(feedforward_payload_weights[None], team, spread)[0]
    cr_rows, cr_cols = feedforward_accept_weights.shape
    whole_cr = lax.all_gather(feedforward_accept_weights, every, axis=0, tiled=False)
    whole_cr = whole_cr.reshape(nd * members, nz * 2, cr_rows, cr_cols)
    whole_cr = whole_cr.transpose(0, 2, 1, 3).reshape(width, width)

    blends = jnp.stack([accept_blend, lookup_blend, payload_blend, valve_blend])[:, None, :]
    mix_f = mix_w.astype(f32)
    now_w = (mix_f * blends).astype(bf16)
    past_w = (mix_f * (1.0 - blends)).astype(bf16)
    cols = heads_here * ATTN_WIDTH
    wide_w = jnp.concatenate([now_w, past_w], 2).reshape(4 * cols, 2 * width)
    wide_w, whole_x1 = lax.optimization_barrier((wide_w, whole_x1))
    rkv = nt(whole_x1, wide_w[: 3 * cols]).astype(bf16)
    gate_pre = nt(whole_x1, wide_w[3 * cols :])
    r, k, v = (
        rkv[:, i * cols : (i + 1) * cols].reshape(members, length, cols) for i in range(3)
    )
    gate_pre = gate_pre.reshape(members, length, cols)

    opening = reorder(piecewise_opening_memory[0], team)
    opening = jnp.stack(team_exchange(opening, team))
    opening = lax.all_gather(opening, "z", axis=0, tiled=False)
    opening = opening.transpose(1, 3, 0, 2).reshape(members, ATTN_WIDTH, cols)
    run_ids = jnp.arange(nz)

    def fade(steps):
        return jnp.where(
            steps >= 0, jnp.exp(-rate * (length * jnp.maximum(steps, 0)).astype(f32)), 0.0
        )

    added = local_state(rate, k, v)
    added = lax.all_gather(added, "z", axis=0, tiled=False)
    weight = fade((zi - 1 - run_ids)[:, None])[:, None, None, :]
    s0 = fade(zi[None, None]) * opening + jnp.sum(weight * added, 0)
    z, y, begin = mix_forward(rate, boost, gn_gain, gn_bias, s0, r, k, v, gate_pre)

    got = jnp.stack(team_exchange([z[i] for i in range(members)], team))
    got = reorder(got, team).reshape(members, 2, tokens, cols)
    mine = lax.dynamic_index_in_dim(got, ci, 1, keepdims=False)
    other = swap(lax.dynamic_index_in_dim(got, 1 - ci, 1, keepdims=False), "c")
    pair = jnp.where(ci == 0, jnp.stack([mine, other]), jnp.stack([other, mine]))
    z_rows = pair.transpose(2, 0, 1, 3).reshape(tokens, width)
    middle = residual + nn(z_rows, whole_o)

    normed2, hat2, inv2 = layer_norm(middle, later_layernorm_scale, later_layernorm_shift)
    local_x2 = normed2.astype(bf16)
    edge2 = lax.ppermute(local_x2[-1:], ("z", "c"), down)
    prev2 = jnp.concatenate([edge2, local_x2[:-1]], 0)
    mixed_ck = token_mix(local_x2, prev2, feedforward_lookup_blend)
    mixed_cr = token_mix(local_x2, prev2, feedforward_accept_blend)
    seq_ck = gather_tokens(mixed_ck, team)
    key_pre = [nt(piece, lookup_t) for piece in seq_ck]
    key_relu = [jax.nn.relu(piece) for piece in key_pre]
    key_sq = [jnp.square(piece).astype(bf16) for piece in key_relu]
    key_relu = [piece.astype(bf16) for piece in key_relu]
    value_sum = reduce_tokens(lambda i: nn(key_sq[i], payload_w).astype(bf16), team)
    sig_two = jax.nn.sigmoid(nn(mixed_cr, whole_cr))
    block_out = (middle + sig_two * value_sum).astype(bf16)

    cot = upstream_adjoint.astype(f32)
    grad_value = (cot * sig_two).astype(bf16)
    grad_r2 = (cot * value_sum * sig_two * (1.0 - sig_two)).astype(bf16)
    seq_gv = gather_tokens(grad_value, team)
    grad_key = [
        (nt(piece, payload_w) * (2.0 * held.astype(f32))).astype(bf16)
        for piece, held in zip(seq_gv, key_relu)
    ]
    grad_ck = reduce_tokens(lambda i: nn(grad_key[i], lookup_t).astype(bf16), team)
    grad_cr = nt(grad_r2, whole_cr)
    cv_part = tn(jnp.concatenate(key_sq, 0), jnp.concatenate(seq_gv, 0)).astype(bf16)
    chan_value_grad = scatter_weights(cv_part[None], team, spread)[0].astype(f32)
    ck_part = tn(jnp.concatenate(grad_key, 0), jnp.concatenate(seq_ck, 0)).astype(bf16)
    chan_key_grad = scatter_weights(ck_part[None], team, spread)[0].T.astype(f32)
    cr_part = tn(mixed_cr, grad_r2).astype(bf16)
    cr_part = cr_part.reshape(nd * members, cr_rows, nz * 2, cr_cols).transpose(0, 2, 1, 3)
    cr_part = cr_part.reshape(nd * members * nz * 2, cr_rows, cr_cols)
    chan_recept_grad = lax.psum_scatter(cr_part, every, scatter_dimension=0, tiled=False).astype(
        f32
    )
    spread_two = local_x2.astype(f32) - prev2.astype(f32)
    chan_mix_k_part = jnp.sum(grad_ck * spread_two, 0)
    chan_mix_r_part = jnp.sum(grad_cr * spread_two, 0)
    delayed_two = grad_ck * (1.0 - feedforward_lookup_blend) + grad_cr * (
        1.0 - feedforward_accept_blend
    )
    edge_up = lax.ppermute(delayed_two[:1], ("z", "c"), up)
    grad_x2 = (
        grad_ck * feedforward_lookup_blend
        + grad_cr * feedforward_accept_blend
        + jnp.concatenate([delayed_two[1:], edge_up], 0)
    )
    ln2_gain_part = jnp.sum(grad_x2 * hat2, 0)
    ln2_bias_part = jnp.sum(grad_x2, 0)
    grad_middle = cot + norm_back(grad_x2, hat2, inv2, later_layernorm_scale)
    grad_mix = grad_middle.astype(bf16)

    grad_z = nt(grad_mix, whole_o).astype(bf16)
    o_part = tn(z_rows, grad_mix).astype(bf16)
    o_part = o_part.reshape(2, members, nz, ATTN_WIDTH, nd * members, nb_cols)
    o_part = o_part.transpose(4, 2, 0, 1, 3, 5).reshape(
        nd * members * nz * 2, members * ATTN_WIDTH, nb_cols
    )
    weight_o_grad = lax.psum_scatter(o_part, every, scatter_dimension=0, tiled=False).astype(f32)
    grad_z = grad_z.reshape(tokens, 2, members, cols).transpose(1, 2, 0, 3)
    mine = lax.dynamic_index_in_dim(grad_z, ci, 0, keepdims=False)
    other = swap(lax.dynamic_index_in_dim(grad_z, 1 - ci, 0, keepdims=False), "c")
    pair = jnp.where(ci == 0, jnp.stack([mine, other], 1), jnp.stack([other, mine], 1))
    pair = reorder(pair.reshape(members, length, cols), team)
    grad_z = jnp.stack(team_exchange(pair, team))

    grad_gate, grad_y, added, gn_sums = gate_back(
        rate, gn_gain, gn_bias, grad_z, y, gate_pre, r
    )
    added = lax.all_gather(added, "z", axis=0, tiled=False)
    weight = fade((run_ids - zi - 1)[:, None])[:, None, None, :]
    end = jnp.sum(weight * added, 0)
    dr, dk, dv, mix_sums = mix_backward(rate, boost, end, begin, r, k, v, grad_y)
    first = jnp.sum(fade(run_ids[:, None])[:, None, None, :] * added, 0)
    first = lax.dynamic_slice_in_dim(first, zi * ATTN_WIDTH, ATTN_WIDTH, 2)
    first = reorder(jnp.stack(team_exchange(first, team)), team)
    initial_state_gradient = first.transpose(0, 2, 1)[None]

    grads = jnp.concatenate([dr, dk, dv, grad_gate], 2)
    edge = lax.ppermute(grads[:, :1], "z", [(i + 1, i) for i in range(nz - 1)])
    both = jnp.concatenate([grads, jnp.concatenate([grads[:, 1:], edge], 1)], 2)
    tall_w = jnp.concatenate([now_w, past_w], 0).reshape(8 * cols, width)
    tall_w, both = lax.optimization_barrier((tall_w, both))
    grad_x1 = reduce_tokens(lambda i: nn(both[i], tall_w).astype(bf16), team)
    wide_part = tn(grads.reshape(members * length, 4 * cols), whole_x1)
    wide_part = wide_part.reshape(4, cols, 2, width)
    now_part, past_part = wide_part[:, :, 0], wide_part[:, :, 1]
    mix_parts = jnp.sum(mix_f * (now_part - past_part), 1)
    weight_parts = (now_part * blends + past_part * (1.0 - blends)).astype(bf16)
    weight_grads = scatter_weights(weight_parts, team, spread)
    weight_r_grad, weight_k_grad, weight_v_grad, weight_g_grad = (
        weight_grads[i].T.astype(f32) for i in range(4)
    )
    ln1_gain_part = jnp.sum(grad_x1 * hat1, 0)
    ln1_bias_part = jnp.sum(grad_x1, 0)
    in_grad = grad_middle + norm_back(grad_x1, hat1, inv1, earlier_layernorm_scale)

    by_head = jnp.stack(
        [
            jnp.sum(gn_sums[:, :, 0], 0),
            jnp.sum(gn_sums[:, :, 1], 0),
            jnp.sum(mix_sums[:, :, 0], 0),
            jnp.sum(mix_sums[:, :, 1], 0),
        ]
    ).reshape(4, nz, 1, 1, ATTN_WIDTH)
    placed = lax.dynamic_update_slice(
        jnp.zeros((4, nz, 2, members, ATTN_WIDTH), f32), by_head, (0, 0, ci, member, 0)
    ).reshape(4, width)
    small = jnp.concatenate(
        [
            mix_parts,
            placed,
            jnp.stack(
                [
                    ln1_gain_part,
                    ln1_bias_part,
                    ln2_gain_part,
                    ln2_bias_part,
                    chan_mix_k_part,
                    chan_mix_r_part,
                ]
            ),
        ],
        0,
    )
    small = lax.psum(small, every)
    here = lax.dynamic_slice_in_dim(
        small[4:8].reshape(4, nz * 2, members * ATTN_WIDTH), zi * 2 + ci, 1, 1
    )[:, 0]
    per_head = here.reshape(4, members, ATTN_WIDTH)
    return (
        block_out,
        in_grad,
        initial_state_gradient,
        small[8],
        small[9],
        small[0],
        small[1],
        small[2],
        small[3],
        weight_r_grad,
        weight_k_grad,
        weight_v_grad,
        weight_g_grad,
        per_head[2],
        per_head[3],
        here[0],
        here[1],
        weight_o_grad,
        small[10],
        small[11],
        small[12],
        small[13],
        chan_key_grad,
        chan_value_grad,
        chan_recept_grad,
    )


def solution(mesh):
    nb, nh = mesh.shape["batch"], mesh.shape["head"]

    def whole(*args):
        attn_count = args[13].shape[0]
        members = attn_count // nh
        team = ("t1", "t0") if members == 4 else ("t0",)
        fine = Mesh(
            mesh.devices.reshape((nb // members,) + (2,) * len(team) + (nh // 2, 2)),
            ("d",) + team + ("z", "c"),
        )
        batch = ("d",) + team
        head = ("z", "c")
        tok = P(batch + head, None)
        state = P(batch, head, None, None)
        cols = P(batch, head)
        rows = P(head, batch)
        per_head = P(head, None)
        channel = P(head)
        same = P()
        in_specs = (
            (tok, state, tok)
            + (same,) * 6
            + (cols,) * 4
            + (per_head,) * 2
            + (channel,) * 2
            + (rows,)
            + (same,) * 4
            + (cols, rows, cols)
        )
        out_specs = (
            (tok, tok, state)
            + (same,) * 6
            + (cols,) * 4
            + (per_head,) * 2
            + (channel,) * 2
            + (rows,)
            + (same,) * 4
            + (cols, rows, cols)
        )
        return jax.shard_map(
            functools.partial(on_device, team),
            mesh=fine,
            in_specs=in_specs,
            out_specs=out_specs,
            check_vma=False,
        )(*args)

    return whole
```

time: 2750 us -> 1840 us (0.67)
  waiting for transfers between devices: 1190 us -> 680 us
  matrix products: 676 us -> 358 us
  other arithmetic: 426 us -> 248 us
  starting transfers between devices: 10.2 us -> 83.1 us
  Pallas kernels: 0 us -> 67.7 us
  blocking collectives: 86.1 us -> 34.7 us
    all_gather x13 -> x7, waiting for transfers between devices: 588 us -> 47.4 us  [the longest x3 47.4 us: gather_weights(): whole = lax.all_gather(mine, spread, axis=0, tiled=False)]
    ppermute x0 -> x88, waiting for transfers between devices: none -> 390 us  [the longest x74 360 us: swap(): return lax.ppermute(value, axis, [(0, 1), (1, 0)])]
    dot_general x36 -> x31, matrix products: 676 us -> 358 us  [the longest x5 144 us: tn(): lax.dot_general(left, right, (((0,), (0,)), ((), ())), preferred_element_...]
    all_to_all x2 -> x0, waiting for transfers between devices: 128 us -> none  [the longest x1 79.8 us: on_device(): lax.all_to_all(upstream_adjoint, 'head', split_axis=1, concat_axis=0, til...]
    reduce_scatter x11 -> x5, waiting for transfers between devices: 322 us -> 204 us  [the longest x1 129 us: on_device(): lax.psum_scatter(o_part, every, scatter_dimension=0, tiled=False)]
    reduce_sum x7 -> x4, other arithmetic: 117 us -> 3.53 us  [the longest x1 2.14 us: on_device(): first = jnp.sum(fade(run_ids[:, None])[:, None, None, :] * added, 0)]
    psum x1, waiting for transfers between devices: 149 us -> 38.2 us  [on_device(): small = lax.psum(small, every)]
    add x66 -> x8, other arithmetic: 121 us -> 14.9 us  [the longest x6 11.3 us: core_reduce(): return mine.astype(f32) + swap(other, 'c').astype(f32)]
  transfers between devices with their start and end apart: 27 -> 101, of which waited for: 13 -> 41; matrix products, arithmetic and copies ran while one was open for 45% -> 44% of each run, Pallas kernels for 0% -> 3%
where the time goes in v1:
time: 1840 us; the launch traced here: 1830 us
  waiting for transfers between devices  680 us (37%)
  matrix products  358 us (19%)
  local copies, waits for them, and re-layouts  339 us (18%)
  other arithmetic  248 us (13%)
  starting transfers between devices  83.1 us (5%)
  Pallas kernels  67.7 us (4%)
  blocking collectives  34.7 us (2%)
    ppermute x74, waiting for transfers between devices, swap(): return lax.ppermute(value, axis, [(0, 1), (1, 0)])  360 us
    dot_general x5, matrix products, tn(): lax.dot_general(left, right, (((0,), (0,)), ((), ())), preferred_element_...  144 us
    reduce_scatter x1, waiting for transfers between devices, on_device(): lax.psum_scatter(o_part, every, scatter_dimension=0, tiled=False)  129 us
    dot_general x14, matrix products, nn(): return jnp.dot(left, right, preferred_element_type=f32)  108 us
    dot_general x12, matrix products, nt(): lax.dot_general(left, right, (((1,), (1,)), ((), ())), preferred_element_...  106 us
    unnamed x275, local copies, waits for them, and re-layouts  77.9 us
    reduce_scatter x3, waiting for transfers between devices, scatter_weights(): mine = lax.psum_scatter(blocks, spread, scatter_dimension=0, tiled=False)  75.2 us
    ppermute x74, starting transfers between devices, swap(): return lax.ppermute(value, axis, [(0, 1), (1, 0)])  59.1 us
  transfers between devices with their start and end apart: 101, of which 41 were waited for; matrix products, arithmetic and copies ran while one was open for 44% of the time, Pallas kernels for 3%

profile of v1, /device:TPU:0, one launch (start us, length us, event | category | flops | bytes accessed | tf_op | source)
XLA Modules:
  0.0 1829.1 jit_solution(12022175744051181115)
XLA Ops:
  24.5 13.4 all-gather
  42.3 26.1 %collective-permute-done.3 = bf16[4,64,512]{2,1,0:T(8,128)(2,1)S(1)} collective-permute-done((bf16[4,64,512]{2,1,0:T(8,128)(2,1)S(1)}, bf16[4,64,512]{2,1,0:T(8,128)(2,1)S(1)}, u32[]{:S(2)}, u32[]{:S(2)}) %collective-permute-start.3) | collective-permute-done | bytes 262176 | tf_op jit(solution)/shard_map/ppermute | solution.py:320
  131.9 23.3 %pad_maximum_fusion = bf16[4,1024,4096]{2,1,0:T(8,128)(2,1)} fusion(bf16[1,1024,4096]{2,1,0:T(8,128)(2,1)} %maximum_bitcast_fusion.3, bf16[1,1024,4096]{2,1,0:T(8,128)(2,1)} %maximum_bitcast_fusion.2, bf16[1,1024,4096]{2,1,0:T(8,128)(2,1)} %maximum_bitcast_fusion.1, bf16[1,1024,4096]{2,1,0:T(8,128)(2,1)} %maximum_bitcast_fusion), kind=kLoop, calls=%fused_computation | loop fusion | flops 50331648 | bytes 67108864 | tf_op jit(solution)/shard_map/stack | solution.py:523
  168.4 12.1 copy.190
  201.9 31.9 %convolution_convert_fusion.2 = bf16[4096,768]{1,0:T(8,128)(2,1)S(1)} fusion(bf16[4096,4096]{1,0:T(8,128)(2,1)} %bitcast.541, bf16[1024,4096]{1,0:T(8,128)(2,1)} %pad_maximum_fusion.1), kind=kOutput, calls=%fused_computation.50 | convolution fusion | flops 25772949504 | bytes 46137344 | tf_op jit(solution)/shard_map/dot_general | solution.py:25
  253.1 21.4 %all-gather.1 = f32[16,64,64]{2,1,0:T(8,128)S(1)} all-gather(f32[4,64,64]{2,1,0:T(8,128)S(1)} %pad_maximum_fusion.14), channel_id=3, replica_groups=mesh['d'=1,'t1'=2,'t0'=2,'z'=4,'c'=2] {'z'}, dimensions={0}, use_global_device_ids=true | all-gather | bytes 327680 | tf_op jit(solution)/shard_map/all_gather | solution.py:558
  280.9 17.9 fusion.96
  300.1 18.5 %mix_forward.1 = (bf16[4,1024,256]{2,1,0:T(8,128)(2,1)S(1)}, f32[4,1024,256]{2,1,0:T(8,128)}, f32[4,4,64,256]{3,2,1,0:T(8,128)S(1)}) custom-call(f32[1,256]{1,0:T(1,128)S(1)} %exp.39.rate_ref, f32[1,256]{1,0:T(1,128)S(1)} %squeeze.187.boost_ref, f32[1,256]{1,0:T(1,128)S(1)} %squeeze.188.gain_ref, f32[1,256]{1,0:T(1,128)S(1)} %squeeze.189.bias_ref, ...), custom_call_target="tpu_custom_call" | custom-call | tf_op jit(solution)/shard_map/mix_forward/pallas_call | solution.py:254
  323.6 17.3 collective-permute-done.19
  346.2 10.5 collective-permute-done.20
  381.0 11.9 copy.193
  392.8 10.4 copy.243
  418.7 45.9 %collective-permute-done.32 = bf16[512,2048]{1,0:T(8,128)(2,1)} collective-permute-done((bf16[512,2048]{1,0:T(8,128)(2,1)S(1)}, bf16[512,2048]{1,0:T(8,128)(2,1)}, u32[]{:S(2)}, u32[]{:S(2)}) %collective-permute-start.32) | collective-permute-done | bytes 2097184 | tf_op jit(solution)/shard_map/ppermute | solution.py:320
  472.8 40.7 %all-gather.18.cloned.1.call-done = bf16[4,4,1,224,512]{4,3,2,1,0:T(8,128)(2,1)} async-done(((bf16[1,4,1,224,512]{4,3,2,1,0:T(8,128)(2,1)}), bf16[4,4,1,224,512]{4,3,2,1,0:T(8,128)(2,1)}) %all-gather.18.cloned.1.call-update) | async-done | bytes 3670032 | tf_op jit(solution)/shard_map/all_gather | solution.py:411
  535.9 16.4 collective-permute-done.35
  619.0 21.1 %collective-permute-done.40 = bf16[256,2048]{1,0:T(8,128)(2,1)S(1)} collective-permute-done((bf16[256,2048]{1,0:T(8,128)(2,1)S(1)}, bf16[256,2048]{1,0:T(8,128)(2,1)S(1)}, u32[]{:S(2)}, u32[]{:S(2)}) %collective-permute-start.40) | collective-permute-done | bytes 1048608 | tf_op jit(solution)/shard_map/ppermute | solution.py:320
  645.9 11.6 copy.194
  657.5 10.7 copy.244
  668.2 20.8 %collective-permute-done.41 = bf16[512,2048]{1,0:T(8,128)(2,1)} collective-permute-done((bf16[512,2048]{1,0:T(8,128)(2,1)}, bf16[512,2048]{1,0:T(8,128)(2,1)}, u32[]{:S(2)}, u32[]{:S(2)}) %collective-permute-start.41) | collective-permute-done | bytes 2097184 | tf_op jit(solution)/shard_map/ppermute | solution.py:320
  691.5 14.4 fusion.54
  707.5 43.9 %collective-permute-done.48 = bf16[512,2048]{1,0:T(8,128)(2,1)S(1)} collective-permute-done((bf16[512,2048]{1,0:T(8,128)(2,1)S(1)}, bf16[512,2048]{1,0:T(8,128)(2,1)S(1)}, u32[]{:S(2)}, u32[]{:S(2)}) %collective-permute-start.48) | collective-permute-done | bytes 2097184 | tf_op jit(solution)/shard_map/ppermute | solution.py:320
  761.9 15.3 collective-permute-done.51
  840.8 18.1 collective-permute-done.60
  871.4 36.6 %collective-permute-done.61 = bf16[512,2048]{1,0:T(8,128)(2,1)} collective-permute-done((bf16[512,2048]{1,0:T(8,128)(2,1)}, bf16[512,2048]{1,0:T(8,128)(2,1)}, u32[]{:S(2)}, u32[]{:S(2)}) %collective-permute-start.61) | collective-permute-done | bytes 2097184 | tf_op jit(solution)/shard_map/ppermute | solution.py:320
  951.0 12.2 collective-permute-done.66
  963.2 10.4 collective-permute-done.65
  975.3 17.8 gate_back.1
  994.5 39.8 %fusion.85 = bf16[896,2048]{1,0:T(8,128)(2,1)} fusion(bf16[1024,2048]{1,0:T(8,128)(2,1)} %copy-done.20, bf16[1024,2048]{1,0:T(8,128)(2,1)} %copy-done.19, bf16[1024,2048]{1,0:T(8,128)(2,1)} %copy-done.18, bf16[1024,2048]{1,0:T(8,128)(2,1)} %copy-done.17, bf16[1024,896]{1,0:T(8,128)(2,1)} %copy-done.111, bf16[1024,896]{1,0:T(8,128)(2,1)} %multiply_convert_fusion.2, ...), kind=kOutput, calls=%fused_computation.158 | convolution fusion | flops 15130689536 | bytes 27787264 | tf_op jit(solution)/shard_map/dot_general | solution.py:29
  1046.2 39.8 %fusion.80 = bf16[896,2048]{1,0:T(8,128)(2,1)} fusion(bf16[1024,2048]{1,0:T(8,128)(2,1)} %copy-done.24, bf16[1024,2048]{1,0:T(8,128)(2,1)} %copy-done.23, bf16[1024,2048]{1,0:T(8,128)(2,1)} %copy-done.22, bf16[1024,2048]{1,0:T(8,128)(2,1)} %copy-done.21, bf16[1024,896]{1,0:T(8,128)(2,1)} %copy-done.108, bf16[1024,896]{1,0:T(8,128)(2,1)} %get-tuple-element.293, ...), kind=kOutput, calls=%fused_computation.157 | convolution fusion | flops 15130689536 | bytes 27787264 | tf_op jit(solution)/shard_map/dot_general | solution.py:29
  1098.8 10.9 reshape.2212
  1109.7 41.6 %copy.209 = bf16[4096,4096]{1,0:T(8,128)(2,1)} copy(bf16[4096,4096]{0,1:T(8,128)(2,1)} %bitcast.543) | data formatting | bytes 67108864 | tf_op jit(solution)/shard_map/dot_general | solution.py:29
  1167.6 10.8 convolution_convert_fusion
  1207.5 28.5 %mix_backward.1 = (bf16[4,1024,256]{2,1,0:T(8,128)(2,1)S(1)}, bf16[4,1024,256]{2,1,0:T(8,128)(2,1)S(1)}, bf16[4,1024,256]{2,1,0:T(8,128)(2,1)}, f32[4,1,2,256]{3,2,1,0:T(2,128)S(1)}) custom-call(f32[1,256]{1,0:T(1,128)S(1)} %exp.39.rate_ref, f32[1,256]{1,0:T(1,128)S(1)} %squeeze.187.boost_ref, f32[4,64,256]{2,1,0:T(8,128)S(1)} %get-tuple-element.116.end_ref, ...), custom_call_target="tpu_custom_call" | custom-call | tf_op jit(solution)/shard_map/mix_backward/pallas_call | solution.py:302
  1251.5 11.3 copy.208
  1262.8 43.2 %fusion.142 = f32[4,256,2,2048]{3,1,2,0:T(8,128)} fusion(bf16[4,256,4096,1]{2,1,3,0:T(8,128)(2,1)} %bitcast.591, bf16[2,2048,4096,1]{2,1,0,3:T(8,128)(2,1)} %bitcast.549), kind=kOutput, calls=%fused_computation.420 | convolution fusion | flops 34359738368 | bytes 58720256 | tf_op jit(solution)/shard_map/dot_general | solution.py:29
  1323.9 12.9 fusion.77
  1337.0 10.8 fusion.74
  1349.8 10.8 fusion.71
  1362.8 11.2 fusion.68
  1387.6 18.9 %collective-permute-done.74 = bf16[256,2048]{1,0:T(8,128)(2,1)S(1)} collective-permute-done((bf16[256,2048]{1,0:T(8,128)(2,1)S(1)}, bf16[256,2048]{1,0:T(8,128)(2,1)S(1)}, u32[]{:S(2)}, u32[]{:S(2)}) %collective-permute-start.74) | collective-permute-done | bytes 1048608 | tf_op jit(solution)/shard_map/ppermute | solution.py:320
  1418.7 10.8 squeeze.218
  1429.5 10.9 squeeze.219
  1440.4 12.4 fusion.55
  1465.5 10.6 convolution_convert_fusion.1
  1476.1 14.8 reshape.2205
  1549.8 38.2 %all-reduce.2.cloned.1.call-done = f32[14,2048]{1,0:T(8,128)} async-done(((f32[14,2048]{1,0:T(8,128)}), f32[14,2048]{1,0:T(8,128)}) %all-reduce.2.cloned.1.call-update) | async-done | bytes 114704 | tf_op jit(solution)/shard_map/psum | solution.py:706
  1590.7 75.2 %reduce-scatter.6.cloned.1.call-done = bf16[1,4,4,64,512]{4,3,2,1,0:T(8,128)(2,1)} async-done(((bf16[4,4,4,64,512]{4,3,2,1,0:T(8,128)(2,1)}), bf16[1,4,4,64,512]{4,3,2,1,0:T(8,128)(2,1)}) %reduce-scatter.6.cloned.1.call-update) | async-done | bytes 1048592 | tf_op jit(solution)/shard_map/reduce_scatter | solution.py:427
  1692.0 128.5 %reduce-scatter.8.cloned.1.call-done = bf16[1,256,512]{2,1,0:T(8,128)(2,1)} async-done(((bf16[32,256,512]{2,1,0:T(8,128)(2,1)}), bf16[1,256,512]{2,1,0:T(8,128)(2,1)}) %reduce-scatter.8.cloned.1.call-update) | async-done | bytes 262160 | tf_op jit(solution)/shard_map/reduce_scatter | solution.py:639
  (739 shorter events, 668.2 us)
Async XLA Ops:
  7.3 154.6 %all-gather.14.cloned.1.call-start = ((), (), s32[]{:S(2)}) async-start(), calls=%async_computation.5 | async-start | bytes 5242880 | tf_op jit(solution)/shard_map/all_gather | solution.py:411
  14.0 57.7 %collective-permute-start.9 = (bf16[512,2048]{1,0:T(8,128)(2,1)}, bf16[512,2048]{1,0:T(8,128)(2,1)}, u32[]{:S(2)}, u32[]{:S(2)}) collective-permute-start(bf16[512,2048]{1,0:T(8,128)(2,1)} %fusion.40), channel_id=1, source_target_pairs={{0,8},{8,0},{1,9},{9,1},{2,10},{10,2},{3,11},{11,3},{4,12},{12,4},... | collective-permute-start | bytes 6291464 | tf_op jit(solution)/shard_map/ppermute | solution.py:320
  16.9 66.0 %collective-permute-start.12 = (bf16[512,2048]{1,0:T(8,128)(2,1)}, bf16[512,2048]{1,0:T(8,128)(2,1)}, u32[]{:S(2)}, u32[]{:S(2)}) collective-permute-start(bf16[512,2048]{1,0:T(8,128)(2,1)} %fusion.40), channel_id=1, source_target_pairs={{0,16},{16,0},{1,17},{17,1},{2,18},{18,2},{3,19},{19,3},{4,20},{20... | collective-permute-start | bytes 6291464 | tf_op jit(solution)/shard_map/ppermute | solution.py:320
  18.4 67.4 %collective-permute-start.6 = (bf16[512,2048]{1,0:T(8,128)(2,1)}, bf16[512,2048]{1,0:T(8,128)(2,1)}, u32[]{:S(2)}, u32[]{:S(2)}) collective-permute-start(bf16[512,2048]{1,0:T(8,128)(2,1)} %fusion.40), channel_id=1, source_target_pairs={{0,1},{1,0},{2,3},{3,2},{4,5},{5,4},{6,7},{7,6},{8,9},{9,8},{10,11... | collective-permute-start | bytes 6291464 | tf_op jit(solution)/shard_map/ppermute | solution.py:320
  23.7 44.7 %collective-permute-start.3 = (bf16[4,64,512]{2,1,0:T(8,128)(2,1)S(1)}, bf16[4,64,512]{2,1,0:T(8,128)(2,1)S(1)}, u32[]{:S(2)}, u32[]{:S(2)}) collective-permute-start(bf16[4,64,512]{2,1,0:T(8,128)(2,1)S(1)} %get-tuple-element.194), channel_id=1, source_target_pairs={{0,8},{8,0},{1,9},{9,1},{2,10},{10,2},{3,11},{11,3},{4,12},{12,4},... | collective-permute-start | bytes 786440 | tf_op jit(solution)/shard_map/ppermute | solution.py:320
  39.2 31.9 %collective-permute-start.5 = (bf16[4,64,512]{2,1,0:T(8,128)(2,1)S(1)}, bf16[4,64,512]{2,1,0:T(8,128)(2,1)S(1)}, u32[]{:S(2)}, u32[]{:S(2)}) collective-permute-start(bf16[4,64,512]{2,1,0:T(8,128)(2,1)S(1)} %get-tuple-element.195), channel_id=1, source_target_pairs={{0,16},{16,0},{1,17},{17,1},{2,18},{18,2},{3,19},{19,3},{4,20},{20... | collective-permute-start | bytes 786440 | tf_op jit(solution)/shard_map/ppermute | solution.py:320
  71.7 35.6 %collective-permute-start.10 = (bf16[512,2048]{1,0:T(8,128)(2,1)}, bf16[512,2048]{1,0:T(8,128)(2,1)S(1)}, u32[]{:S(2)}, u32[]{:S(2)}) collective-permute-start(bf16[512,2048]{1,0:T(8,128)(2,1)} %collective-permute-done.9), channel_id=1, source_target_pairs={{0,1},{1,0},{2,3},{3,2},{4,5},{5,4},{6,7},{7,6},{8,9},{9,8},{10,11... | collective-permute-start | bytes 6291464 | tf_op jit(solution)/shard_map/ppermute | solution.py:320
  79.7 219.0 %all-gather.20.cloned.1.call-start = ((), (), s32[]{:S(2)}) async-start(), calls=%async_computation.14 | async-start | bytes 1310720 | tf_op jit(solution)/shard_map/all_gather | solution.py:568
  85.8 30.1 %collective-permute-start.13 = (bf16[512,2048]{1,0:T(8,128)(2,1)}, bf16[512,2048]{1,0:T(8,128)(2,1)S(1)}, u32[]{:S(2)}, u32[]{:S(2)}) collective-permute-start(bf16[512,2048]{1,0:T(8,128)(2,1)} %collective-permute-done.12), channel_id=1, source_target_pairs={{0,1},{1,0},{2,3},{3,2},{4,5},{5,4},{6,7},{7,6},{8,9},{9,8},{10,11... | collective-permute-start | bytes 6291464 | tf_op jit(solution)/shard_map/ppermute | solution.py:320
  239.9 141.1 %all-gather.22.cloned.1.call-start = ((), (), s32[]{:S(2)}) async-start(), calls=%async_computation.15 | async-start | bytes 8650752 | tf_op jit(solution)/shard_map/all_gather | solution.py:532
  240.6 224.3 %all-gather.16.cloned.1.call-start = ((), (), s32[]{:S(2)}) async-start(), calls=%async_computation.6 | async-start | bytes 4587520 | tf_op jit(solution)/shard_map/all_gather | solution.py:411
  247.3 28.5 %collective-permute-start.27 = (bf16[1,224,512]{2,1,0:T(8,128)(2,1)}, bf16[1,224,512]{2,1,0:T(8,128)(2,1)S(1)}, u32[]{:S(2)}, u32[]{:S(2)}) collective-permute-start(bf16[1,224,512]{2,1,0:T(8,128)(2,1)} %get-tuple-element.241), channel_id=1, source_target_pairs={{0,16},{16,0},{1,17},{17,1},{2,18},{18,2},{3,19},{19,3},{4,20},{20... | collective-permute-start | bytes 688136 | tf_op jit(solution)/shard_map/ppermute | solution.py:320
  280.8 232.8 %all-gather.18.cloned.1.call-start = ((), (), s32[]{:S(2)}) async-start(), calls=%async_computation.7 | async-start | bytes 4587520 | tf_op jit(solution)/shard_map/all_gather | solution.py:411
  322.0 34.7 %collective-permute-start.20 = (bf16[1024,256]{1,0:T(8,128)(2,1)S(1)}, bf16[1024,256]{1,0:T(8,128)(2,1)S(1)}, u32[]{:S(2)}, u32[]{:S(2)}) collective-permute-start(bf16[1024,256]{1,0:T(8,128)(2,1)S(1)} %get-tuple-element.174), channel_id=1, source_target_pairs={{0,24},{8,16},{16,8},{24,0},{1,25},{9,17},{17,9},{25,1},{2,26},{10... | collective-permute-start | bytes 1572872 | tf_op jit(solution)/shard_map/ppermute | solution.py:328
  376.5 269.4 %all-gather.24.cloned.1.call-start = ((), (), s32[]{:S(2)}) async-start(), calls=%async_computation.16 | async-start | bytes 8650752 | tf_op jit(solution)/shard_map/all_gather | solution.py:538
  416.6 48.1 %collective-permute-start.32 = (bf16[512,2048]{1,0:T(8,128)(2,1)S(1)}, bf16[512,2048]{1,0:T(8,128)(2,1)}, u32[]{:S(2)}, u32[]{:S(2)}) collective-permute-start(bf16[512,2048]{1,0:T(8,128)(2,1)S(1)} %fusion.50), channel_id=1, source_target_pairs={{0,8},{8,0},{1,9},{9,1},{2,10},{10,2},{3,11},{11,3},{4,12},{12,4},... | collective-permute-start | bytes 6291464 | tf_op jit(solution)/shard_map/ppermute | solution.py:320
  417.3 106.0 %collective-permute-start.36 = (bf16[512,2048]{1,0:T(8,128)(2,1)S(1)}, bf16[512,2048]{1,0:T(8,128)(2,1)}, u32[]{:S(2)}, u32[]{:S(2)}) collective-permute-start(bf16[512,2048]{1,0:T(8,128)(2,1)S(1)} %fusion.50), channel_id=1, source_target_pairs={{0,16},{16,0},{1,17},{17,1},{2,18},{18,2},{3,19},{19,3},{4,20},{20... | collective-permute-start | bytes 6291464 | tf_op jit(solution)/shard_map/ppermute | solution.py:320
  418.7 107.5 %collective-permute-start.24 = (bf16[512,2048]{1,0:T(8,128)(2,1)S(1)}, bf16[512,2048]{1,0:T(8,128)(2,1)}, u32[]{:S(2)}, u32[]{:S(2)}) collective-permute-start(bf16[512,2048]{1,0:T(8,128)(2,1)S(1)} %fusion.50), channel_id=1, source_target_pairs={{0,1},{1,0},{2,3},{3,2},{4,5},{5,4},{6,7},{7,6},{8,9},{9,8},{10,11... | collective-permute-start | bytes 6291464 | tf_op jit(solution)/shard_map/ppermute | solution.py:320
  464.6 92.4 %collective-permute-start.33 = (bf16[512,2048]{1,0:T(8,128)(2,1)}, bf16[512,2048]{1,0:T(8,128)(2,1)}, u32[]{:S(2)}, u32[]{:S(2)}) collective-permute-start(bf16[512,2048]{1,0:T(8,128)(2,1)} %collective-permute-done.32), channel_id=1, source_target_pairs={{0,1},{1,0},{2,3},{3,2},{4,5},{5,4},{6,7},{7,6},{8,9},{9,8},{10,11... | collective-permute-start | bytes 6291464 | tf_op jit(solution)/shard_map/ppermute | solution.py:320
  464.7 740.2 %all-gather.26.cloned.1.call-start = ((), (), s32[]{:S(2)}) async-start(), calls=%async_computation.17 | async-start | bytes 1310720 | tf_op jit(solution)/shard_map/all_gather | solution.py:650
  521.7 30.6 %collective-permute-start.35 = (bf16[256,2048]{1,0:T(8,128)(2,1)S(1)}, bf16[256,2048]{1,0:T(8,128)(2,1)S(1)}, u32[]{:S(2)}, u32[]{:S(2)}) collective-permute-start(bf16[256,2048]{1,0:T(8,128)(2,1)S(1)} %slice.910), channel_id=1, source_target_pairs={{0,16},{16,0},{1,17},{17,1},{2,18},{18,2},{3,19},{19,3},{4,20},{20... | collective-permute-start | bytes 3145736 | tf_op jit(solution)/shard_map/ppermute | solution.py:320
  524.6 32.1 %collective-permute-start.37 = (bf16[256,2048]{1,0:T(8,128)(2,1)S(1)}, bf16[256,2048]{1,0:T(8,128)(2,1)S(1)}, u32[]{:S(2)}, u32[]{:S(2)}) collective-permute-start(bf16[256,2048]{1,0:T(8,128)(2,1)S(1)} %slice.911), channel_id=1, source_target_pairs={{0,8},{8,0},{1,9},{9,1},{2,10},{10,2},{3,11},{11,3},{4,12},{12,4},... | collective-permute-start | bytes 3145736 | tf_op jit(solution)/shard_map/ppermute | solution.py:320
  526.2 48.0 %collective-permute-start.42 = (bf16[512,2048]{1,0:T(8,128)(2,1)}, bf16[512,2048]{1,0:T(8,128)(2,1)S(1)}, u32[]{:S(2)}, u32[]{:S(2)}) collective-permute-start(bf16[512,2048]{1,0:T(8,128)(2,1)} %collective-permute-done.36), channel_id=1, source_target_pairs={{0,1},{1,0},{2,3},{3,2},{4,5},{5,4},{6,7},{7,6},{8,9},{9,8},{10,11... | collective-permute-start | bytes 6291464 | tf_op jit(solution)/shard_map/ppermute | solution.py:320
  557.0 27.1 %collective-permute-start.38 = (bf16[512,2048]{1,0:T(8,128)(2,1)S(1)}, bf16[512,2048]{1,0:T(8,128)(2,1)S(1)}, u32[]{:S(2)}, u32[]{:S(2)}) collective-permute-start(bf16[512,2048]{1,0:T(8,128)(2,1)S(1)} %pad_maximum_fusion.5), channel_id=1, source_target_pairs={{0,1},{1,0},{2,3},{3,2},{4,5},{5,4},{6,7},{7,6},{8,9},{9,8},{10,11... | collective-permute-start | bytes 6291464 | tf_op jit(solution)/shard_map/ppermute | solution.py:320
  573.7 42.0 %collective-permute-start.34 = (bf16[512,2048]{1,0:T(8,128)(2,1)S(1)}, bf16[512,2048]{1,0:T(8,128)(2,1)S(1)}, u32[]{:S(2)}, u32[]{:S(2)}) collective-permute-start(bf16[512,2048]{1,0:T(8,128)(2,1)S(1)} %constant_dynamic-slice_fusion.17), channel_id=1, source_target_pairs={{0,1},{1,0},{2,3},{3,2},{4,5},{5,4},{6,7},{7,6},{8,9},{9,8},{10,11... | collective-permute-start | bytes 6291464 | tf_op jit(solution)/shard_map/ppermute | solution.py:320
  613.5 54.7 %collective-permute-start.31 = (bf16[512,2048]{1,0:T(8,128)(2,1)}, bf16[512,2048]{1,0:T(8,128)(2,1)}, u32[]{:S(2)}, u32[]{:S(2)}) collective-permute-start(bf16[512,2048]{1,0:T(8,128)(2,1)} %constant_dynamic-slice_fusion.18), channel_id=1, source_target_pairs={{0,1},{1,0},{2,3},{3,2},{4,5},{5,4},{6,7},{7,6},{8,9},{9,8},{10,11... | collective-permute-start | bytes 6291464 | tf_op jit(solution)/shard_map/ppermute | solution.py:320
  642.0 47.1 %collective-permute-start.41 = (bf16[512,2048]{1,0:T(8,128)(2,1)}, bf16[512,2048]{1,0:T(8,128)(2,1)}, u32[]{:S(2)}, u32[]{:S(2)}) collective-permute-start(bf16[512,2048]{1,0:T(8,128)(2,1)} %pad_maximum_fusion.6), channel_id=1, source_target_pairs={{0,8},{8,0},{1,9},{9,1},{2,10},{10,2},{3,11},{11,3},{4,12},{12,4},... | collective-permute-start | bytes 6291464 | tf_op jit(solution)/shard_map/ppermute | solution.py:320
  644.7 46.8 %collective-permute-start.45 = (bf16[512,2048]{1,0:T(8,128)(2,1)}, bf16[512,2048]{1,0:T(8,128)(2,1)}, u32[]{:S(2)}, u32[]{:S(2)}) collective-permute-start(bf16[512,2048]{1,0:T(8,128)(2,1)} %pad_maximum_fusion.7), channel_id=1, source_target_pairs={{0,16},{16,0},{1,17},{17,1},{2,18},{18,2},{3,19},{19,3},{4,20},{20... | collective-permute-start | bytes 6291464 | tf_op jit(solution)/shard_map/ppermute | solution.py:320
  705.9 45.5 %collective-permute-start.48 = (bf16[512,2048]{1,0:T(8,128)(2,1)S(1)}, bf16[512,2048]{1,0:T(8,128)(2,1)S(1)}, u32[]{:S(2)}, u32[]{:S(2)}) collective-permute-start(bf16[512,2048]{1,0:T(8,128)(2,1)S(1)} %get-tuple-element.138), channel_id=1, source_target_pairs={{0,8},{8,0},{1,9},{9,1},{2,10},{10,2},{3,11},{11,3},{4,12},{12,4},... | collective-permute-start | bytes 6291464 | tf_op jit(solution)/shard_map/ppermute | solution.py:320
  707.0 45.7 %collective-permute-start.52 = (bf16[512,2048]{1,0:T(8,128)(2,1)S(1)}, bf16[512,2048]{1,0:T(8,128)(2,1)S(1)}, u32[]{:S(2)}, u32[]{:S(2)}) collective-permute-start(bf16[512,2048]{1,0:T(8,128)(2,1)S(1)} %get-tuple-element.138), channel_id=1, source_target_pairs={{0,16},{16,0},{1,17},{17,1},{2,18},{18,2},{3,19},{19,3},{4,20},{20... | collective-permute-start | bytes 6291464 | tf_op jit(solution)/shard_map/ppermute | solution.py:320
  707.5 45.9 %collective-permute-start.46 = (bf16[512,2048]{1,0:T(8,128)(2,1)S(1)}, bf16[512,2048]{1,0:T(8,128)(2,1)S(1)}, u32[]{:S(2)}, u32[]{:S(2)}) collective-permute-start(bf16[512,2048]{1,0:T(8,128)(2,1)S(1)} %get-tuple-element.138), channel_id=1, source_target_pairs={{0,1},{1,0},{2,3},{3,2},{4,5},{5,4},{6,7},{7,6},{8,9},{9,8},{10,11... | collective-permute-start | bytes 6291464 | tf_op jit(solution)/shard_map/ppermute | solution.py:320
  753.4 38.3 %collective-permute-start.58 = (bf16[512,2048]{1,0:T(8,128)(2,1)S(1)}, bf16[512,2048]{1,0:T(8,128)(2,1)}, u32[]{:S(2)}, u32[]{:S(2)}) collective-permute-start(bf16[512,2048]{1,0:T(8,128)(2,1)S(1)} %collective-permute-done.52), channel_id=1, source_target_pairs={{0,1},{1,0},{2,3},{3,2},{4,5},{5,4},{6,7},{7,6},{8,9},{9,8},{10,11... | collective-permute-start | bytes 6291464 | tf_op jit(solution)/shard_map/ppermute | solution.py:320
  791.2 43.0 %collective-permute-start.50 = (bf16[512,2048]{1,0:T(8,128)(2,1)S(1)}, bf16[512,2048]{1,0:T(8,128)(2,1)}, u32[]{:S(2)}, u32[]{:S(2)}) collective-permute-start(bf16[512,2048]{1,0:T(8,128)(2,1)S(1)} %constant_dynamic-slice_fusion.13), channel_id=1, source_target_pairs={{0,1},{1,0},{2,3},{3,2},{4,5},{5,4},{6,7},{7,6},{8,9},{9,8},{10,11... | collective-permute-start | bytes 6291464 | tf_op jit(solution)/shard_map/ppermute | solution.py:320
  832.1 39.3 %collective-permute-start.47 = (bf16[512,2048]{1,0:T(8,128)(2,1)}, bf16[512,2048]{1,0:T(8,128)(2,1)}, u32[]{:S(2)}, u32[]{:S(2)}) collective-permute-start(bf16[512,2048]{1,0:T(8,128)(2,1)} %constant_dynamic-slice_fusion.14), channel_id=1, source_target_pairs={{0,1},{1,0},{2,3},{3,2},{4,5},{5,4},{6,7},{7,6},{8,9},{9,8},{10,11... | collective-permute-start | bytes 6291464 | tf_op jit(solution)/shard_map/ppermute | solution.py:320
  860.8 47.2 %collective-permute-start.61 = (bf16[512,2048]{1,0:T(8,128)(2,1)}, bf16[512,2048]{1,0:T(8,128)(2,1)}, u32[]{:S(2)}, u32[]{:S(2)}) collective-permute-start(bf16[512,2048]{1,0:T(8,128)(2,1)} %pad_maximum_fusion.10), channel_id=1, source_target_pairs={{0,16},{16,0},{1,17},{17,1},{2,18},{18,2},{3,19},{19,3},{4,20},{20... | collective-permute-start | bytes 6291464 | tf_op jit(solution)/shard_map/ppermute | solution.py:320
  863.7 46.8 %collective-permute-start.57 = (bf16[512,2048]{1,0:T(8,128)(2,1)}, bf16[512,2048]{1,0:T(8,128)(2,1)S(1)}, u32[]{:S(2)}, u32[]{:S(2)}) collective-permute-start(bf16[512,2048]{1,0:T(8,128)(2,1)} %pad_maximum_fusion.9), channel_id=1, source_target_pairs={{0,8},{8,0},{1,9},{9,1},{2,10},{10,2},{3,11},{11,3},{4,12},{12,4},... | collective-permute-start | bytes 6291464 | tf_op jit(solution)/shard_map/ppermute | solution.py:320
  994.4 505.1 %reduce-scatter.10.cloned.1.call-start = ((), (), s32[]{:S(2)}) async-start(), calls=%async_computation.11 | async-start | bytes 4587520 | tf_op jit(solution)/shard_map/reduce_scatter | solution.py:427
  1046.1 454.5 %reduce-scatter.12.cloned.1.call-start = ((), (), s32[]{:S(2)}) async-start(), calls=%async_computation.12 | async-start | bytes 4587520 | tf_op jit(solution)/shard_map/reduce_scatter | solution.py:427
  1098.0 444.4 %reduce-scatter.14.cloned.1.call-start = ((), (), s32[]{:S(2)}) async-start(), calls=%async_computation.13 | async-start | bytes 8650752 | tf_op jit(solution)/shard_map/reduce_scatter | solution.py:613
  1204.7 383.3 %all-reduce.2.cloned.1.call-start = ((), (), s32[]{:S(2)}) async-start(), calls=%async_computation.8 | async-start | bytes 262144 | tf_op jit(solution)/shard_map/psum | solution.py:706
  1250.2 65.7 %collective-permute-start.67 = (bf16[4,1,1024]{2,1,0:T(2,128)(2,1)S(1)}, bf16[4,1,1024]{2,1,0:T(2,128)(2,1)S(1)}, u32[]{:S(2)}, u32[]{:S(2)}) collective-permute-start(bf16[4,1,1024]{2,1,0:T(2,128)(2,1)S(1)} %slice.938), channel_id=1, source_target_pairs={{2,0},{4,2},{6,4},{3,1},{5,3},{7,5},{10,8},{12,10},{14,12},{11,9},... | collective-permute-start | bytes 24584 | tf_op jit(solution)/shard_map/ppermute | solution.py:660
  1336.9 45.3 %collective-permute-start.73 = (bf16[512,2048]{1,0:T(8,128)(2,1)S(1)}, bf16[512,2048]{1,0:T(8,128)(2,1)}, u32[]{:S(2)}, u32[]{:S(2)}) collective-permute-start(bf16[512,2048]{1,0:T(8,128)(2,1)S(1)} %constant_dynamic-slice_fusion.5), channel_id=1, source_target_pairs={{0,1},{1,0},{2,3},{3,2},{4,5},{5,4},{6,7},{7,6},{8,9},{9,8},{10,11... | collective-permute-start | bytes 6291464 | tf_op jit(solution)/shard_map/ppermute | solution.py:320
  1375.8 77.1 %collective-permute-start.68 = (bf16[512,2048]{1,0:T(8,128)(2,1)}, bf16[512,2048]{1,0:T(8,128)(2,1)}, u32[]{:S(2)}, u32[]{:S(2)}) collective-permute-start(bf16[512,2048]{1,0:T(8,128)(2,1)} %constant_dynamic-slice_fusion.8), channel_id=1, source_target_pairs={{0,1},{1,0},{2,3},{3,2},{4,5},{5,4},{6,7},{7,6},{8,9},{9,8},{10,11... | collective-permute-start | bytes 6291464 | tf_op jit(solution)/shard_map/ppermute | solution.py:320
  1377.2 31.4 %collective-permute-start.71 = (bf16[256,2048]{1,0:T(8,128)(2,1)S(1)}, bf16[256,2048]{1,0:T(8,128)(2,1)S(1)}, u32[]{:S(2)}, u32[]{:S(2)}) collective-permute-start(bf16[256,2048]{1,0:T(8,128)(2,1)S(1)} %get-tuple-element.142), channel_id=1, source_target_pairs={{0,16},{16,0},{1,17},{17,1},{2,18},{18,2},{3,19},{19,3},{4,20},{20... | collective-permute-start | bytes 3145736 | tf_op jit(solution)/shard_map/ppermute | solution.py:320
  1408.3 46.7 %collective-permute-start.75 = (bf16[512,2048]{1,0:T(8,128)(2,1)}, bf16[512,2048]{1,0:T(8,128)(2,1)}, u32[]{:S(2)}, u32[]{:S(2)}) collective-permute-start(bf16[512,2048]{1,0:T(8,128)(2,1)} %pad_maximum_fusion.13), channel_id=1, source_target_pairs={{0,16},{16,0},{1,17},{17,1},{2,18},{18,2},{3,19},{19,3},{4,20},{20... | collective-permute-start | bytes 6291464 | tf_op jit(solution)/shard_map/ppermute | solution.py:320
  1410.6 46.7 %collective-permute-start.72 = (bf16[512,2048]{1,0:T(8,128)(2,1)}, bf16[512,2048]{1,0:T(8,128)(2,1)}, u32[]{:S(2)}, u32[]{:S(2)}) collective-permute-start(bf16[512,2048]{1,0:T(8,128)(2,1)} %pad_maximum_fusion.12), channel_id=1, source_target_pairs={{0,8},{8,0},{1,9},{9,1},{2,10},{10,2},{3,11},{11,3},{4,12},{12,4},... | collective-permute-start | bytes 6291464 | tf_op jit(solution)/shard_map/ppermute | solution.py:320
  1464.9 201.1 %reduce-scatter.6.cloned.1.call-start = ((), (), s32[]{:S(2)}) async-start(), calls=%async_computation.9 | async-start | bytes 5242880 | tf_op jit(solution)/shard_map/reduce_scatter | solution.py:427
  1465.4 355.1 %reduce-scatter.8.cloned.1.call-start = ((), (), s32[]{:S(2)}) async-start(), calls=%async_computation.10 | async-start | bytes 8650752 | tf_op jit(solution)/shard_map/reduce_scatter | solution.py:639
  (179 other events, 3408.3 us)
Sparse Core Ops, SparseCore 0:
  79.9 81.9 all-gather.13
  240.0 35.0 all-gather.19
  278.1 91.6 all-gather.21
  371.7 69.6 all-gather.15
  442.8 70.6 all-gather.17
  516.4 82.0 all-gather.23
  994.6 27.1 all-gather.25
  1046.2 67.6 reduce-scatter.9
  1116.2 68.7 reduce-scatter.11
  1204.8 152.8 reduce-scatter.13
  1465.0 122.9 all-reduce.1
  1590.1 75.7 reduce-scatter.5
  1668.3 152.1 reduce-scatter.7

commit v2 on v1

--- a/solution.py
+++ b/solution.py
@@ -212,7 +212,17 @@
     carry[...] = passed + jnp.where(blocks, tn(gy, qt), 0.0)
 
 
-VMEM_LIMIT = 48 * 1024 * 1024
+VMEM_LIMIT = 56 * 1024 * 1024
+params = pltpu.CompilerParams(vmem_limit_bytes=VMEM_LIMIT)
+
+
+def lasts(microseconds):
+    return pl.CostEstimate(
+        flops=int(FLOPS_PER_US * microseconds), bytes_accessed=0, transcendentals=0
+    )
+
+
+FLOPS_PER_US = 3e9
 
 
 def vec_spec():
@@ -231,30 +241,39 @@
     return jax.ShapeDtypeStruct(shape, dtype)
 
 
-def local_state(rate, k, v):
-    segs, length, width = k.shape
-    block = pl.BlockSpec((1, length, QUAD), lambda s, q: (s, 0, q))
+def local_state(rate, rkv):
+    _, segs, length, width = rkv.shape
+
+    def block(i):
+        return pl.BlockSpec((None, 1, length, QUAD), lambda s, q: (i, s, 0, q))
+
     return pl.pallas_call(
         local_state_kernel,
         grid=(segs, width // QUAD),
-        in_specs=[pl.BlockSpec((1, QUAD), lambda s, q: (0, q)), block, block],
+        in_specs=[pl.BlockSpec((1, QUAD), lambda s, q: (0, q)), block(1), block(2)],
         out_specs=pl.BlockSpec((1, ATTN_WIDTH, QUAD), lambda s, q: (s, 0, q)),
         out_shape=sds((segs, ATTN_WIDTH, width), f32),
-        compiler_params=pltpu.CompilerParams(vmem_limit_bytes=VMEM_LIMIT),
+        compiler_params=params,
+        cost_estimate=lasts(5),
         name="local_state",
-    )(rate, k, v)
-
-
-def mix_forward(rate, boost, gain, bias, s0, r, k, v, g):
-    segs, length, width = r.shape
+    )(rate, rkv, rkv)
+
+
+def mix_forward(rate, boost, gain, bias, s0, rkv, g):
+    _, segs, length, width = rkv.shape
     span = min(QUAD, length)
     count = length // span
     quads = width // QUAD
     block = pl.BlockSpec((1, span, QUAD), lambda s, q, c: (s, c, q))
+
+    def part(i):
+        return pl.BlockSpec((None, 1, span, QUAD), lambda s, q, c: (i, s, c, q))
+
     return pl.pallas_call(
         forward_kernel,
         grid=(segs, quads, count),
-        in_specs=[vec_spec()] * 4 + [state_spec()] + [block] * 4,
+        in_specs=[vec_spec()] * 4
+        + [state_spec(), part(0), part(1), part(2), block],
         out_specs=[
             block,
             block,
@@ -266,20 +285,22 @@
             sds((segs, count, ATTN_WIDTH, width), f32),
         ],
         scratch_shapes=[pltpu.VMEM((QUAD, QUAD), f32)],
-        compiler_params=pltpu.CompilerParams(vmem_limit_bytes=VMEM_LIMIT),
+        compiler_params=params,
+        cost_estimate=lasts(20),
         name="mix_forward",
-    )(rate, boost, gain, bias, s0, r, k, v, g)
-
-
-def gate_back(rate, gain, bias, gz, y, g, r):
-    segs, length, width = r.shape
+    )(rate, boost, gain, bias, s0, rkv, rkv, rkv, g)
+
+
+def gate_back(rate, gain, bias, gz, y, g, rkv):
+    _, segs, length, width = rkv.shape
     span = min(QUAD, length)
     quads = width // QUAD
     block = pl.BlockSpec((1, span, QUAD), lambda s, q, c: (s, c, q))
+    lead = pl.BlockSpec((None, 1, span, QUAD), lambda s, q, c: (0, s, c, q))
     return pl.pallas_call(
         gate_back_kernel,
         grid=(segs, quads, length // span),
-        in_specs=[vec_spec()] * 3 + [block] * 4,
+        in_specs=[vec_spec()] * 3 + [block, block, block, lead],
         out_specs=[block, block, state_spec(), sums_spec()],
         out_shape=[
             sds((segs, length, width), bf16),
@@ -288,17 +309,22 @@
             sds((segs, quads, 2, QUAD), f32),
         ],
         scratch_shapes=[pltpu.VMEM((QUAD, QUAD), f32)],
-        compiler_params=pltpu.CompilerParams(vmem_limit_bytes=VMEM_LIMIT),
+        compiler_params=params,
+        cost_estimate=lasts(18 / 8),
         name="gate_back",
-    )(rate, gain, bias, gz, y, g, r)
-
-
-def mix_backward(rate, boost, end, begin, r, k, v, gy):
-    segs, length, width = r.shape
+    )(rate, gain, bias, gz, y, g, rkv)
+
+
+def mix_backward(rate, boost, end, begin, rkv, gy):
+    _, segs, length, width = rkv.shape
     span = min(QUAD, length)
     count = length // span
     quads = width // QUAD
     block = pl.BlockSpec((1, span, QUAD), lambda s, q, c: (s, count - 1 - c, q))
+
+    def part(i):
+        return pl.BlockSpec((None, 1, span, QUAD), lambda s, q, c: (i, s, count - 1 - c, q))
+
     return pl.pallas_call(
         backward_kernel,
         grid=(segs, quads, count),
@@ -307,13 +333,423 @@
             state_spec(),
             pl.BlockSpec((1, 1, ATTN_WIDTH, QUAD), lambda s, q, c: (s, count - 1 - c, 0, q)),
         ]
-        + [block] * 4,
+        + [part(0), part(1), part(2), block],
         out_specs=[block, block, block, sums_spec()],
         out_shape=[sds((segs, length, width), bf16)] * 3 + [sds((segs, quads, 2, QUAD), f32)],
         scratch_shapes=[pltpu.VMEM((QUAD, QUAD), f32)],
-        compiler_params=pltpu.CompilerParams(vmem_limit_bytes=VMEM_LIMIT),
+        compiler_params=params,
+        cost_estimate=lasts(29 / 8),
         name="mix_backward",
-    )(rate, boost, end, begin, r, k, v, gy)
+    )(rate, boost, end, begin, rkv, rkv, rkv, gy)
+
+
+def project_kernel(core_ref, x_ref, halo_ref, w_ref, rkv_ref, gate_ref, carry):
+    x = x_ref[...]
+    now_w = w_ref[0].reshape(-1, x.shape[1])
+    past_w = w_ref[1].reshape(-1, x.shape[1])
+    now = nt(x, now_w)
+    past = nt(x, past_w)
+
+    @pl.when(pl.program_id(1) == 0)
+    def _():
+        carry[...] = nt(halo_ref[...], past_w)
+
+    rows = lax.broadcasted_iota(jnp.int32, past.shape, 0)
+    out = now + jnp.where(rows == 0, carry[0:1, :], pltpu.roll(past, 1, 0))
+    cols = gate_ref.shape[1]
+    for i in range(3):
+        rkv_ref[i] = out[:, i * cols : (i + 1) * cols].astype(bf16)
+    gate_ref[...] = out[:, 3 * cols :]
+    carry[0:1, :] = past[past.shape[0] - 1 :, :]
+
+
+def project(core, x, halos, weights):
+    segs, _, tokens, width = x.shape
+    cols = weights.shape[2]
+    spec = pltpu.PrefetchScalarGridSpec(
+        num_scalar_prefetch=1,
+        grid=(segs, 2),
+        in_specs=[
+            pl.BlockSpec((None, None, tokens, width), lambda s, h, core: (s, h ^ core[0], 0, 0)),
+            pl.BlockSpec((None, 8, width), lambda s, h, core: (s, 0, 0)),
+            pl.BlockSpec((2, 4, cols, width), lambda s, h, core: (0, 0, 0, 0)),
+        ],
+        out_specs=[
+            pl.BlockSpec((3, None, tokens, cols), lambda s, h, core: (0, s, h, 0)),
+            pl.BlockSpec((None, tokens, cols), lambda s, h, core: (s, h, 0)),
+        ],
+        scratch_shapes=[pltpu.VMEM((8, 4 * cols), f32)],
+    )
+    return pl.pallas_call(
+        project_kernel,
+        grid_spec=spec,
+        out_shape=[
+            sds((3, segs, 2 * tokens, cols), bf16),
+            sds((segs, 2 * tokens, cols), f32),
+        ],
+        compiler_params=params,
+        cost_estimate=lasts(50),
+        name="project",
+    )(core, x, halos, weights)
+
+
+def project_back_kernel(core_ref, r_ref, k_ref, v_ref, g_ref, edge_ref, w_ref, out_ref, carry):
+    refs = (r_ref, k_ref, v_ref, g_ref)
+    tokens = r_ref.shape[0]
+    now = jnp.concatenate([ref[...] for ref in refs], 1)
+
+    @pl.when(pl.program_id(0) == 0)
+    def _():
+        carry[...] = jnp.concatenate([edge_ref[i] for i in range(4)], 1).astype(f32)
+
+    wide = now.astype(f32)
+    rows = lax.broadcasted_iota(jnp.int32, wide.shape, 0)
+    later = jnp.where(rows == tokens - 1, carry[0:1, :], pltpu.roll(wide, tokens - 1, 0))
+    carry[0:1, :] = wide[0:1, :]
+    both = jnp.concatenate([now, later.astype(bf16)], 1)
+    out_ref[...] = nn(both, w_ref[...]).astype(bf16)
+
+
+def project_back(core, seg, grads, edges, weights):
+    segs, length, cols = grads[0].shape
+    tokens = length // 2
+    width = weights.shape[3]
+    block = pl.BlockSpec((None, tokens, cols), lambda h, core: (seg, 1 - h, 0))
+    spec = pltpu.PrefetchScalarGridSpec(
+        num_scalar_prefetch=1,
+        grid=(2,),
+        in_specs=[block] * 4
+        + [
+            pl.BlockSpec((None, 4, 8, cols), lambda h, core: (seg, 0, 0, 0)),
+            pl.BlockSpec((8 * cols, width), lambda h, core: (0, 0)),
+        ],
+        out_specs=pl.BlockSpec((None, tokens, width), lambda h, core: ((1 - h) ^ core[0], 0, 0)),
+        scratch_shapes=[pltpu.VMEM((8, 4 * cols), f32)],
+    )
+    return pl.pallas_call(
+        project_back_kernel,
+        grid_spec=spec,
+        out_shape=sds((2, tokens, width), bf16),
+        compiler_params=params,
+        cost_estimate=lasts(14 / 8),
+        name="project_back",
+    )(core, *grads, edges, weights.reshape(8 * cols, width))
+
+
+def mix_weight_kernel(count, core_ref, *refs):
+    grads, (edge_ref, x_ref, w_ref, blend_ref) = refs[:count], refs[count : count + 4]
+    out_ref, mix_ref, flat, total = refs[count + 4 :]
+    group, tile = pl.program_id(0), pl.program_id(1)
+    segs, length, cols = grads[0].shape
+    tokens = length // 2
+
+    @pl.when(tile == 0)
+    def _():
+        for s in range(segs):
+            for i, ref in enumerate(grads):
+                here = ref[s].astype(f32)
+                rows = lax.broadcasted_iota(jnp.int32, here.shape, 0)
+                later = jnp.where(
+                    rows == length - 1,
+                    edge_ref[s, i, 0:1, :].astype(f32),
+                    pltpu.roll(here, length - 1, 0),
+                )
+                for h in range(2):
+                    at = pl.multiple_of((2 * s + (h ^ core_ref[0])) * tokens, tokens)
+                    part = slice(h * tokens, (h + 1) * tokens)
+                    flat[i * cols : (i + 1) * cols, pl.ds(at, tokens)] = here[part].T.astype(bf16)
+                    flat[(count + i) * cols : (count + i + 1) * cols, pl.ds(at, tokens)] = (
+                        later[part].T.astype(bf16)
+                    )
+
+    got = nn(flat[...], x_ref[...].reshape(segs * length, x_ref.shape[3]))
+    final = group == pl.num_programs(0) - 1
+
+    @pl.when(jnp.logical_and(group == 0, jnp.logical_not(final)))
+    def _():
+        total[tile] = got
+
+    @pl.when(jnp.logical_and(group > 0, jnp.logical_not(final)))
+    def _():
+        total[tile] += got
+
+    @pl.when(final)
+    def _():
+        whole = jnp.where(group == 0, 0.0, total[tile]) + got
+        nz, fine = out_ref.shape[0], out_ref.shape[2]
+        for i in range(count):
+            a = whole[i * cols : (i + 1) * cols]
+            b = whole[(count + i) * cols : (count + i + 1) * cols]
+            blend = blend_ref[i]
+            grad = (a * blend + b * (1.0 - blend)).astype(bf16)
+            mix_ref[i] = jnp.sum(w_ref[i].astype(f32) * (a - b), 0, keepdims=True)
+            for z in range(nz):
+                out_ref[z, i] = grad[z * fine : (z + 1) * fine]
+
+
+def mix_weight_grads(core, grads, edges, x, plain, blends, nd, members, nz):
+    count = len(grads)
+    segs, length, cols = grads[0].shape
+    tokens = length // 2
+    width = x.shape[3]
+    tiles = nd * members
+    tile = width // tiles
+    fine = cols // nz
+    groups = segs // 2
+    block = pl.BlockSpec((2, length, cols), lambda t, n, core: (t, 0, 0))
+
+    def last(t, n):
+        return jnp.where(t == groups - 1, n, 0)
+
+    spec = pltpu.PrefetchScalarGridSpec(
+        num_scalar_prefetch=1,
+        grid=(groups, tiles),
+        in_specs=[block] * count
+        + [
+            pl.BlockSpec((2, count, 8, cols), lambda t, n, core: (t, 0, 0, 0)),
+            pl.BlockSpec((2, 2, tokens, tile), lambda t, n, core: (t, 0, 0, n)),
+            pl.BlockSpec((count, cols, tile), lambda t, n, core: (0, 0, last(t, n))),
+            pl.BlockSpec((count, 1, tile), lambda t, n, core: (0, 0, last(t, n))),
+        ],
+        out_specs=[
+            pl.BlockSpec(
+                (None, nz, None, count, fine, tile),
+                lambda t, n, core: (last(t, n) // members, 0, last(t, n) % members, 0, 0, 0),
+            ),
+            pl.BlockSpec((count, 1, tile), lambda t, n, core: (0, 0, last(t, n))),
+        ],
+        scratch_shapes=[
+            pltpu.VMEM((2 * count * cols, 2 * length), bf16),
+            pltpu.VMEM((tiles, 2 * count * cols, tile), f32),
+        ],
+    )
+    return pl.pallas_call(
+        functools.partial(mix_weight_kernel, count),
+        grid_spec=spec,
+        out_shape=[
+            sds((nd, nz, members, count, fine, tile), bf16),
+            sds((count, 1, width), f32),
+        ],
+        compiler_params=params,
+        cost_estimate=lasts(13 * count / 8),
+        name="mix_weight_grads",
+    )(core, *grads, edges, x, plain, blends[:, None, :])
+
+
+def outer_kernel(count, *refs):
+    lefts, rights = refs[:count], refs[count : 2 * count]
+    out_ref, flat, total = refs[2 * count :]
+    group, tile = pl.program_id(0), pl.program_id(1)
+    length = lefts[0].shape[0]
+    final = group == count // 2 - 1
+    for i in range(count // 2):
+
+        @pl.when(group == i)
+        def _(i=i):
+            @pl.when(tile == 0)
+            def _():
+                flat[:, :length] = lefts[2 * i][...].T
+                flat[:, length:] = lefts[2 * i + 1][...].T
+
+            got = nn(flat[...], jnp.concatenate([rights[2 * i][...], rights[2 * i + 1][...]], 0))
+            if i > 0:
+                got = got + total[tile]
+            if i < count // 2 - 1:
+                total[tile] = got
+            else:
+                nz, fine = out_ref.shape[0], out_ref.shape[2]
+                low = got.astype(bf16)
+                for z in range(nz):
+                    out_ref[z, 0] = low[z * fine : (z + 1) * fine, :]
+
+
+def outer_grads(lefts, rights, nd, members, nz):
+    length, rows = lefts[0].shape
+    width = rights[0].shape[1]
+    tiles = nd * members
+    tile = width // tiles
+    fine = rows // nz
+    count = len(lefts)
+    groups = count // 2
+
+    def right(i):
+        def index(t, n):
+            return 0, jnp.where(t < i // 2, 0, jnp.where(t > i // 2, tiles - 1, n))
+
+        return pl.BlockSpec((length, tile), index)
+
+    def last(t, n):
+        return jnp.where(t == groups - 1, n, 0)
+
+    return pl.pallas_call(
+        functools.partial(outer_kernel, count),
+        grid=(groups, tiles),
+        in_specs=[pl.BlockSpec((length, rows), lambda t, n: (0, 0))] * count
+        + [right(i) for i in range(count)],
+        out_specs=pl.BlockSpec(
+            (None, nz, None, 1, fine, tile),
+            lambda t, n: (last(t, n) // members, 0, last(t, n) % members, 0, 0, 0),
+        ),
+        out_shape=sds((nd, nz, members, 1, fine, tile), bf16),
+        scratch_shapes=[
+            pltpu.VMEM((rows, 2 * length), bf16),
+            pltpu.VMEM((tiles, rows, tile), f32),
+        ],
+        compiler_params=params,
+        cost_estimate=lasts(25 / 8),
+        name="outer_grads",
+    )(*lefts, *rights)
+
+
+def side_kernel(nd, nz, where_ref, z_ref, gm_ref, gr_ref, cr_ref, out_ref, z_flat, gr_flat):
+    distance = pl.program_id(0)
+    members = pl.num_programs(0)
+    core, member = where_ref[0], where_ref[1]
+    width = z_ref.shape[1]
+    cols = width // (nd * members)
+    half = width // 2
+    head = half // nz
+
+    @pl.when(distance == 0)
+    def _():
+        z_flat[...] = z_ref[...].T
+        for c in range(2):
+            for z in range(nz):
+                at = (2 * z + c) * head
+                gr_flat[c * half + z * head : c * half + (z + 1) * head, :] = (
+                    gr_ref[:, at : at + head].T
+                )
+
+    for d in range(nd):
+        at = pl.multiple_of((d * members + (member ^ distance)) * cols, cols)
+        for i, (flat, right) in enumerate(((z_flat, gm_ref), (gr_flat, cr_ref))):
+            got = nn(flat[...], right[:, pl.ds(at, cols)]).astype(bf16)
+            place = slice(i * nd * cols + d * cols, i * nd * cols + (d + 1) * cols)
+            for c in range(2):
+                out_ref[c ^ core, :, place] = got[c * half : (c + 1) * half]
+
+
+def side_grads(where, z_rows, grad_mix, grad_r2, mixed_cr, nd, members, nz):
+    tokens, width = z_rows.shape
+    wide = width // members
+    whole = pl.BlockSpec((tokens, width), lambda i, where: (0, 0))
+    out = pl.pallas_call(
+        functools.partial(side_kernel, nd, nz),
+        grid_spec=pltpu.PrefetchScalarGridSpec(
+            num_scalar_prefetch=1,
+            grid=(members,),
+            in_specs=[whole] * 4,
+            out_specs=pl.BlockSpec(
+                (None, 2, width // 2, 2 * wide), lambda i, where: (i, 0, 0, 0)
+            ),
+            scratch_shapes=[pltpu.VMEM((width, tokens), bf16)] * 2,
+        ),
+        out_shape=sds((members, 2, width // 2, 2 * wide), bf16),
+        compiler_params=params,
+        cost_estimate=lasts(17 / 8),
+        name="side_grads",
+    )(where, z_rows, grad_mix, grad_r2, mixed_cr)
+    return out.reshape(members, width, 2 * wide)
+
+
+def place_mix_kernel(in_ref, blend_ref, both_ref):
+    nd, members = in_ref.shape[0], in_ref.shape[1]
+    cols = in_ref.shape[3]
+    blend = blend_ref[...]
+    for d in range(nd):
+        for b in range(members):
+            place = slice((d * members + b) * cols, (d * members + b + 1) * cols)
+            w = in_ref[d, b].astype(f32)
+            m = blend[:, place]
+            both_ref[0, :, place] = (w * m).astype(bf16)
+            both_ref[1, :, place] = (w * (1.0 - m)).astype(bf16)
+
+
+def place_mix(raw, blends):
+    nd, nz, members, n, fine, cols = raw.shape
+    width = nd * members * cols
+    return pl.pallas_call(
+        place_mix_kernel,
+        grid=(n, nz),
+        in_specs=[
+            pl.BlockSpec((nd, None, members, None, fine, cols), lambda i, z: (0, z, 0, i, 0, 0)),
+            pl.BlockSpec((None, 1, width), lambda i, z: (i, 0, 0)),
+        ],
+        out_specs=pl.BlockSpec((2, None, fine, width), lambda i, z: (0, i, z, 0)),
+        out_shape=sds((2, n, nz * fine, width), bf16),
+        compiler_params=params,
+        cost_estimate=lasts(11),
+        name="place_mix",
+    )(raw, blends)
+
+
+def place_emission_kernel(in_ref, out_ref):
+    cols = in_ref.shape[3]
+    for b in range(in_ref.shape[0]):
+        out_ref[:, :, b * cols : (b + 1) * cols] = in_ref[b]
+
+
+def place_emission(raw):
+    nb, nz, nc, members, fine, cols = raw.shape
+    out = pl.pallas_call(
+        place_emission_kernel,
+        grid=(nc, nz),
+        in_specs=[
+            pl.BlockSpec((nb, None, None, members, fine, cols), lambda c, z: (0, z, c, 0, 0, 0))
+        ],
+        out_specs=pl.BlockSpec((None, members, fine, nb * cols), lambda c, z: (c, 0, z, 0)),
+        out_shape=sds((nc, members, nz * fine, nb * cols), bf16),
+        compiler_params=params,
+        cost_estimate=lasts(9),
+        name="place_emission",
+    )(raw)
+    return out.reshape(nc * members * nz * fine, nb * cols)
+
+
+def place_accept_kernel(in_ref, out_ref):
+    cols = in_ref.shape[2]
+    for h in range(in_ref.shape[0]):
+        out_ref[:, h * cols : (h + 1) * cols] = in_ref[h]
+
+
+def place_accept(raw):
+    nb, nh, rows, cols = raw.shape
+    return pl.pallas_call(
+        place_accept_kernel,
+        grid=(nb,),
+        in_specs=[pl.BlockSpec((None, nh, rows, cols), lambda b: (b, 0, 0, 0))],
+        out_specs=pl.BlockSpec((rows, nh * cols), lambda b: (b, 0)),
+        out_shape=sds((nb * rows, nh * cols), bf16),
+        compiler_params=params,
+        cost_estimate=lasts(7),
+        name="place_accept",
+    )(raw)
+
+
+def place_kernel(in_ref, out_ref):
+    nd, members = in_ref.shape[0], in_ref.shape[1]
+    cols = in_ref.shape[3]
+    for d in range(nd):
+        for b in range(members):
+            place = slice((d * members + b) * cols, (d * members + b + 1) * cols)
+            out_ref[:, place] = in_ref[d, b]
+
+
+def place_rows(raw):
+    nd, nz, members, n, fine, cols = raw.shape
+    width = nd * members * cols
+    return pl.pallas_call(
+        place_kernel,
+        grid=(n, nz),
+        in_specs=[
+            pl.BlockSpec((nd, None, members, None, fine, cols), lambda i, z: (0, z, 0, i, 0, 0))
+        ],
+        out_specs=pl.BlockSpec((None, fine, width), lambda i, z: (i, z, 0)),
+        out_shape=sds((n, nz * fine, width), bf16),
+        compiler_params=params,
+        cost_estimate=lasts(5),
+        name="place_rows",
+    )(raw)
 
 
 def swap(value, axis):
@@ -364,69 +800,128 @@
     return [value, near, side, corner]
 
 
-def core_pair(value):
-    other = swap(value, "c")
-    first = lax.axis_index("c") == 0
-    return jnp.where(
-        first, jnp.concatenate([value, other], 0), jnp.concatenate([other, value], 0)
-    )
-
-
-def gather_tokens(value, team):
-    return [core_pair(piece) for piece in team_copies(value, team)]
+def after(value, *events):
+    return lax.optimization_barrier((value, events))[0]
+
+
+def tie_kernel(*refs):
+    pass
+
+
+def tie(value, *events):
+    anywhere = pl.BlockSpec(memory_space=pl.ANY)
+    return pl.pallas_call(
+        tie_kernel,
+        in_specs=[anywhere] * (1 + len(events)),
+        out_specs=anywhere,
+        out_shape=sds(value.shape, value.dtype),
+        input_output_aliases={0: 0},
+        name="tie",
+    )(value, *events)
+
+
+def gather_tokens(value, team, event=None):
+    pieces = team_copies(value, team)
+    if event is not None:
+        pieces[1:-1] = [after(piece, event) for piece in pieces[1:-1]]
+    return [jnp.concatenate([piece, swap(piece, "c")], 0) for piece in pieces]
 
 
 def core_reduce(part):
     tokens = part.shape[0] // 2
-    core = lax.axis_index("c")
-    mine = lax.dynamic_slice_in_dim(part, core * tokens, tokens, 0)
-    other = lax.dynamic_slice_in_dim(part, (1 - core) * tokens, tokens, 0)
-    return mine.astype(f32) + swap(other, "c").astype(f32)
-
-
-def reduce_tokens(make_part, team):
+    return part[:tokens].astype(f32) + swap(part[tokens:], "c").astype(f32)
+
+
+def reduce_tokens(make_part, team, early=None, late=None, hold=None, finish=None):
+    def free(value):
+        return value
+
+    extra = None
     if len(team) == 1:
-        away = core_reduce(make_part(1)).astype(bf16)
+        away = core_reduce(make_part(1, free)).astype(bf16)
+
+        def pin(value):
+            return after(value, away)
+
         got = swap(away, team[0])
-        return core_reduce(make_part(0)) + got.astype(f32)
-    corner = core_reduce(make_part(3)).astype(bf16)
+        work = early or late
+        own = core_reduce(make_part(0, pin))
+        if work:
+            extra = work(pin)
+            own = after(own, extra)
+        return own + got.astype(f32), extra
+    corner = core_reduce(make_part(3, free)).astype(bf16)
     half = corner.shape[0] // 2
     to_near = swap(corner[:half], team[0])
     to_side = swap(corner[half:], team[1])
-    near = core_reduce(make_part(1))
+    if early:
+        extra = early(lambda v: after(v, corner))
+        near, side = make_part(1, lambda v: after(v, extra)), make_part(2, lambda v: after(v, extra))
+    else:
+        near, side = make_part(1, free), make_part(2, free)
+    if hold is not None:
+        near, side = tie(near, hold), tie(side, hold)
+    near, side = core_reduce(near), core_reduce(side)
     near = jnp.concatenate([near[:half] + to_near.astype(f32), near[half:]], 0).astype(bf16)
+    side = jnp.concatenate([side[:half], side[half:] + to_side.astype(f32)], 0).astype(bf16)
+
+    def pin(value):
+        return after(value, near, side)
+
     from_near = swap(near, team[1])
-    side = core_reduce(make_part(2))
-    side = jnp.concatenate([side[:half], side[half:] + to_side.astype(f32)], 0).astype(bf16)
     from_side = swap(side, team[0])
-    return core_reduce(make_part(0)) + from_near.astype(f32) + from_side.astype(f32)
-
-
-def gather_weights(shards, team, spread):
+    own = core_reduce(make_part(0, pin))
+    if late:
+        extra = late(pin)
+        own = after(own, extra)
+    if finish is not None:
+        own = tie(own, finish)
+    return own + from_near.astype(f32) + from_side.astype(f32), extra
+
+
+def split_rows(shards, team):
     n, rows, cols = shards.shape
     members = team_size(team)
-    fine = rows // members
-    blocks = shards.reshape(n, members, fine, cols).transpose(1, 0, 2, 3)
-    mine = abs_exchange(blocks, team)
+    blocks = shards.reshape(n, members, rows // members, cols).transpose(1, 0, 2, 3)
+    return abs_exchange(blocks, team)
+
+
+def along_z(mine, spread):
     whole = lax.all_gather(mine, spread, axis=0, tiled=False)
-    nz = lax.axis_size("z")
-    nd = whole.shape[0] // nz
-    whole = whole.reshape(nd, nz, members, n, fine, cols)
-    return whole.transpose(3, 1, 4, 0, 2, 5).reshape(n, nz * fine, nd * members * cols)
-
-
-def scatter_weights(grads, team, spread):
-    n, rows, width = grads.shape
-    members = team_size(team)
-    nz = lax.axis_size("z")
-    nd = lax.axis_size("d")
-    fine = rows // nz
-    cols = width // (nd * members)
-    blocks = grads.reshape(n, nz, fine, nd, members, cols).transpose(3, 1, 4, 0, 2, 5)
-    blocks = blocks.reshape(nd * nz, members, n, fine, cols)
-    mine = lax.psum_scatter(blocks, spread, scatter_dimension=0, tiled=False)
+    return whole.reshape((-1, lax.axis_size("z")) + mine.shape)
+
+
+def scatter_weights(grads, spread):
+    nd, nz, members, n, fine, cols = grads.shape
+    blocks = grads.reshape(nd * nz, members, n, fine, cols)
+    return lax.psum_scatter(blocks, spread, scatter_dimension=0, tiled=False)
+
+
+def join_rows(mine, team):
+    members, n, fine, cols = mine.shape
     mine = abs_exchange(mine, team)
     return mine.transpose(1, 0, 2, 3).reshape(n, members * fine, cols)
+
+
+def z_ring(value):
+    nz = lax.axis_size("z")
+    got = [value] + [
+        lax.ppermute(value, "z", [((i + s) % nz, i) for i in range(nz)]) for s in range(1, nz)
+    ]
+    twice = jnp.stack(got + got)
+    start = (nz - lax.axis_index("z")) % nz
+    return lax.dynamic_slice_in_dim(twice, start, nz, 0)
+
+
+def sum_everywhere(value, team):
+    for axis in ("c",) + team[::-1]:
+        value = value + swap(value, axis)
+    nz = lax.axis_size("z")
+    step = 1
+    while step < nz:
+        value = value + lax.ppermute(value, "z", [(i, i ^ step) for i in range(nz)])
+        step *= 2
+    return lax.psum(value, "d") if lax.axis_size("d") > 1 else value
 
 
 def layer_norm(payload_lines, gain, bias):
@@ -494,10 +989,25 @@
     down = [(i, i + 1) for i in line[:-1]]
     up = [(i + 1, i) for i in line[:-1]]
 
+    core = ci[None].astype(jnp.int32)
+
     mix_shards = jnp.stack(
         [w.T for w in (accept_weights, lookup_weights, payload_weights, valve_weights)]
     )
-    mix_w = gather_weights(mix_shards, team, spread)
+    mix_mine = split_rows(mix_shards, team)
+    residual = layer_source.astype(f32)
+    normed1, hat1, inv1 = layer_norm(residual, earlier_layernorm_scale, earlier_layernorm_shift)
+    local_x1 = normed1.astype(bf16)
+    mix_mine, local_x1 = lax.optimization_barrier((mix_mine, local_x1))
+    mix_raw = along_z(mix_mine, spread)
+    tail = lax.ppermute(layer_source[-1:], "z", [(i, i + 1) for i in range(nz - 1)])
+    tail = jnp.where(ci == 1, tail, swap(tail, "c"))
+    halo = layer_norm(tail.astype(f32), earlier_layernorm_scale, earlier_layernorm_shift)[0]
+    halo = jnp.where(zi > 0, halo, 0.0).astype(bf16)
+    halos = jnp.stack([jnp.pad(h, ((0, 7), (0, 0))) for h in team_copies(halo, team)])
+    whole_x1 = jnp.stack(gather_tokens(local_x1, team))
+    whole_x1 = whole_x1.reshape(members, 2, tokens, width)
+
     vectors = jnp.stack(
         [
             forgetting_loglog,
@@ -506,57 +1016,32 @@
             groupwise_shift.reshape(members, ATTN_WIDTH),
         ]
     )
-    vectors = lax.all_gather(vectors, "z", axis=0, tiled=False)
-    vectors = lax.dynamic_index_in_dim(vectors, member, 2, keepdims=False)
-    vectors = vectors.transpose(1, 0, 2).reshape(4, 1, heads_here * ATTN_WIDTH)
+    vectors = lax.dynamic_index_in_dim(vectors, member, 1, keepdims=False)
+    cols = heads_here * ATTN_WIDTH
+    vectors = z_ring(vectors).transpose(1, 0, 2).reshape(4, 1, cols)
     rate, boost, gn_gain, gn_bias = jnp.exp(vectors[0]), vectors[1], vectors[2], vectors[3]
-
-    residual = layer_source.astype(f32)
-    normed1, hat1, inv1 = layer_norm(residual, earlier_layernorm_scale, earlier_layernorm_shift)
-    local_x1 = normed1.astype(bf16)
-    tail = lax.ppermute(layer_source[-1:], "z", [(i, i + 1) for i in range(nz - 1)])
-    tail = jnp.where(ci == 1, tail, swap(tail, "c"))
-    halo = layer_norm(tail.astype(f32), earlier_layernorm_scale, earlier_layernorm_shift)[0]
-    halo = jnp.where(zi > 0, halo, 0.0).astype(bf16)
-    halos = team_copies(halo, team)
-    x1 = gather_tokens(local_x1, team)
-    whole_x1 = jnp.stack(
-        [
-            jnp.concatenate([now, jnp.concatenate([edge, now[:-1]], 0)], 1)
-            for now, edge in zip(x1, halos)
-        ]
-    )
-    whole_x1 = whole_x1.reshape(members * length, 2 * width)
+    opening = reorder(piecewise_opening_memory[0], team)
+    opening = z_ring(jnp.stack(team_exchange(opening, team)))
+    opening = opening.transpose(1, 3, 0, 2).reshape(members, ATTN_WIDTH, cols)
 
     nb_cols = emission_weights.shape[1]
-    whole_o = lax.all_gather(emission_weights, every, axis=0, tiled=False)
-    whole_o = whole_o.reshape(nd * members, nz, 2, members, ATTN_WIDTH, nb_cols)
-    whole_o = whole_o.transpose(2, 3, 1, 4, 0, 5).reshape(width, width)
-    lookup_t = gather_weights(feedforward_lookup_weights.T[None], team, spread)[0]
-    payload_w = gather_weights(feedforward_payload_weights[None], team, spread)[0]
     cr_rows, cr_cols = feedforward_accept_weights.shape
-    whole_cr = lax.all_gather(feedforward_accept_weights, every, axis=0, tiled=False)
-    whole_cr = whole_cr.reshape(nd * members, nz * 2, cr_rows, cr_cols)
-    whole_cr = whole_cr.transpose(0, 2, 1, 3).reshape(width, width)
-
-    blends = jnp.stack([accept_blend, lookup_blend, payload_blend, valve_blend])[:, None, :]
-    mix_f = mix_w.astype(f32)
-    now_w = (mix_f * blends).astype(bf16)
-    past_w = (mix_f * (1.0 - blends)).astype(bf16)
-    cols = heads_here * ATTN_WIDTH
-    wide_w = jnp.concatenate([now_w, past_w], 2).reshape(4 * cols, 2 * width)
-    wide_w, whole_x1 = lax.optimization_barrier((wide_w, whole_x1))
-    rkv = nt(whole_x1, wide_w[: 3 * cols]).astype(bf16)
-    gate_pre = nt(whole_x1, wide_w[3 * cols :])
-    r, k, v = (
-        rkv[:, i * cols : (i + 1) * cols].reshape(members, length, cols) for i in range(3)
-    )
-    gate_pre = gate_pre.reshape(members, length, cols)
-
-    opening = reorder(piecewise_opening_memory[0], team)
-    opening = jnp.stack(team_exchange(opening, team))
-    opening = lax.all_gather(opening, "z", axis=0, tiled=False)
-    opening = opening.transpose(1, 3, 0, 2).reshape(members, ATTN_WIDTH, cols)
+    lookup_raw = along_z(split_rows(feedforward_lookup_weights.T[None], team), spread)
+    payload_raw = along_z(split_rows(feedforward_payload_weights[None], team), spread)
+    o_raw = lax.all_gather(emission_weights, every, axis=0, tiled=False)
+    cr_raw = lax.all_gather(feedforward_accept_weights, every, axis=0, tiled=False)
+    whole_o = place_emission(
+        o_raw.reshape(nd * members, nz, 2, members, ATTN_WIDTH, nb_cols)
+    )
+    lookup_t = place_rows(lookup_raw)[0]
+    payload_w = place_rows(payload_raw)[0]
+    whole_cr = place_accept(cr_raw.reshape(nd * members, nz * 2, cr_rows, cr_cols))
+
+    blends = jnp.stack([accept_blend, lookup_blend, payload_blend, valve_blend])
+    both_w = place_mix(mix_raw, blends[:, None, :])
+    rkv, gate_pre = project(core, whole_x1, halos, both_w)
+    plain_w = place_rows(mix_raw)
+
     run_ids = jnp.arange(nz)
 
     def fade(steps):
@@ -564,11 +1049,11 @@
             steps >= 0, jnp.exp(-rate * (length * jnp.maximum(steps, 0)).astype(f32)), 0.0
         )
 
-    added = local_state(rate, k, v)
-    added = lax.all_gather(added, "z", axis=0, tiled=False)
+    added = local_state(rate, rkv)
+    added = z_ring(added.astype(bf16)).astype(f32)
     weight = fade((zi - 1 - run_ids)[:, None])[:, None, None, :]
     s0 = fade(zi[None, None]) * opening + jnp.sum(weight * added, 0)
-    z, y, begin = mix_forward(rate, boost, gn_gain, gn_bias, s0, r, k, v, gate_pre)
+    z, y, begin = mix_forward(rate, boost, gn_gain, gn_bias, s0, rkv, gate_pre)
 
     got = jnp.stack(team_exchange([z[i] for i in range(members)], team))
     got = reorder(got, team).reshape(members, 2, tokens, cols)
@@ -576,7 +1061,7 @@
     other = swap(lax.dynamic_index_in_dim(got, 1 - ci, 1, keepdims=False), "c")
     pair = jnp.where(ci == 0, jnp.stack([mine, other]), jnp.stack([other, mine]))
     z_rows = pair.transpose(2, 0, 1, 3).reshape(tokens, width)
-    middle = residual + nn(z_rows, whole_o)
+    middle = residual + nn(after(z_rows, payload_raw), whole_o)
 
     normed2, hat2, inv2 = layer_norm(middle, later_layernorm_scale, later_layernorm_shift)
     local_x2 = normed2.astype(bf16)
@@ -585,34 +1070,40 @@
     mixed_ck = token_mix(local_x2, prev2, feedforward_lookup_blend)
     mixed_cr = token_mix(local_x2, prev2, feedforward_accept_blend)
     seq_ck = gather_tokens(mixed_ck, team)
-    key_pre = [nt(piece, lookup_t) for piece in seq_ck]
+    key_pre = [nt(piece, lookup_t) for piece in seq_ck[:-1]]
+    key_pre.append(nt(after(seq_ck[-1], key_pre), lookup_t))
     key_relu = [jax.nn.relu(piece) for piece in key_pre]
     key_sq = [jnp.square(piece).astype(bf16) for piece in key_relu]
     key_relu = [piece.astype(bf16) for piece in key_relu]
-    value_sum = reduce_tokens(lambda i: nn(key_sq[i], payload_w).astype(bf16), team)
-    sig_two = jax.nn.sigmoid(nn(mixed_cr, whole_cr))
+    value_sum, recept2 = reduce_tokens(
+        lambda i, pin: nn(pin(key_sq[i]), payload_w).astype(bf16),
+        team,
+        late=lambda pin: nn(pin(mixed_cr), whole_cr),
+    )
+    sig_two = jax.nn.sigmoid(recept2)
     block_out = (middle + sig_two * value_sum).astype(bf16)
 
     cot = upstream_adjoint.astype(f32)
     grad_value = (cot * sig_two).astype(bf16)
     grad_r2 = (cot * value_sum * sig_two * (1.0 - sig_two)).astype(bf16)
     seq_gv = gather_tokens(grad_value, team)
-    grad_key = [
-        (nt(piece, payload_w) * (2.0 * held.astype(f32))).astype(bf16)
-        for piece, held in zip(seq_gv, key_relu)
-    ]
-    grad_ck = reduce_tokens(lambda i: nn(grad_key[i], lookup_t).astype(bf16), team)
-    grad_cr = nt(grad_r2, whole_cr)
-    cv_part = tn(jnp.concatenate(key_sq, 0), jnp.concatenate(seq_gv, 0)).astype(bf16)
-    chan_value_grad = scatter_weights(cv_part[None], team, spread)[0].astype(f32)
-    ck_part = tn(jnp.concatenate(grad_key, 0), jnp.concatenate(seq_ck, 0)).astype(bf16)
-    chan_key_grad = scatter_weights(ck_part[None], team, spread)[0].T.astype(f32)
-    cr_part = tn(mixed_cr, grad_r2).astype(bf16)
-    cr_part = cr_part.reshape(nd * members, cr_rows, nz * 2, cr_cols).transpose(0, 2, 1, 3)
-    cr_part = cr_part.reshape(nd * members * nz * 2, cr_rows, cr_cols)
-    chan_recept_grad = lax.psum_scatter(cr_part, every, scatter_dimension=0, tiled=False).astype(
-        f32
-    )
+    grad_key = []
+    for piece, kept in zip(seq_gv, key_relu):
+        if len(grad_key) == members - 1:
+            piece = tie(after(piece, grad_key), plain_w)
+        grad_key.append((nt(piece, payload_w) * (2.0 * kept.astype(f32))).astype(bf16))
+
+    def channel_weights(pin):
+        first = outer_grads([pin(key_sq[0])] + key_sq[1:], seq_gv, nd, members, nz)
+        second = outer_grads([pin(grad_key[0])] + grad_key[1:], seq_ck, nd, members, nz)
+        return first, second
+
+    grad_ck, (cv_part, ck_part) = reduce_tokens(
+        lambda i, pin: nn(pin(grad_key[i]), lookup_t).astype(bf16), team, late=channel_weights
+    )
+    grad_cr = lax.optimization_barrier(nt(grad_r2, whole_cr))
+    cv_sum = scatter_weights(cv_part, spread)
+    ck_sum = scatter_weights(after(ck_part, cv_sum), spread)
     spread_two = local_x2.astype(f32) - prev2.astype(f32)
     chan_mix_k_part = jnp.sum(grad_ck * spread_two, 0)
     chan_mix_r_part = jnp.sum(grad_cr * spread_two, 0)
@@ -631,12 +1122,6 @@
     grad_mix = grad_middle.astype(bf16)
 
     grad_z = nt(grad_mix, whole_o).astype(bf16)
-    o_part = tn(z_rows, grad_mix).astype(bf16)
-    o_part = o_part.reshape(2, members, nz, ATTN_WIDTH, nd * members, nb_cols)
-    o_part = o_part.transpose(4, 2, 0, 1, 3, 5).reshape(
-        nd * members * nz * 2, members * ATTN_WIDTH, nb_cols
-    )
-    weight_o_grad = lax.psum_scatter(o_part, every, scatter_dimension=0, tiled=False).astype(f32)
     grad_z = grad_z.reshape(tokens, 2, members, cols).transpose(1, 2, 0, 3)
     mine = lax.dynamic_index_in_dim(grad_z, ci, 0, keepdims=False)
     other = swap(lax.dynamic_index_in_dim(grad_z, 1 - ci, 0, keepdims=False), "c")
@@ -645,32 +1130,73 @@
     grad_z = jnp.stack(team_exchange(pair, team))
 
     grad_gate, grad_y, added, gn_sums = gate_back(
-        rate, gn_gain, gn_bias, grad_z, y, gate_pre, r
-    )
-    added = lax.all_gather(added, "z", axis=0, tiled=False)
+        rate, gn_gain, gn_bias, grad_z, y, gate_pre, rkv
+    )
+    added = z_ring(added.astype(bf16)).astype(f32)
     weight = fade((run_ids - zi - 1)[:, None])[:, None, None, :]
     end = jnp.sum(weight * added, 0)
-    dr, dk, dv, mix_sums = mix_backward(rate, boost, end, begin, r, k, v, grad_y)
+    dr, dk, dv, mix_sums = mix_backward(
+        rate, boost, end, begin, rkv, grad_y
+    )
     first = jnp.sum(fade(run_ids[:, None])[:, None, None, :] * added, 0)
     first = lax.dynamic_slice_in_dim(first, zi * ATTN_WIDTH, ATTN_WIDTH, 2)
     first = reorder(jnp.stack(team_exchange(first, team)), team)
     initial_state_gradient = first.transpose(0, 2, 1)[None]
 
-    grads = jnp.concatenate([dr, dk, dv, grad_gate], 2)
-    edge = lax.ppermute(grads[:, :1], "z", [(i + 1, i) for i in range(nz - 1)])
-    both = jnp.concatenate([grads, jnp.concatenate([grads[:, 1:], edge], 1)], 2)
-    tall_w = jnp.concatenate([now_w, past_w], 0).reshape(8 * cols, width)
-    tall_w, both = lax.optimization_barrier((tall_w, both))
-    grad_x1 = reduce_tokens(lambda i: nn(both[i], tall_w).astype(bf16), team)
-    wide_part = tn(grads.reshape(members * length, 4 * cols), whole_x1)
-    wide_part = wide_part.reshape(4, cols, 2, width)
-    now_part, past_part = wide_part[:, :, 0], wide_part[:, :, 1]
-    mix_parts = jnp.sum(mix_f * (now_part - past_part), 1)
-    weight_parts = (now_part * blends + past_part * (1.0 - blends)).astype(bf16)
-    weight_grads = scatter_weights(weight_parts, team, spread)
-    weight_r_grad, weight_k_grad, weight_v_grad, weight_g_grad = (
-        weight_grads[i].T.astype(f32) for i in range(4)
-    )
+    def edges_of(parts):
+        edges = jnp.stack([g[:, 0] for g in parts], 1)
+        edges = lax.ppermute(edges, "z", [(i + 1, i) for i in range(nz - 1)])
+        return jnp.pad(edges[:, :, None], ((0, 0), (0, 0), (0, 7), (0, 0)))
+
+    gate_edges = edges_of((grad_gate,))
+    gate_part, gate_mix = mix_weight_grads(
+        core, (grad_gate,), gate_edges, whole_x1, plain_w[3:], blends[3:], nd, members, nz
+    )
+    gate_sum = scatter_weights(gate_part, spread)
+    main_edges = edges_of((dr, dk, dv))
+    edges = tie(jnp.concatenate([main_edges, gate_edges], 1), cv_sum)
+
+    def main_weights(pin):
+        return mix_weight_grads(
+            core, (pin(dr), dk, dv), main_edges, whole_x1, plain_w[:3], blends[:3], nd, members, nz
+        )
+
+    grad_x1, (main_part, main_mix) = reduce_tokens(
+        lambda i, pin: project_back(
+            core, i, (pin(after(dr, ck_sum)), dk, dv, grad_gate), edges, both_w
+        ).reshape(length, width),
+        team,
+        early=main_weights,
+    )
+    where = jnp.stack([ci, member]).astype(jnp.int32)
+    side_parts = side_grads(
+        where, tie(z_rows, grad_y), grad_mix, grad_r2, mixed_cr, nd, members, nz
+    )
+    sides = reduce_tokens(
+        lambda i, pin: pin(side_parts)[i], team, hold=dr, finish=main_part
+    )[0].astype(bf16)
+    sides = sides.reshape(width // 2, 2, nd, nb_cols)
+    o_sum = sides[:, 0].reshape(members, nz, ATTN_WIDTH, nd, nb_cols)
+    o_sum = o_sum.transpose(3, 1, 0, 2, 4).reshape(nd * nz, members * ATTN_WIDTH, nb_cols)
+    cr_sum = sides[:, 1].reshape(nz, cr_cols, nd, nb_cols)
+    cr_sum = cr_sum.transpose(2, 0, 1, 3).reshape(nd * nz, cr_cols, nb_cols)
+    sides = jnp.concatenate([o_sum, cr_sum], 1)
+    sides = lax.psum_scatter(
+        sides, spread, scatter_dimension=0, tiled=False
+    ).reshape(2, cr_cols, nb_cols)
+    weight_o_grad = sides[0].astype(f32)
+    chan_recept_grad = sides[1].T.astype(f32)
+
+    weight_r_grad, weight_k_grad, weight_v_grad = (
+        w.T.astype(f32)
+        for w in join_rows(
+            scatter_weights(tie(main_part, ck_sum, gate_sum), spread), team
+        )
+    )
+    chan_value_grad = join_rows(cv_sum, team)[0].astype(f32)
+    chan_key_grad = join_rows(ck_sum, team)[0].T.astype(f32)
+    weight_g_grad = join_rows(gate_sum, team)[0].T.astype(f32)
+    mix_parts = jnp.concatenate([main_mix[:, 0], gate_mix[:, 0]], 0)
     ln1_gain_part = jnp.sum(grad_x1 * hat1, 0)
     ln1_bias_part = jnp.sum(grad_x1, 0)
     in_grad = grad_middle + norm_back(grad_x1, hat1, inv1, earlier_layernorm_scale)
@@ -686,38 +1212,30 @@
     placed = lax.dynamic_update_slice(
         jnp.zeros((4, nz, 2, members, ATTN_WIDTH), f32), by_head, (0, 0, ci, member, 0)
     ).reshape(4, width)
-    small = jnp.concatenate(
+    early = jnp.concatenate(
         [
-            mix_parts,
             placed,
-            jnp.stack(
-                [
-                    ln1_gain_part,
-                    ln1_bias_part,
-                    ln2_gain_part,
-                    ln2_bias_part,
-                    chan_mix_k_part,
-                    chan_mix_r_part,
-                ]
-            ),
+            jnp.stack([ln2_gain_part, ln2_bias_part, chan_mix_k_part, chan_mix_r_part]),
         ],
         0,
     )
-    small = lax.psum(small, every)
+    early = sum_everywhere(early, team)
+    late = jnp.concatenate([mix_parts, jnp.stack([ln1_gain_part, ln1_bias_part])], 0)
+    late = sum_everywhere(late, team)
     here = lax.dynamic_slice_in_dim(
-        small[4:8].reshape(4, nz * 2, members * ATTN_WIDTH), zi * 2 + ci, 1, 1
+        early[:4].reshape(4, nz * 2, members * ATTN_WIDTH), zi * 2 + ci, 1, 1
     )[:, 0]
     per_head = here.reshape(4, members, ATTN_WIDTH)
     return (
         block_out,
         in_grad,
         initial_state_gradient,
-        small[8],
-        small[9],
-        small[0],
-        small[1],
-        small[2],
-        small[3],
+        late[4],
+        late[5],
+        late[0],
+        late[1],
+        late[2],
+        late[3],
         weight_r_grad,
         weight_k_grad,
         weight_v_grad,
@@ -727,10 +1245,10 @@
         here[0],
         here[1],
         weight_o_grad,
-        small[10],
-        small[11],
-        small[12],
-        small[13],
+        early[4],
+        early[5],
+        early[6],
+        early[7],
         chan_key_grad,
         chan_value_grad,
         chan_recept_grad,

time: 1840 us -> 1390 us (0.76)
  Pallas kernels: 67.7 us -> 352 us
  waiting for transfers between devices: 680 us -> 440 us
  matrix products: 358 us -> 126 us
  local copies, waits for them, and re-layouts: 339 us -> 145 us
  other arithmetic: 248 us -> 169 us
  starting transfers between devices: 83.1 us -> 127 us
  blocking collectives: 34.7 us -> 0 us
    pallas_call x0 -> x23, Pallas kernels: none -> 281 us  [the longest x4 58.1 us: project_back(): pl.pallas_call(project_back_kernel, grid_spec=spec, out_shape=sds((2, tok...]
    reduce_scatter x5, waiting for transfers between devices: 204 us -> 0.03 us  [the longest x4 0.03 us: scatter_weights(): return lax.psum_scatter(blocks, spread, scatter_dimension=0, tiled=False)]
    dot_general x5 -> x0, matrix products: 144 us -> none  [tn(): lax.dot_general(left, right, (((0,), (0,)), ((), ())), preferred_element_...]
    dot_general x14 -> x10, matrix products: 108 us -> 52.3 us  [nn(): return jnp.dot(left, right, preferred_element_type=f32)]
    dot_general x2 -> x0, local copies, waits for them, and re-layouts: 53 us -> none  [tn(): lax.dot_general(left, right, (((0,), (0,)), ((), ())), preferred_element_...]
    ppermute x1 -> x18, waiting for transfers between devices: 0.01 us -> 50.9 us  [the longest x12 34.1 us: z_ring(): lax.ppermute(value, 'z', [((i + s) % nz, i) for i in range(nz)])]
    select_n x13 -> x0, other arithmetic: 47.4 us -> none  [the longest x12 44.7 us: core_pair(): jnp.where(first, jnp.concatenate([value, other], 0), jnp.concatenate([oth...]
    all_gather x6 -> x4, waiting for transfers between devices: 47.4 us -> 0.04 us  [the longest x3 0.02 us: along_z(): whole = lax.all_gather(mine, spread, axis=0, tiled=False)]
  transfers between devices with their start and end apart: 101 -> 132, of which waited for: 41 -> 51; matrix products, arithmetic and copies ran while one was open for 44% -> 26% of each run, Pallas kernels for 3% -> 26%
where the time goes in v2:
time: 1390 us; the launch traced here: 1380 us
  waiting for transfers between devices  440 us (32%)
  Pallas kernels  352 us (25%)
  other arithmetic  169 us (12%)
  local copies, waits for them, and re-layouts  145 us (10%)
  starting transfers between devices  127 us (9%)
  matrix products  126 us (9%)
  between operations  19.3 us (1%)
    ppermute x90, waiting for transfers between devices, swap(): return lax.ppermute(value, axis, [(0, 1), (1, 0)])  328 us
    dot_general x10, matrix products, nt(): lax.dot_general(left, right, (((1,), (1,)), ((), ())), preferred_element_...  73.3 us
    ppermute x90, starting transfers between devices, swap(): return lax.ppermute(value, axis, [(0, 1), (1, 0)])  70.9 us
    ppermute x11, waiting for transfers between devices, send_far(): return lax.ppermute(value, team, [(i, 3 - i) for i in range(4)])  59.6 us
    pallas_call x4, Pallas kernels, project_back(): pl.pallas_call(project_back_kernel, grid_spec=spec, out_shape=sds((2, tok...  58.1 us
    pallas_call x2, Pallas kernels, mix_weight_grads(): pl.pallas_call(functools.partial(mix_weight_kernel, count), grid_spec=spe...  56.1 us
    dot_general x10, matrix products, nn(): return jnp.dot(left, right, preferred_element_type=f32)  52.3 us
    pallas_call x2, Pallas kernels, outer_grads(): pl.pallas_call(functools.partial(outer_kernel, count), grid=(groups, tile...  51.4 us
  transfers between devices with their start and end apart: 132, of which 51 were waited for; matrix products, arithmetic and copies ran while one was open for 26% of the time, Pallas kernels for 26%

profile of v2, /device:TPU:0, one launch (start us, length us, event | category | flops | bytes accessed | tf_op | source)
XLA Modules:
  0.0 1378.9 jit_solution(17618580023251531192)
XLA Ops:
  23.6 7.1 collective-permute-done.11
  38.0 7.9 collective-permute-done.34
  73.2 43.0 %collective-permute-done.23 = bf16[1,2048]{1,0:T(2,128)(2,1)S(1)} collective-permute-done((bf16[1,2048]{1,0:T(2,128)(2,1)S(1)}, bf16[1,2048]{1,0:T(2,128)(2,1)S(1)}, u32[]{:S(2)}, u32[]{:S(2)}) %collective-permute-start.23) | collective-permute-done | bytes 4128 | tf_op jit(solution)/shard_map/ppermute | solution.py:756
  134.8 16.9 %collective-permute-done.7 = f32[4,64,64]{2,1,0:T(8,128)S(1)} collective-permute-done((f32[4,64,64]{2,1,0:T(8,128)S(1)}, f32[4,64,64]{2,1,0:T(8,128)S(1)}, u32[]{:S(2)}, u32[]{:S(2)}) %collective-permute-start.7) | collective-permute-done | bytes 65568 | tf_op jit(solution)/shard_map/ppermute | solution.py:909
  180.8 7.0 pad_maximum_fusion.x_ref.refs_4_.refs_2_
  187.8 11.1 place_mix.1.w_ref
  199.0 50.2 %project.1 = (bf16[3,4,1024,256]{3,2,1,0:T(8,128)(2,1)}, f32[4,1024,256]{2,1,0:T(8,128)}) custom-call(s32[1]{0:T(128)} %bitcast.28.core_ref, bf16[4,2,512,2048]{3,2,1,0:T(8,128)(2,1)} %pad_maximum_fusion.x_ref.refs_4_.refs_2_, bf16[4,8,2048]{2,1,0:T(8,128)(2,1)} %pad_maximum_fusion.22.halo_ref, bf16[2,4,256,2048]{3,2,1,0:T(8,128)(2,1)} %place_mix.1.w_ref), custom_call_target="tpu_custom_call" | custom-call | flops 149999992832 | tf_op jit(solution)/shard_map/project/pallas_call | solution.py:383
  268.9 14.0 %collective-permute-done.26 = bf16[4,64,256]{2,1,0:T(8,128)(2,1)S(1)} collective-permute-done((bf16[4,64,256]{2,1,0:T(8,128)(2,1)S(1)}, bf16[4,64,256]{2,1,0:T(8,128)(2,1)S(1)}, u32[]{:S(2)}, u32[]{:S(2)}) %collective-permute-start.26) | collective-permute-done | bytes 131104 | tf_op jit(solution)/shard_map/ppermute | solution.py:909
  283.9 19.7 %mix_forward.1 = (bf16[4,1024,256]{2,1,0:T(8,128)(2,1)}, f32[4,1024,256]{2,1,0:T(8,128)}, f32[4,4,64,256]{3,2,1,0:T(8,128)}) custom-call(f32[1,256]{1,0:T(1,128)} %exp.39.rate_ref, f32[1,256]{1,0:T(1,128)} %squeeze.196.boost_ref, f32[1,256]{1,0:T(1,128)} %squeeze.197.gain_ref, f32[1,256]{1,0:T(1,128)} %squeeze.198.bias_ref, ...), custom_call_target="tpu_custom_call" | custom-call | flops 60000002048 | tf_op jit(solution)/shard_map/mix_forward/pallas_call | solution.py:272
  309.5 20.0 %collective-permute-done.30 = bf16[1024,256]{1,0:T(8,128)(2,1)S(1)} collective-permute-done((bf16[1024,256]{1,0:T(8,128)(2,1)}, bf16[1024,256]{1,0:T(8,128)(2,1)S(1)}, u32[]{:S(2)}, u32[]{:S(2)}) %collective-permute-start.30) | collective-permute-done | bytes 524320 | tf_op jit(solution)/shard_map/ppermute | solution.py:756
  341.8 9.8 place_emission.1
  351.6 7.0 fusion.119
  379.0 53.4 %collective-permute-done.36 = bf16[512,2048]{1,0:T(8,128)(2,1)} collective-permute-done((bf16[512,2048]{1,0:T(8,128)(2,1)S(1)}, bf16[512,2048]{1,0:T(8,128)(2,1)}, u32[]{:S(2)}, u32[]{:S(2)}) %collective-permute-start.36) | collective-permute-done | bytes 2097184 | tf_op jit(solution)/shard_map/ppermute | solution.py:756
  443.6 8.4 multiply_convert_fusion.4
  506.1 20.3 %collective-permute-done.51 = bf16[256,2048]{1,0:T(8,128)(2,1)S(1)} collective-permute-done((bf16[256,2048]{1,0:T(8,128)(2,1)S(1)}, bf16[256,2048]{1,0:T(8,128)(2,1)S(1)}, u32[]{:S(2)}, u32[]{:S(2)}) %collective-permute-start.51) | collective-permute-done | bytes 1048608 | tf_op jit(solution)/shard_map/ppermute | solution.py:756
  541.8 7.6 place_accept.1
  549.4 7.0 fusion.120
  558.9 16.6 %collective-permute-done.54 = bf16[512,2048]{1,0:T(8,128)(2,1)S(1)} collective-permute-done((bf16[512,2048]{1,0:T(8,128)(2,1)}, bf16[512,2048]{1,0:T(8,128)(2,1)S(1)}, u32[]{:S(2)}, u32[]{:S(2)}) %collective-permute-start.54) | collective-permute-done | bytes 2097184 | tf_op jit(solution)/shard_map/ppermute | solution.py:756
  578.7 5.9 fusion.21
  586.8 10.1 place_rows.5.refs_1_
  596.9 33.8 %collective-permute-done.56 = bf16[512,2048]{1,0:T(8,128)(2,1)S(1)} collective-permute-done((bf16[512,2048]{1,0:T(8,128)(2,1)S(1)}, bf16[512,2048]{1,0:T(8,128)(2,1)S(1)}, u32[]{:S(2)}, u32[]{:S(2)}) %collective-permute-start.56) | collective-permute-done | bytes 2097184 | tf_op jit(solution)/shard_map/ppermute | solution.py:756
  634.7 8.5 multiply_convert_fusion.3.refs_0_
  643.2 11.3 collective-permute-done.59
  657.3 9.4 multiply_convert_fusion.1.refs_2_
  676.6 8.5 multiply_convert_fusion.refs_3_
  717.0 17.9 %collective-permute-done.67 = bf16[256,2048]{1,0:T(8,128)(2,1)S(1)} collective-permute-done((bf16[256,2048]{1,0:T(8,128)(2,1)S(1)}, bf16[256,2048]{1,0:T(8,128)(2,1)S(1)}, u32[]{:S(2)}, u32[]{:S(2)}) %collective-permute-start.67) | collective-permute-done | bytes 1048608 | tf_op jit(solution)/shard_map/ppermute | solution.py:756
  749.0 6.1 fusion.121
  761.8 25.5 %outer_grads.2 = bf16[1,4,4,1,224,512]{5,4,3,2,1,0:T(8,128)(2,1)} custom-call(bf16[1024,896]{1,0:T(8,128)(2,1)} %copy-done.120, bf16[1024,896]{1,0:T(8,128)(2,1)} %copy-done.122, bf16[1024,896]{1,0:T(8,128)(2,1)} %copy-done.121, bf16[1024,896]{1,0:T(8,128)(2,1)} %copy-done.123, bf16[1024,2048]{1,0:T(8,128)(2,1)} %pad_maximum_fusion.6.refs_4_, ...), custom_call_target="tpu_custom_call" | custom-call | flops 9374999552 | tf_op jit(solution)/shard_map/outer_grads/pallas_call | solution.py:584
  787.3 25.9 %outer_grads.3 = bf16[1,4,4,1,224,512]{5,4,3,2,1,0:T(8,128)(2,1)} custom-call(bf16[1024,896]{1,0:T(8,128)(2,1)} %multiply_convert_fusion.3.refs_0_, bf16[1024,896]{1,0:T(8,128)(2,1)} %multiply_convert_fusion.2.refs_1_, bf16[1024,896]{1,0:T(8,128)(2,1)} %multiply_convert_fusion.1.refs_2_, bf16[1024,896]{1,0:T(8,128)(2,1)} %copy-done.127, ...), custom_call_target="tpu_custom_call" | custom-call | flops 9374999552 | tf_op jit(solution)/shard_map/outer_grads/pallas_call | solution.py:584
  825.5 6.2 multiply_reduce_fusion.2
  836.3 9.4 convolution_convert_fusion.8
  875.8 10.6 collective-permute-done.74
  889.3 17.9 %gate_back.1 = (bf16[4,1024,256]{2,1,0:T(8,128)(2,1)}, bf16[4,1024,256]{2,1,0:T(8,128)(2,1)}, f32[4,64,256]{2,1,0:T(8,128)}, f32[4,1,2,256]{3,2,1,0:T(2,128)}) custom-call(f32[1,256]{1,0:T(1,128)} %exp.39.rate_ref, f32[1,256]{1,0:T(1,128)} %squeeze.197.gain_ref, f32[1,256]{1,0:T(1,128)} %squeeze.198.bias_ref, ...), custom_call_target="tpu_custom_call" | custom-call | flops 6750000128 | tf_op jit(solution)/shard_map/gate_back/pallas_call | solution.py:300
  910.9 17.2 %side_grads.1 = bf16[4,2,1024,1024]{3,2,1,0:T(8,128)(2,1)} custom-call(s32[2]{0:T(128)} %pad_add_fusion.where_ref, bf16[512,2048]{1,0:T(8,128)(2,1)} %tie.10.z_ref, bf16[512,2048]{1,0:T(8,128)(2,1)} %copy-done.23, bf16[512,2048]{1,0:T(8,128)(2,1)} %get-tuple-element.174.gr_ref, bf16[512,2048]{1,0:T(8,128)(2,1)} %get-tuple-element.66.cr_ref), custom_call_target="tpu_custom_call" | custom-call | flops 6375000064 | tf_op jit(solution)/shard_map/side_grads/pallas_call | solution.py:636
  928.1 6.1 fusion.90
  950.8 29.1 %mix_backward.1 = (bf16[4,1024,256]{2,1,0:T(8,128)(2,1)}, bf16[4,1024,256]{2,1,0:T(8,128)(2,1)}, bf16[4,1024,256]{2,1,0:T(8,128)(2,1)}, f32[4,1,2,256]{3,2,1,0:T(2,128)}) custom-call(f32[1,256]{1,0:T(1,128)} %exp.39.rate_ref, f32[1,256]{1,0:T(1,128)} %squeeze.196.boost_ref, f32[4,64,256]{2,1,0:T(8,128)} %get-tuple-element.154.end_ref, ...), custom_call_target="tpu_custom_call" | custom-call | flops 10874999808 | tf_op jit(solution)/shard_map/mix_backward/pallas_call | solution.py:328
  990.5 16.7 %mix_weight_grads.3 = (bf16[1,4,4,1,64,512]{5,4,3,2,1,0:T(8,128)(2,1)}, f32[1,1,2048]{2,1,0:T(1,128)}) custom-call(s32[1]{0:T(128)} %bitcast.28.core_ref, bf16[4,1024,256]{2,1,0:T(8,128)(2,1)} %get-tuple-element.82.g_ref.refs_0_, bf16[4,1,8,256]{3,2,1,0:T(8,128)(2,1)} %pad.26.refs_1_, bf16[4,2,512,2048]{3,2,1,0:T(8,128)(2,1)} %pad_maximum_fusion.x_ref.refs_4_.refs_2_, ...), custom_call_target="tpu_custom_call" | custom-call | flops 4874999808 | tf_op jit(solution)/shard_map/mix_weight_grads/pallas_call | solution.py:526
  1030.6 7.4 collective-permute-done.107
  1048.9 14.3 %collective-permute-done.112 = bf16[512,1024]{1,0:T(8,128)(2,1)S(1)} collective-permute-done((bf16[512,1024]{1,0:T(8,128)(2,1)S(1)}, bf16[512,1024]{1,0:T(8,128)(2,1)S(1)}, u32[]{:S(2)}, u32[]{:S(2)}) %collective-permute-start.112) | collective-permute-done | bytes 1048608 | tf_op jit(solution)/shard_map/ppermute | solution.py:756
  1070.0 14.5 %project_back.4 = bf16[2,512,2048]{2,1,0:T(8,128)(2,1)} custom-call(s32[1]{0:T(128)} %bitcast.28.core_ref, bf16[4,1024,256]{2,1,0:T(8,128)(2,1)} %get-tuple-element.87.r_ref.refs_0_.refs_1_, bf16[4,1024,256]{2,1,0:T(8,128)(2,1)} %get-tuple-element.80.k_ref.refs_1_, bf16[4,1024,256]{2,1,0:T(8,128)(2,1)} %get-tuple-element.81.v_ref.refs_2_, ...), custom_call_target="tpu_custom_call" | custom-call | flops 5249999872 | tf_op jit(solution)/shard_map/project_back/pallas_call | solution.py:429
  1108.4 39.4 %mix_weight_grads.2 = (bf16[1,4,4,3,64,512]{5,4,3,2,1,0:T(8,128)(2,1)}, f32[3,1,2048]{2,1,0:T(1,128)}) custom-call(s32[1]{0:T(128)} %bitcast.28.core_ref, bf16[4,1024,256]{2,1,0:T(8,128)(2,1)} %get-tuple-element.87.r_ref.refs_0_.refs_1_, bf16[4,1024,256]{2,1,0:T(8,128)(2,1)} %get-tuple-element.80.k_ref.refs_1_, ...), custom_call_target="tpu_custom_call" | custom-call | flops 14625000448 | tf_op jit(solution)/shard_map/mix_weight_grads/pallas_call | solution.py:526
  1147.7 5.9 add_convert_fusion
  1164.5 14.6 %project_back.6 = bf16[2,512,2048]{2,1,0:T(8,128)(2,1)} custom-call(s32[1]{0:T(128)} %bitcast.28.core_ref, bf16[4,1024,256]{2,1,0:T(8,128)(2,1)} %get-tuple-element.87.r_ref.refs_0_.refs_1_, bf16[4,1024,256]{2,1,0:T(8,128)(2,1)} %get-tuple-element.80.k_ref.refs_1_, bf16[4,1024,256]{2,1,0:T(8,128)(2,1)} %get-tuple-element.81.v_ref.refs_2_, ...), custom_call_target="tpu_custom_call" | custom-call | flops 5249999872 | tf_op jit(solution)/shard_map/project_back/pallas_call | solution.py:429
  1182.3 14.4 %project_back.5 = bf16[2,512,2048]{2,1,0:T(8,128)(2,1)} custom-call(s32[1]{0:T(128)} %bitcast.28.core_ref, bf16[4,1024,256]{2,1,0:T(8,128)(2,1)} %get-tuple-element.87.r_ref.refs_0_.refs_1_, bf16[4,1024,256]{2,1,0:T(8,128)(2,1)} %get-tuple-element.80.k_ref.refs_1_, bf16[4,1024,256]{2,1,0:T(8,128)(2,1)} %get-tuple-element.81.v_ref.refs_2_, ...), custom_call_target="tpu_custom_call" | custom-call | flops 5249999872 | tf_op jit(solution)/shard_map/project_back/pallas_call | solution.py:429
  1216.6 21.2 %collective-permute-done.85 = bf16[256,2048]{1,0:T(8,128)(2,1)S(1)} collective-permute-done((bf16[256,2048]{1,0:T(8,128)(2,1)S(1)}, bf16[256,2048]{1,0:T(8,128)(2,1)S(1)}, u32[]{:S(2)}, u32[]{:S(2)}) %collective-permute-start.85) | collective-permute-done | bytes 1048608 | tf_op jit(solution)/shard_map/ppermute | solution.py:756
  1243.5 14.6 %project_back.7 = bf16[2,512,2048]{2,1,0:T(8,128)(2,1)} custom-call(s32[1]{0:T(128)} %bitcast.28.core_ref, bf16[4,1024,256]{2,1,0:T(8,128)(2,1)} %get-tuple-element.87.r_ref.refs_0_.refs_1_, bf16[4,1024,256]{2,1,0:T(8,128)(2,1)} %get-tuple-element.80.k_ref.refs_1_, bf16[4,1024,256]{2,1,0:T(8,128)(2,1)} %get-tuple-element.81.v_ref.refs_2_, ...), custom_call_target="tpu_custom_call" | custom-call | flops 5249999872 | tf_op jit(solution)/shard_map/project_back/pallas_call | solution.py:429
  1266.8 49.0 %collective-permute-done.120 = bf16[1,224,512]{2,1,0:T(8,128)(2,1)S(1)} collective-permute-done((bf16[1,224,512]{2,1,0:T(8,128)(2,1)S(1)}, bf16[1,224,512]{2,1,0:T(8,128)(2,1)S(1)}, u32[]{:S(2)}, u32[]{:S(2)}) %collective-permute-start.120) | collective-permute-done | bytes 229408 | tf_op jit(solution)/shard_map/ppermute | solution.py:764
  1322.1 6.1 fusion.12
  (888 shorter events, 555.0 us)
Async XLA Ops:
  7.2 180.6 %all-gather.13.cloned.1.call-start = ((), (), s32[]{:S(2)}) async-start(), calls=%async_computation.12 | async-start | bytes 5242880 | tf_op jit(solution)/shard_map/all_gather | solution.py:890
  33.7 308.1 %all-gather.9.cloned.1.call-start = ((), (), s32[]{:S(2)}) async-start(), calls=%async_computation.5 | async-start | bytes 4587520 | tf_op jit(solution)/shard_map/all_gather | solution.py:890
  48.7 293.1 %all-gather.15.cloned.1.call-start = ((), (), s32[]{:S(2)}) async-start(), calls=%async_computation.13 | async-start | bytes 8650752 | tf_op jit(solution)/shard_map/all_gather | solution.py:1031
  58.0 62.4 %collective-permute-start.5 = (f32[64,64]{1,0:T(8,128)S(1)}, f32[64,64]{1,0:T(8,128)S(1)}, u32[]{:S(2)}, u32[]{:S(2)}) collective-permute-start(f32[64,64]{1,0:T(8,128)S(1)} %get-tuple-element.304), channel_id=1, source_target_pairs={{0,24},{8,16},{16,8},{24,0},{1,25},{9,17},{17,9},{25,1},{2,26},{10... | collective-permute-start | bytes 49160 | tf_op jit(solution)/shard_map/ppermute | solution.py:764
  60.5 314.0 %all-gather.11.cloned.1.call-start = ((), (), s32[]{:S(2)}) async-start(), calls=%async_computation.6 | async-start | bytes 4587520 | tf_op jit(solution)/shard_map/all_gather | solution.py:890
  63.4 58.5 %collective-permute-start.4 = (f32[64,64]{1,0:T(8,128)S(1)}, f32[64,64]{1,0:T(8,128)S(1)}, u32[]{:S(2)}, u32[]{:S(2)}) collective-permute-start(f32[64,64]{1,0:T(8,128)S(1)} %get-tuple-element.305), channel_id=1, source_target_pairs={{0,16},{16,0},{1,17},{17,1},{2,18},{18,2},{3,19},{19,3},{4,20},{20... | collective-permute-start | bytes 49160 | tf_op jit(solution)/shard_map/ppermute | solution.py:756
  67.9 60.2 %collective-permute-start.15 = (bf16[512,2048]{1,0:T(8,128)(2,1)S(1)}, bf16[512,2048]{1,0:T(8,128)(2,1)}, u32[]{:S(2)}, u32[]{:S(2)}) collective-permute-start(bf16[512,2048]{1,0:T(8,128)(2,1)S(1)} %copy-done.19), channel_id=1, source_target_pairs={{0,16},{16,0},{1,17},{17,1},{2,18},{18,2},{3,19},{19,3},{4,20},{20... | collective-permute-start | bytes 6291464 | tf_op jit(solution)/shard_map/ppermute | solution.py:756
  69.5 60.3 %collective-permute-start.13 = (bf16[512,2048]{1,0:T(8,128)(2,1)S(1)}, bf16[512,2048]{1,0:T(8,128)(2,1)}, u32[]{:S(2)}, u32[]{:S(2)}) collective-permute-start(bf16[512,2048]{1,0:T(8,128)(2,1)S(1)} %copy-done.19), channel_id=1, source_target_pairs={{0,8},{8,0},{1,9},{9,1},{2,10},{10,2},{3,11},{11,3},{4,12},{12,4},... | collective-permute-start | bytes 6291464 | tf_op jit(solution)/shard_map/ppermute | solution.py:756
  72.6 43.6 %collective-permute-start.23 = (bf16[1,2048]{1,0:T(2,128)(2,1)S(1)}, bf16[1,2048]{1,0:T(2,128)(2,1)S(1)}, u32[]{:S(2)}, u32[]{:S(2)}) collective-permute-start(bf16[1,2048]{1,0:T(2,128)(2,1)S(1)} %fusion.75), channel_id=1, source_target_pairs={{0,16},{16,0},{1,17},{17,1},{2,18},{18,2},{3,19},{19,3},{4,20},{20... | collective-permute-start | bytes 12296 | tf_op jit(solution)/shard_map/ppermute | solution.py:756
  120.4 35.8 %collective-permute-start.40 = (bf16[1,224,512]{2,1,0:T(8,128)(2,1)S(1)}, bf16[1,224,512]{2,1,0:T(8,128)(2,1)S(1)}, u32[]{:S(2)}, u32[]{:S(2)}) collective-permute-start(bf16[1,224,512]{2,1,0:T(8,128)(2,1)S(1)} %get-tuple-element.245), channel_id=1, source_target_pairs={{0,16},{16,0},{1,17},{17,1},{2,18},{18,2},{3,19},{19,3},{4,20},{20... | collective-permute-start | bytes 688136 | tf_op jit(solution)/shard_map/ppermute | solution.py:756
  262.0 279.8 %all-gather.17.cloned.1.call-start = ((), (), s32[]{:S(2)}) async-start(), calls=%async_computation.14 | async-start | bytes 8650752 | tf_op jit(solution)/shard_map/all_gather | solution.py:1032
  333.4 524.3 %reduce-scatter.6.cloned.1.call-start = ((), (), s32[]{:S(2)}) async-start(), calls=%async_computation.7 | async-start | bytes 4587520 | tf_op jit(solution)/shard_map/reduce_scatter | solution.py:897
  367.1 68.2 %collective-permute-start.43 = (bf16[512,2048]{1,0:T(8,128)(2,1)S(1)}, bf16[512,2048]{1,0:T(8,128)(2,1)}, u32[]{:S(2)}, u32[]{:S(2)}) collective-permute-start(bf16[512,2048]{1,0:T(8,128)(2,1)S(1)} %get-tuple-element.178), channel_id=1, source_target_pairs={{0,16},{16,0},{1,17},{17,1},{2,18},{18,2},{3,19},{19,3},{4,20},{20... | collective-permute-start | bytes 6291464 | tf_op jit(solution)/shard_map/ppermute | solution.py:756
  368.5 63.9 %collective-permute-start.36 = (bf16[512,2048]{1,0:T(8,128)(2,1)S(1)}, bf16[512,2048]{1,0:T(8,128)(2,1)}, u32[]{:S(2)}, u32[]{:S(2)}) collective-permute-start(bf16[512,2048]{1,0:T(8,128)(2,1)S(1)} %get-tuple-element.178), channel_id=1, source_target_pairs={{0,8},{8,0},{1,9},{9,1},{2,10},{10,2},{3,11},{11,3},{4,12},{12,4},... | collective-permute-start | bytes 6291464 | tf_op jit(solution)/shard_map/ppermute | solution.py:756
  370.1 73.5 %collective-permute-start.46 = (bf16[512,2048]{1,0:T(8,128)(2,1)S(1)}, bf16[512,2048]{1,0:T(8,128)(2,1)}, u32[]{:S(2)}, u32[]{:S(2)}) collective-permute-start(bf16[512,2048]{1,0:T(8,128)(2,1)S(1)} %get-tuple-element.178), channel_id=1, source_target_pairs={{0,1},{1,0},{2,3},{3,2},{4,5},{5,4},{6,7},{7,6},{8,9},{9,8},{10,11... | collective-permute-start | bytes 6291464 | tf_op jit(solution)/shard_map/ppermute | solution.py:756
  528.1 47.4 %collective-permute-start.54 = (bf16[512,2048]{1,0:T(8,128)(2,1)}, bf16[512,2048]{1,0:T(8,128)(2,1)S(1)}, u32[]{:S(2)}, u32[]{:S(2)}) collective-permute-start(bf16[512,2048]{1,0:T(8,128)(2,1)} %pad_maximum_fusion.11), channel_id=1, source_target_pairs={{0,16},{16,0},{1,17},{17,1},{2,18},{18,2},{3,19},{19,3},{4,20},{20... | collective-permute-start | bytes 6291464 | tf_op jit(solution)/shard_map/ppermute | solution.py:756
  531.4 47.3 %collective-permute-start.53 = (bf16[512,2048]{1,0:T(8,128)(2,1)}, bf16[512,2048]{1,0:T(8,128)(2,1)}, u32[]{:S(2)}, u32[]{:S(2)}) collective-permute-start(bf16[512,2048]{1,0:T(8,128)(2,1)} %pad_maximum_fusion.10), channel_id=1, source_target_pairs={{0,8},{8,0},{1,9},{9,1},{2,10},{10,2},{3,11},{11,3},{4,12},{12,4},... | collective-permute-start | bytes 6291464 | tf_op jit(solution)/shard_map/ppermute | solution.py:756
  584.6 46.0 %collective-permute-start.56 = (bf16[512,2048]{1,0:T(8,128)(2,1)S(1)}, bf16[512,2048]{1,0:T(8,128)(2,1)S(1)}, u32[]{:S(2)}, u32[]{:S(2)}) collective-permute-start(bf16[512,2048]{1,0:T(8,128)(2,1)S(1)} %get-tuple-element.176), channel_id=1, source_target_pairs={{0,8},{8,0},{1,9},{9,1},{2,10},{10,2},{3,11},{11,3},{4,12},{12,4},... | collective-permute-start | bytes 6291464 | tf_op jit(solution)/shard_map/ppermute | solution.py:756
  586.3 46.8 %collective-permute-start.60 = (bf16[512,2048]{1,0:T(8,128)(2,1)S(1)}, bf16[512,2048]{1,0:T(8,128)(2,1)S(1)}, u32[]{:S(2)}, u32[]{:S(2)}) collective-permute-start(bf16[512,2048]{1,0:T(8,128)(2,1)S(1)} %get-tuple-element.176), channel_id=1, source_target_pairs={{0,16},{16,0},{1,17},{17,1},{2,18},{18,2},{3,19},{19,3},{4,20},{20... | collective-permute-start | bytes 6291464 | tf_op jit(solution)/shard_map/ppermute | solution.py:756
  586.8 47.7 %collective-permute-start.55 = (bf16[512,2048]{1,0:T(8,128)(2,1)S(1)}, bf16[512,2048]{1,0:T(8,128)(2,1)}, u32[]{:S(2)}, u32[]{:S(2)}) collective-permute-start(bf16[512,2048]{1,0:T(8,128)(2,1)S(1)} %get-tuple-element.176), channel_id=1, source_target_pairs={{0,1},{1,0},{2,3},{3,2},{4,5},{5,4},{6,7},{7,6},{8,9},{9,8},{10,11... | collective-permute-start | bytes 6291464 | tf_op jit(solution)/shard_map/ppermute | solution.py:756
  748.1 65.2 %collective-permute-start.68 = (bf16[512,2048]{1,0:T(8,128)(2,1)}, bf16[512,2048]{1,0:T(8,128)(2,1)}, u32[]{:S(2)}, u32[]{:S(2)}) collective-permute-start(bf16[512,2048]{1,0:T(8,128)(2,1)} %slice.1153), channel_id=1, source_target_pairs={{0,1},{1,0},{2,3},{3,2},{4,5},{5,4},{6,7},{7,6},{8,9},{9,8},{10,11... | collective-permute-start | bytes 6291464 | tf_op jit(solution)/shard_map/ppermute | solution.py:756
  759.3 57.2 %collective-permute-start.70 = (bf16[512,2048]{1,0:T(8,128)(2,1)}, bf16[512,2048]{1,0:T(8,128)(2,1)S(1)}, u32[]{:S(2)}, u32[]{:S(2)}) collective-permute-start(bf16[512,2048]{1,0:T(8,128)(2,1)} %pad_maximum_fusion.14), channel_id=1, source_target_pairs={{0,16},{16,0},{1,17},{17,1},{2,18},{18,2},{3,19},{19,3},{4,20},{20... | collective-permute-start | bytes 6291464 | tf_op jit(solution)/shard_map/ppermute | solution.py:756
  761.0 55.5 %collective-permute-start.69 = (bf16[512,2048]{1,0:T(8,128)(2,1)}, bf16[512,2048]{1,0:T(8,128)(2,1)}, u32[]{:S(2)}, u32[]{:S(2)}) collective-permute-start(bf16[512,2048]{1,0:T(8,128)(2,1)} %pad_maximum_fusion.13), channel_id=1, source_target_pairs={{0,8},{8,0},{1,9},{9,1},{2,10},{10,2},{3,11},{11,3},{4,12},{12,4},... | collective-permute-start | bytes 6291464 | tf_op jit(solution)/shard_map/ppermute | solution.py:756
  787.3 282.8 %reduce-scatter.8.cloned.1.call-start = ((), (), s32[]{:S(2)}) async-start(), calls=%async_computation.8 | async-start | bytes 4587520 | tf_op jit(solution)/shard_map/reduce_scatter | solution.py:897
  857.7 230.6 %reduce-scatter.10.cloned.1.call-start = ((), (), s32[]{:S(2)}) async-start(), calls=%async_computation.9 | async-start | bytes 1310720 | tf_op jit(solution)/shard_map/reduce_scatter | solution.py:897
  908.8 35.4 %collective-permute-start.76 = (bf16[4,64,256]{2,1,0:T(8,128)(2,1)S(1)}, bf16[4,64,256]{2,1,0:T(8,128)(2,1)S(1)}, u32[]{:S(2)}, u32[]{:S(2)}) collective-permute-start(bf16[4,64,256]{2,1,0:T(8,128)(2,1)S(1)} %get-tuple-element.163), channel_id=1, source_target_pairs={{2,0},{4,2},{6,4},{0,6},{3,1},{5,3},{7,5},{1,7},{10,8},{12,10},{14... | collective-permute-start | bytes 393224 | tf_op jit(solution)/shard_map/ppermute | solution.py:909
  908.8 36.1 %collective-permute-start.77 = (bf16[4,64,256]{2,1,0:T(8,128)(2,1)S(1)}, bf16[4,64,256]{2,1,0:T(8,128)(2,1)S(1)}, u32[]{:S(2)}, u32[]{:S(2)}) collective-permute-start(bf16[4,64,256]{2,1,0:T(8,128)(2,1)S(1)} %get-tuple-element.163), channel_id=1, source_target_pairs={{4,0},{6,2},{0,4},{2,6},{5,1},{7,3},{1,5},{3,7},{12,8},{14,10},{8,... | collective-permute-start | bytes 393224 | tf_op jit(solution)/shard_map/ppermute | solution.py:909
  910.9 34.7 %collective-permute-start.78 = (bf16[4,64,256]{2,1,0:T(8,128)(2,1)S(1)}, bf16[4,64,256]{2,1,0:T(8,128)(2,1)S(1)}, u32[]{:S(2)}, u32[]{:S(2)}) collective-permute-start(bf16[4,64,256]{2,1,0:T(8,128)(2,1)S(1)} %get-tuple-element.163), channel_id=1, source_target_pairs={{6,0},{0,2},{2,4},{4,6},{7,1},{1,3},{3,5},{5,7},{14,8},{8,10},{10,... | collective-permute-start | bytes 393224 | tf_op jit(solution)/shard_map/ppermute | solution.py:909
  939.6 98.4 %collective-permute-start.109 = (bf16[1024,1024]{1,0:T(8,128)(2,1)}, bf16[1024,1024]{1,0:T(8,128)(2,1)S(1)}, u32[]{:S(2)}, u32[]{:S(2)}) collective-permute-start(bf16[1024,1024]{1,0:T(8,128)(2,1)} %slice_bitcast_fusion), channel_id=1, source_target_pairs={{0,1},{1,0},{2,3},{3,2},{4,5},{5,4},{6,7},{7,6},{8,9},{9,8},{10,11... | collective-permute-start | bytes 6291464 | tf_op jit(solution)/shard_map/ppermute | solution.py:756
  982.1 28.3 %collective-permute-start.79 = (bf16[4,3,256]{2,1,0:T(4,128)(2,1)S(1)}, bf16[4,3,256]{2,1,0:T(4,128)(2,1)S(1)}, u32[]{:S(2)}, u32[]{:S(2)}) collective-permute-start(bf16[4,3,256]{2,1,0:T(4,128)(2,1)S(1)} %pad_maximum_fusion.26), channel_id=1, source_target_pairs={{2,0},{4,2},{6,4},{3,1},{5,3},{7,5},{10,8},{12,10},{14,12},{11,9},... | collective-permute-start | bytes 18440 | tf_op jit(solution)/shard_map/ppermute | solution.py:1148
  984.9 26.9 %collective-permute-start.91 = (f32[64,64]{1,0:T(8,128)S(1)}, f32[64,64]{1,0:T(8,128)S(1)}, u32[]{:S(2)}, u32[]{:S(2)}) collective-permute-start(f32[64,64]{1,0:T(8,128)S(1)} %get-tuple-element.300), channel_id=1, source_target_pairs={{0,16},{16,0},{1,17},{17,1},{2,18},{18,2},{3,19},{19,3},{4,20},{20... | collective-permute-start | bytes 49160 | tf_op jit(solution)/shard_map/ppermute | solution.py:756
  989.3 53.9 %collective-permute-start.111 = (bf16[1024,1024]{1,0:T(8,128)(2,1)}, bf16[1024,1024]{1,0:T(8,128)(2,1)}, u32[]{:S(2)}, u32[]{:S(2)}) collective-permute-start(bf16[1024,1024]{1,0:T(8,128)(2,1)} %slice.1225), channel_id=1, source_target_pairs={{0,1},{1,0},{2,3},{3,2},{4,5},{5,4},{6,7},{7,6},{8,9},{9,8},{10,11... | collective-permute-start | bytes 6291464 | tf_op jit(solution)/shard_map/ppermute | solution.py:756
  1007.2 344.3 %reduce-scatter.14.cloned.1.call-start = ((), (), s32[]{:S(2)}) async-start(), calls=%async_computation.11 | async-start | bytes 2621440 | tf_op jit(solution)/shard_map/reduce_scatter | solution.py:1184
  1013.3 32.9 %collective-permute-start.108 = (bf16[1024,1024]{1,0:T(8,128)(2,1)}, bf16[1024,1024]{1,0:T(8,128)(2,1)}, u32[]{:S(2)}, u32[]{:S(2)}) collective-permute-start(bf16[1024,1024]{1,0:T(8,128)(2,1)} %slice.1217), channel_id=1, source_target_pairs={{0,1},{1,0},{2,3},{3,2},{4,5},{5,4},{6,7},{7,6},{8,9},{9,8},{10,11... | collective-permute-start | bytes 6291464 | tf_op jit(solution)/shard_map/ppermute | solution.py:756
  1070.0 30.9 %collective-permute-start.113 = (bf16[1024,1024]{1,0:T(8,128)(2,1)}, bf16[1024,1024]{1,0:T(8,128)(2,1)}, u32[]{:S(2)}, u32[]{:S(2)}) collective-permute-start(bf16[1024,1024]{1,0:T(8,128)(2,1)} %slice_bitcast_fusion.10), channel_id=1, source_target_pairs={{0,1},{1,0},{2,3},{3,2},{4,5},{5,4},{6,7},{7,6},{8,9},{9,8},{10,11... | collective-permute-start | bytes 6291464 | tf_op jit(solution)/shard_map/ppermute | solution.py:756
  1098.0 49.7 %collective-permute-start.115 = (bf16[1024,1024]{1,0:T(8,128)(2,1)}, bf16[1024,1024]{1,0:T(8,128)(2,1)}, u32[]{:S(2)}, u32[]{:S(2)}) collective-permute-start(bf16[1024,1024]{1,0:T(8,128)(2,1)} %pad_maximum_fusion.19), channel_id=1, source_target_pairs={{0,16},{16,0},{1,17},{17,1},{2,18},{18,2},{3,19},{19,3},{4,20},{20... | collective-permute-start | bytes 6291464 | tf_op jit(solution)/shard_map/ppermute | solution.py:756
  1098.9 48.9 %collective-permute-start.114 = (bf16[1024,1024]{1,0:T(8,128)(2,1)}, bf16[1024,1024]{1,0:T(8,128)(2,1)}, u32[]{:S(2)}, u32[]{:S(2)}) collective-permute-start(bf16[1024,1024]{1,0:T(8,128)(2,1)} %pad_maximum_fusion.18), channel_id=1, source_target_pairs={{0,8},{8,0},{1,9},{9,1},{2,10},{10,2},{3,11},{11,3},{4,12},{12,4},... | collective-permute-start | bytes 6291464 | tf_op jit(solution)/shard_map/ppermute | solution.py:756
  1162.2 192.3 %reduce-scatter.12.cloned.1.call-start = ((), (), s32[]{:S(2)}) async-start(), calls=%async_computation.10 | async-start | bytes 3932160 | tf_op jit(solution)/shard_map/reduce_scatter | solution.py:897
  1201.4 60.2 %collective-permute-start.118 = (bf16[1,224,512]{2,1,0:T(8,128)(2,1)}, bf16[1,224,512]{2,1,0:T(8,128)(2,1)S(1)}, u32[]{:S(2)}, u32[]{:S(2)}) collective-permute-start(bf16[1,224,512]{2,1,0:T(8,128)(2,1)} %get-tuple-element.235), channel_id=1, source_target_pairs={{0,16},{16,0},{1,17},{17,1},{2,18},{18,2},{3,19},{19,3},{4,20},{20... | collective-permute-start | bytes 688136 | tf_op jit(solution)/shard_map/ppermute | solution.py:756
  1202.7 59.7 %collective-permute-start.117 = (bf16[1,224,512]{2,1,0:T(8,128)(2,1)}, bf16[1,224,512]{2,1,0:T(8,128)(2,1)S(1)}, u32[]{:S(2)}, u32[]{:S(2)}) collective-permute-start(bf16[1,224,512]{2,1,0:T(8,128)(2,1)} %get-tuple-element.236), channel_id=1, source_target_pairs={{0,24},{8,16},{16,8},{24,0},{1,25},{9,17},{17,9},{25,1},{2,26},{10... | collective-permute-start | bytes 688136 | tf_op jit(solution)/shard_map/ppermute | solution.py:764
  1203.8 58.8 %collective-permute-start.116 = (bf16[1,224,512]{2,1,0:T(8,128)(2,1)}, bf16[1,224,512]{2,1,0:T(8,128)(2,1)S(1)}, u32[]{:S(2)}, u32[]{:S(2)}) collective-permute-start(bf16[1,224,512]{2,1,0:T(8,128)(2,1)} %get-tuple-element.234), channel_id=1, source_target_pairs={{0,8},{8,0},{1,9},{9,1},{2,10},{10,2},{3,11},{11,3},{4,12},{12,4},... | collective-permute-start | bytes 688136 | tf_op jit(solution)/shard_map/ppermute | solution.py:756
  1207.8 29.9 %collective-permute-start.85 = (bf16[256,2048]{1,0:T(8,128)(2,1)S(1)}, bf16[256,2048]{1,0:T(8,128)(2,1)S(1)}, u32[]{:S(2)}, u32[]{:S(2)}) collective-permute-start(bf16[256,2048]{1,0:T(8,128)(2,1)S(1)} %get-tuple-element.184), channel_id=1, source_target_pairs={{0,8},{8,0},{1,9},{9,1},{2,10},{10,2},{3,11},{11,3},{4,12},{12,4},... | collective-permute-start | bytes 3145736 | tf_op jit(solution)/shard_map/ppermute | solution.py:756
  1212.3 28.6 %collective-permute-start.83 = (bf16[256,2048]{1,0:T(8,128)(2,1)S(1)}, bf16[256,2048]{1,0:T(8,128)(2,1)S(1)}, u32[]{:S(2)}, u32[]{:S(2)}) collective-permute-start(bf16[256,2048]{1,0:T(8,128)(2,1)S(1)} %get-tuple-element.183), channel_id=1, source_target_pairs={{0,16},{16,0},{1,17},{17,1},{2,18},{18,2},{3,19},{19,3},{4,20},{20... | collective-permute-start | bytes 3145736 | tf_op jit(solution)/shard_map/ppermute | solution.py:756
  1241.0 81.0 %collective-permute-start.88 = (bf16[512,2048]{1,0:T(8,128)(2,1)}, bf16[512,2048]{1,0:T(8,128)(2,1)}, u32[]{:S(2)}, u32[]{:S(2)}) collective-permute-start(bf16[512,2048]{1,0:T(8,128)(2,1)} %pad_maximum_fusion.17), channel_id=1, source_target_pairs={{0,16},{16,0},{1,17},{17,1},{2,18},{18,2},{3,19},{19,3},{4,20},{20... | collective-permute-start | bytes 6291464 | tf_op jit(solution)/shard_map/ppermute | solution.py:756
  1261.5 60.5 %collective-permute-start.87 = (bf16[512,2048]{1,0:T(8,128)(2,1)}, bf16[512,2048]{1,0:T(8,128)(2,1)}, u32[]{:S(2)}, u32[]{:S(2)}) collective-permute-start(bf16[512,2048]{1,0:T(8,128)(2,1)} %pad_maximum_fusion.16), channel_id=1, source_target_pairs={{0,8},{8,0},{1,9},{9,1},{2,10},{10,2},{3,11},{11,3},{4,12},{12,4},... | collective-permute-start | bytes 6291464 | tf_op jit(solution)/shard_map/ppermute | solution.py:756
  1262.5 59.6 %collective-permute-start.86 = (bf16[512,2048]{1,0:T(8,128)(2,1)}, bf16[512,2048]{1,0:T(8,128)(2,1)}, u32[]{:S(2)}, u32[]{:S(2)}) collective-permute-start(bf16[512,2048]{1,0:T(8,128)(2,1)} %slice_bitcast_fusion.2), channel_id=1, source_target_pairs={{0,1},{1,0},{2,3},{3,2},{4,5},{5,4},{6,7},{7,6},{8,9},{9,8},{10,11... | collective-permute-start | bytes 6291464 | tf_op jit(solution)/shard_map/ppermute | solution.py:756
  1262.6 53.2 %collective-permute-start.120 = (bf16[1,224,512]{2,1,0:T(8,128)(2,1)S(1)}, bf16[1,224,512]{2,1,0:T(8,128)(2,1)S(1)}, u32[]{:S(2)}, u32[]{:S(2)}) collective-permute-start(bf16[1,224,512]{2,1,0:T(8,128)(2,1)S(1)} %copy-done.73), channel_id=1, source_target_pairs={{0,24},{8,16},{16,8},{24,0},{1,25},{9,17},{17,9},{25,1},{2,26},{10... | collective-permute-start | bytes 688136 | tf_op jit(solution)/shard_map/ppermute | solution.py:764
  1264.5 53.0 %collective-permute-start.119 = (bf16[1,224,512]{2,1,0:T(8,128)(2,1)S(1)}, bf16[1,224,512]{2,1,0:T(8,128)(2,1)S(1)}, u32[]{:S(2)}, u32[]{:S(2)}) collective-permute-start(bf16[1,224,512]{2,1,0:T(8,128)(2,1)S(1)} %copy-done.72), channel_id=1, source_target_pairs={{0,8},{8,0},{1,9},{9,1},{2,10},{10,2},{3,11},{11,3},{4,12},{12,4},... | collective-permute-start | bytes 688136 | tf_op jit(solution)/shard_map/ppermute | solution.py:756
  (224 other events, 2247.9 us)
Sparse Core Ops, SparseCore 0:
  33.8 82.3 all-gather.12
  117.8 78.5 all-gather.8
  199.3 84.8 all-gather.14
  286.3 69.6 all-gather.10
  358.8 94.8 all-gather.16
  787.4 66.0 reduce-scatter.5
  857.9 75.0 reduce-scatter.7
  1007.3 31.4 reduce-scatter.9
  1162.3 44.0 reduce-scatter.13
  1208.5 59.5 reduce-scatter.11

commit v3 on v2

--- a/solution.py
+++ b/solution.py
@@ -832,7 +832,7 @@
     return part[:tokens].astype(f32) + swap(part[tokens:], "c").astype(f32)
 
 
-def reduce_tokens(make_part, team, early=None, late=None, hold=None, finish=None):
+def reduce_tokens(make_part, team, late=None):
     def free(value):
         return value
 
@@ -844,7 +844,7 @@
             return after(value, away)
 
         got = swap(away, team[0])
-        work = early or late
+        work = late
         own = core_reduce(make_part(0, pin))
         if work:
             extra = work(pin)
@@ -854,14 +854,7 @@
     half = corner.shape[0] // 2
     to_near = swap(corner[:half], team[0])
     to_side = swap(corner[half:], team[1])
-    if early:
-        extra = early(lambda v: after(v, corner))
-        near, side = make_part(1, lambda v: after(v, extra)), make_part(2, lambda v: after(v, extra))
-    else:
-        near, side = make_part(1, free), make_part(2, free)
-    if hold is not None:
-        near, side = tie(near, hold), tie(side, hold)
-    near, side = core_reduce(near), core_reduce(side)
+    near, side = core_reduce(make_part(1, free)), core_reduce(make_part(2, free))
     near = jnp.concatenate([near[:half] + to_near.astype(f32), near[half:]], 0).astype(bf16)
     side = jnp.concatenate([side[:half], side[half:] + to_side.astype(f32)], 0).astype(bf16)
 
@@ -874,9 +867,30 @@
     if late:
         extra = late(pin)
         own = after(own, extra)
-    if finish is not None:
-        own = tie(own, finish)
     return own + from_near.astype(f32) + from_side.astype(f32), extra
+
+
+def reduce_first(part, team):
+    sent = core_reduce(part).astype(bf16)
+    if len(team) == 1:
+        return sent, (swap(sent, team[0]),)
+    half = sent.shape[0] // 2
+    return sent, (swap(sent[:half], team[0]), swap(sent[half:], team[1]))
+
+
+def reduce_second(got, near, side, team):
+    half = near.shape[0] // 4
+    near, side = core_reduce(near), core_reduce(side)
+    near = jnp.concatenate([near[:half] + got[0].astype(f32), near[half:]], 0).astype(bf16)
+    side = jnp.concatenate([side[:half], side[half:] + got[1].astype(f32)], 0).astype(bf16)
+    return (near, side), (swap(near, team[1]), swap(side, team[0]))
+
+
+def reduce_last(own, got):
+    own = core_reduce(own)
+    for piece in got:
+        own = own + piece.astype(f32)
+    return own
 
 
 def split_rows(shards, team):
@@ -1135,14 +1149,17 @@
     added = z_ring(added.astype(bf16)).astype(f32)
     weight = fade((run_ids - zi - 1)[:, None])[:, None, None, :]
     end = jnp.sum(weight * added, 0)
-    dr, dk, dv, mix_sums = mix_backward(
-        rate, boost, end, begin, rkv, grad_y
-    )
     first = jnp.sum(fade(run_ids[:, None])[:, None, None, :] * added, 0)
     first = lax.dynamic_slice_in_dim(first, zi * ATTN_WIDTH, ATTN_WIDTH, 2)
     first = reorder(jnp.stack(team_exchange(first, team)), team)
     initial_state_gradient = first.transpose(0, 2, 1)[None]
 
+    where = jnp.stack([ci, member]).astype(jnp.int32)
+    side_parts = side_grads(
+        where, tie(z_rows, grad_y), grad_mix, grad_r2, mixed_cr, nd, members, nz
+    )
+    side_sent, side_got = reduce_first(side_parts[members - 1], team)
+
     def edges_of(parts):
         edges = jnp.stack([g[:, 0] for g in parts], 1)
         edges = lax.ppermute(edges, "z", [(i + 1, i) for i in range(nz - 1)])
@@ -1153,50 +1170,50 @@
         core, (grad_gate,), gate_edges, whole_x1, plain_w[3:], blends[3:], nd, members, nz
     )
     gate_sum = scatter_weights(gate_part, spread)
+    end = tie(end, gate_part)
+    dr, dk, dv, mix_sums = mix_backward(
+        rate, boost, end, begin, rkv, grad_y
+    )
     main_edges = edges_of((dr, dk, dv))
     edges = tie(jnp.concatenate([main_edges, gate_edges], 1), cv_sum)
 
-    def main_weights(pin):
-        return mix_weight_grads(
-            core, (pin(dr), dk, dv), main_edges, whole_x1, plain_w[:3], blends[:3], nd, members, nz
-        )
-
-    grad_x1, (main_part, main_mix) = reduce_tokens(
-        lambda i, pin: project_back(
-            core, i, (pin(after(dr, ck_sum)), dk, dv, grad_gate), edges, both_w
-        ).reshape(length, width),
-        team,
-        early=main_weights,
-    )
-    where = jnp.stack([ci, member]).astype(jnp.int32)
-    side_parts = side_grads(
-        where, tie(z_rows, grad_y), grad_mix, grad_r2, mixed_cr, nd, members, nz
-    )
-    sides = reduce_tokens(
-        lambda i, pin: pin(side_parts)[i], team, hold=dr, finish=main_part
-    )[0].astype(bf16)
+    def back(i, held):
+        grads = (held, dk, dv, grad_gate)
+        return project_back(core, i, grads, edges, both_w).reshape(length, width)
+
+    x1_sent, x1_got = reduce_first(back(members - 1, dr), team)
+    held = tie(dr, x1_sent)
+    main_part, main_mix = mix_weight_grads(
+        core, (held, dk, dv), main_edges, whole_x1, plain_w[:3], blends[:3], nd, members, nz
+    )
+    held = tie(held, main_part)
+    if members > 2:
+        x1_sent, x1_got = reduce_second(x1_got, back(1, held), back(2, held), team)
+        side_near, side_side = tie(side_parts[1], *x1_sent), tie(side_parts[2], *x1_sent)
+        side_sent, side_got = reduce_second(side_got, side_near, side_side, team)
+    held = tie(held, *jax.tree.leaves(x1_sent), *jax.tree.leaves(side_sent))
+    grad_x1 = reduce_last(back(0, held), x1_got)
+    main_sum = scatter_weights(tie(main_part, ck_sum, gate_sum), spread)
+    mix_parts = jnp.concatenate([main_mix[:, 0], gate_mix[:, 0]], 0)
+
+    side_own = tie(side_parts[0], grad_x1)
+    sides = reduce_last(side_own, side_got).astype(bf16)
     sides = sides.reshape(width // 2, 2, nd, nb_cols)
     o_sum = sides[:, 0].reshape(members, nz, ATTN_WIDTH, nd, nb_cols)
     o_sum = o_sum.transpose(3, 1, 0, 2, 4).reshape(nd * nz, members * ATTN_WIDTH, nb_cols)
     cr_sum = sides[:, 1].reshape(nz, cr_cols, nd, nb_cols)
     cr_sum = cr_sum.transpose(2, 0, 1, 3).reshape(nd * nz, cr_cols, nb_cols)
     sides = jnp.concatenate([o_sum, cr_sum], 1)
-    sides = lax.psum_scatter(
-        sides, spread, scatter_dimension=0, tiled=False
-    ).reshape(2, cr_cols, nb_cols)
+    sides = lax.psum_scatter(sides, spread, scatter_dimension=0, tiled=False)
+    sides = sides.reshape(2, cr_cols, nb_cols)
     weight_o_grad = sides[0].astype(f32)
     chan_recept_grad = sides[1].T.astype(f32)
-
     weight_r_grad, weight_k_grad, weight_v_grad = (
-        w.T.astype(f32)
-        for w in join_rows(
-            scatter_weights(tie(main_part, ck_sum, gate_sum), spread), team
-        )
+        w.T.astype(f32) for w in join_rows(main_sum, team)
     )
     chan_value_grad = join_rows(cv_sum, team)[0].astype(f32)
     chan_key_grad = join_rows(ck_sum, team)[0].T.astype(f32)
     weight_g_grad = join_rows(gate_sum, team)[0].T.astype(f32)
-    mix_parts = jnp.concatenate([main_mix[:, 0], gate_mix[:, 0]], 0)
     ln1_gain_part = jnp.sum(grad_x1 * hat1, 0)
     ln1_bias_part = jnp.sum(grad_x1, 0)
     in_grad = grad_middle + norm_back(grad_x1, hat1, inv1, earlier_layernorm_scale)

time: 1390 us -> 1410 us (1.014)
  waiting for transfers between devices: 440 us -> 472 us
    ppermute x90, waiting for transfers between devices: 328 us -> 383 us  [swap(): return lax.ppermute(value, axis, [(0, 1), (1, 0)])]
    ppermute x11, waiting for transfers between devices: 59.6 us -> 13.7 us  [send_far(): return lax.ppermute(value, team, [(i, 3 - i) for i in range(4)])]
    reduce_scatter x1, waiting for transfers between devices: 0.01 us -> 18.7 us  [on_device(): sides = lax.psum_scatter(sides, spread, scatter_dimension=0, tiled=False)]
    unnamed x319 -> x285, local copies, waits for them, and re-layouts: 44.1 us -> 35.8 us
  transfers between devices with their start and end apart: 132 -> 132, of which waited for: 51 -> 51; matrix products, arithmetic and copies ran while one was open for 26% -> 24% of each run, Pallas kernels for 26% -> 24%
where the time goes in v3:
time: 1410 us; the launch traced here: 1390 us
  waiting for transfers between devices  472 us (33%)
  Pallas kernels  350 us (25%)
  other arithmetic  167 us (12%)
  local copies, waits for them, and re-layouts  142 us (10%)
  matrix products  124 us (9%)
  starting transfers between devices  120 us (9%)
  between operations  19 us (1%)
    ppermute x90, waiting for transfers between devices, swap(): return lax.ppermute(value, axis, [(0, 1), (1, 0)])  383 us
    ppermute x90, starting transfers between devices, swap(): return lax.ppermute(value, axis, [(0, 1), (1, 0)])  72.1 us
    dot_general x10, matrix products, nt(): lax.dot_general(left, right, (((1,), (1,)), ((), ())), preferred_element_...  72 us
    pallas_call x4, Pallas kernels, project_back(): pl.pallas_call(project_back_kernel, grid_spec=spec, out_shape=sds((2, tok...  57.5 us
    pallas_call x2, Pallas kernels, mix_weight_grads(): pl.pallas_call(functools.partial(mix_weight_kernel, count), grid_spec=spe...  56.1 us
    dot_general x10, matrix products, nn(): return jnp.dot(left, right, preferred_element_type=f32)  52.1 us
    pallas_call x2, Pallas kernels, outer_grads(): pl.pallas_call(functools.partial(outer_kernel, count), grid=(groups, tile...  50.4 us
    pallas_call x1, Pallas kernels, project(): pl.pallas_call(project_kernel, grid_spec=spec, out_shape=[sds((3, segs, 2...  50.2 us
  transfers between devices with their start and end apart: 132, of which 51 were waited for; matrix products, arithmetic and copies ran while one was open for 24% of the time, Pallas kernels for 24%

profile of v3, /device:TPU:0, one launch (start us, length us, event | category | flops | bytes accessed | tf_op | source)
XLA Modules:
  0.0 1394.2 jit_solution(17246782110410618327)
XLA Ops:
  23.6 7.1 collective-permute-done.11
  38.0 7.9 collective-permute-done.34
  73.2 43.0 %collective-permute-done.23 = bf16[1,2048]{1,0:T(2,128)(2,1)S(1)} collective-permute-done((bf16[1,2048]{1,0:T(2,128)(2,1)S(1)}, bf16[1,2048]{1,0:T(2,128)(2,1)S(1)}, u32[]{:S(2)}, u32[]{:S(2)}) %collective-permute-start.23) | collective-permute-done | bytes 4128 | tf_op jit(solution)/shard_map/ppermute | solution.py:756
  134.8 16.9 %collective-permute-done.7 = f32[4,64,64]{2,1,0:T(8,128)S(1)} collective-permute-done((f32[4,64,64]{2,1,0:T(8,128)S(1)}, f32[4,64,64]{2,1,0:T(8,128)S(1)}, u32[]{:S(2)}, u32[]{:S(2)}) %collective-permute-start.7) | collective-permute-done | bytes 65568 | tf_op jit(solution)/shard_map/ppermute | solution.py:923
  180.8 7.0 pad_maximum_fusion.x_ref.refs_2_.refs_4_
  187.9 11.2 place_mix.1.w_ref
  199.0 50.2 %project.1 = (bf16[3,4,1024,256]{3,2,1,0:T(8,128)(2,1)}, f32[4,1024,256]{2,1,0:T(8,128)}) custom-call(s32[1]{0:T(128)} %bitcast.28.core_ref, bf16[4,2,512,2048]{3,2,1,0:T(8,128)(2,1)} %pad_maximum_fusion.x_ref.refs_2_.refs_4_, bf16[4,8,2048]{2,1,0:T(8,128)(2,1)} %pad_maximum_fusion.22.halo_ref, bf16[2,4,256,2048]{3,2,1,0:T(8,128)(2,1)} %place_mix.1.w_ref), custom_call_target="tpu_custom_call" | custom-call | flops 149999992832 | tf_op jit(solution)/shard_map/project/pallas_call | solution.py:383
  269.3 13.6 collective-permute-done.26
  283.9 19.7 %mix_forward.1 = (bf16[4,1024,256]{2,1,0:T(8,128)(2,1)}, f32[4,1024,256]{2,1,0:T(8,128)}, f32[4,4,64,256]{3,2,1,0:T(8,128)}) custom-call(f32[1,256]{1,0:T(1,128)} %exp.39.rate_ref, f32[1,256]{1,0:T(1,128)} %squeeze.198.boost_ref, f32[1,256]{1,0:T(1,128)} %squeeze.199.gain_ref, f32[1,256]{1,0:T(1,128)} %squeeze.200.bias_ref, ...), custom_call_target="tpu_custom_call" | custom-call | flops 60000002048 | tf_op jit(solution)/shard_map/mix_forward/pallas_call | solution.py:272
  309.6 20.1 %collective-permute-done.30 = bf16[1024,256]{1,0:T(8,128)(2,1)S(1)} collective-permute-done((bf16[1024,256]{1,0:T(8,128)(2,1)}, bf16[1024,256]{1,0:T(8,128)(2,1)S(1)}, u32[]{:S(2)}, u32[]{:S(2)}) %collective-permute-start.30) | collective-permute-done | bytes 524320 | tf_op jit(solution)/shard_map/ppermute | solution.py:756
  342.0 9.7 place_emission.1
  351.7 7.0 fusion.119
  379.0 53.2 %collective-permute-done.36 = bf16[512,2048]{1,0:T(8,128)(2,1)} collective-permute-done((bf16[512,2048]{1,0:T(8,128)(2,1)S(1)}, bf16[512,2048]{1,0:T(8,128)(2,1)}, u32[]{:S(2)}, u32[]{:S(2)}) %collective-permute-start.36) | collective-permute-done | bytes 2097184 | tf_op jit(solution)/shard_map/ppermute | solution.py:756
  443.7 8.4 multiply_convert_fusion.4
  506.1 20.3 %collective-permute-done.51 = bf16[256,2048]{1,0:T(8,128)(2,1)S(1)} collective-permute-done((bf16[256,2048]{1,0:T(8,128)(2,1)S(1)}, bf16[256,2048]{1,0:T(8,128)(2,1)S(1)}, u32[]{:S(2)}, u32[]{:S(2)}) %collective-permute-start.51) | collective-permute-done | bytes 1048608 | tf_op jit(solution)/shard_map/ppermute | solution.py:756
  541.7 7.6 place_accept.1
  549.2 7.0 fusion.120
  558.8 16.8 %collective-permute-done.54 = bf16[512,2048]{1,0:T(8,128)(2,1)S(1)} collective-permute-done((bf16[512,2048]{1,0:T(8,128)(2,1)}, bf16[512,2048]{1,0:T(8,128)(2,1)S(1)}, u32[]{:S(2)}, u32[]{:S(2)}) %collective-permute-start.54) | collective-permute-done | bytes 2097184 | tf_op jit(solution)/shard_map/ppermute | solution.py:756
  586.8 10.1 place_rows.5.refs_1_
  596.9 33.8 %collective-permute-done.56 = bf16[512,2048]{1,0:T(8,128)(2,1)S(1)} collective-permute-done((bf16[512,2048]{1,0:T(8,128)(2,1)S(1)}, bf16[512,2048]{1,0:T(8,128)(2,1)S(1)}, u32[]{:S(2)}, u32[]{:S(2)}) %collective-permute-start.56) | collective-permute-done | bytes 2097184 | tf_op jit(solution)/shard_map/ppermute | solution.py:756
  634.9 8.5 multiply_convert_fusion.3.refs_0_
  643.3 11.3 collective-permute-done.59
  657.3 9.8 multiply_convert_fusion.1.refs_2_
  677.1 8.5 multiply_convert_fusion.refs_3_
  717.6 17.9 %collective-permute-done.67 = bf16[256,2048]{1,0:T(8,128)(2,1)S(1)} collective-permute-done((bf16[256,2048]{1,0:T(8,128)(2,1)S(1)}, bf16[256,2048]{1,0:T(8,128)(2,1)S(1)}, u32[]{:S(2)}, u32[]{:S(2)}) %collective-permute-start.67) | collective-permute-done | bytes 1048608 | tf_op jit(solution)/shard_map/ppermute | solution.py:756
  759.3 25.3 %outer_grads.3 = bf16[1,4,4,1,224,512]{5,4,3,2,1,0:T(8,128)(2,1)} custom-call(bf16[1024,896]{1,0:T(8,128)(2,1)} %multiply_convert_fusion.3.refs_0_, bf16[1024,896]{1,0:T(8,128)(2,1)} %multiply_convert_fusion.2.refs_1_, bf16[1024,896]{1,0:T(8,128)(2,1)} %multiply_convert_fusion.1.refs_2_, bf16[1024,896]{1,0:T(8,128)(2,1)} %copy-done.110, ...), custom_call_target="tpu_custom_call" | custom-call | flops 9374999552 | tf_op jit(solution)/shard_map/outer_grads/pallas_call | solution.py:584
  784.6 25.1 %outer_grads.2 = bf16[1,4,4,1,224,512]{5,4,3,2,1,0:T(8,128)(2,1)} custom-call(bf16[1024,896]{1,0:T(8,128)(2,1)} %copy-done.103, bf16[1024,896]{1,0:T(8,128)(2,1)} %copy-done.105, bf16[1024,896]{1,0:T(8,128)(2,1)} %copy-done.104, bf16[1024,896]{1,0:T(8,128)(2,1)} %copy-done.106, bf16[1024,2048]{1,0:T(8,128)(2,1)} %pad_maximum_fusion.6.refs_4_, ...), custom_call_target="tpu_custom_call" | custom-call | flops 9374999552 | tf_op jit(solution)/shard_map/outer_grads/pallas_call | solution.py:584
  821.9 6.4 multiply_reduce_fusion.2
  832.8 9.3 convolution_convert_fusion.8
  867.6 10.4 collective-permute-done.74
  880.7 17.9 %gate_back.1 = (bf16[4,1024,256]{2,1,0:T(8,128)(2,1)}, bf16[4,1024,256]{2,1,0:T(8,128)(2,1)}, f32[4,64,256]{2,1,0:T(8,128)}, f32[4,1,2,256]{3,2,1,0:T(2,128)}) custom-call(f32[1,256]{1,0:T(1,128)} %exp.39.rate_ref, f32[1,256]{1,0:T(1,128)} %squeeze.199.gain_ref, f32[1,256]{1,0:T(1,128)} %squeeze.200.bias_ref, ...), custom_call_target="tpu_custom_call" | custom-call | flops 6750000128 | tf_op jit(solution)/shard_map/gate_back/pallas_call | solution.py:300
  904.7 17.0 %side_grads.1 = bf16[4,2,1024,1024]{3,2,1,0:T(8,128)(2,1)} custom-call(s32[2]{0:T(128)} %pad_add_fusion.where_ref, bf16[512,2048]{1,0:T(8,128)(2,1)} %tie.16.z_ref, bf16[512,2048]{1,0:T(8,128)(2,1)} %copy-done.21, bf16[512,2048]{1,0:T(8,128)(2,1)} %get-tuple-element.165.gr_ref, bf16[512,2048]{1,0:T(8,128)(2,1)} %get-tuple-element.61.cr_ref), custom_call_target="tpu_custom_call" | custom-call | flops 6375000064 | tf_op jit(solution)/shard_map/side_grads/pallas_call | solution.py:636
  922.3 16.8 %mix_weight_grads.2 = (bf16[1,4,4,1,64,512]{5,4,3,2,1,0:T(8,128)(2,1)}, f32[1,1,2048]{2,1,0:T(1,128)}) custom-call(s32[1]{0:T(128)} %bitcast.28.core_ref, bf16[4,1024,256]{2,1,0:T(8,128)(2,1)} %get-tuple-element.70.refs_0_.g_ref, bf16[4,1,8,256]{3,2,1,0:T(8,128)(2,1)} %pad.25.refs_1_, bf16[4,2,512,2048]{3,2,1,0:T(8,128)(2,1)} %pad_maximum_fusion.x_ref.refs_2_.refs_4_, ...), custom_call_target="tpu_custom_call" | custom-call | flops 4874999808 | tf_op jit(solution)/shard_map/mix_weight_grads/pallas_call | solution.py:526
  940.1 29.1 %mix_backward.1 = (bf16[4,1024,256]{2,1,0:T(8,128)(2,1)}, bf16[4,1024,256]{2,1,0:T(8,128)(2,1)}, bf16[4,1024,256]{2,1,0:T(8,128)(2,1)}, f32[4,1,2,256]{3,2,1,0:T(2,128)}) custom-call(f32[1,256]{1,0:T(1,128)} %exp.39.rate_ref, f32[1,256]{1,0:T(1,128)} %squeeze.198.boost_ref, f32[4,64,256]{2,1,0:T(8,128)} %tie.12.end_ref, ...), custom_call_target="tpu_custom_call" | custom-call | flops 10874999808 | tf_op jit(solution)/shard_map/mix_backward/pallas_call | solution.py:328
  979.0 14.3 %project_back.4 = bf16[2,512,2048]{2,1,0:T(8,128)(2,1)} custom-call(s32[1]{0:T(128)} %bitcast.28.core_ref, bf16[4,1024,256]{2,1,0:T(8,128)(2,1)} %get-tuple-element.74.r_ref.refs_0_, bf16[4,1024,256]{2,1,0:T(8,128)(2,1)} %get-tuple-element.75.k_ref.refs_1_, bf16[4,1024,256]{2,1,0:T(8,128)(2,1)} %get-tuple-element.76.v_ref.refs_2_, ...), custom_call_target="tpu_custom_call" | custom-call | flops 5249999872 | tf_op jit(solution)/shard_map/project_back/pallas_call | solution.py:429
  996.5 9.0 fusion.90
  1028.4 9.7 collective-permute-done.112
  1042.5 39.4 %mix_weight_grads.3 = (bf16[1,4,4,3,64,512]{5,4,3,2,1,0:T(8,128)(2,1)}, f32[3,1,2048]{2,1,0:T(1,128)}) custom-call(s32[1]{0:T(128)} %bitcast.28.core_ref, bf16[4,1024,256]{2,1,0:T(8,128)(2,1)} %tie.14.refs_0_, bf16[4,1024,256]{2,1,0:T(8,128)(2,1)} %get-tuple-element.75.k_ref.refs_1_, bf16[4,1024,256]{2,1,0:T(8,128)(2,1)} %get-tuple-element.76.v_ref.refs_2_, ...), custom_call_target="tpu_custom_call" | custom-call | flops 14625000448 | tf_op jit(solution)/shard_map/mix_weight_grads/pallas_call | solution.py:526
  1081.9 14.3 %project_back.6 = bf16[2,512,2048]{2,1,0:T(8,128)(2,1)} custom-call(s32[1]{0:T(128)} %bitcast.28.core_ref, bf16[4,1024,256]{2,1,0:T(8,128)(2,1)} %tie.15.r_ref.refs_0_, bf16[4,1024,256]{2,1,0:T(8,128)(2,1)} %get-tuple-element.75.k_ref.refs_1_, bf16[4,1024,256]{2,1,0:T(8,128)(2,1)} %get-tuple-element.76.v_ref.refs_2_, ...), custom_call_target="tpu_custom_call" | custom-call | flops 5249999872 | tf_op jit(solution)/shard_map/project_back/pallas_call | solution.py:429
  1099.4 14.5 %project_back.5 = bf16[2,512,2048]{2,1,0:T(8,128)(2,1)} custom-call(s32[1]{0:T(128)} %bitcast.28.core_ref, bf16[4,1024,256]{2,1,0:T(8,128)(2,1)} %tie.15.r_ref.refs_0_, bf16[4,1024,256]{2,1,0:T(8,128)(2,1)} %get-tuple-element.75.k_ref.refs_1_, bf16[4,1024,256]{2,1,0:T(8,128)(2,1)} %get-tuple-element.76.v_ref.refs_2_, ...), custom_call_target="tpu_custom_call" | custom-call | flops 5249999872 | tf_op jit(solution)/shard_map/project_back/pallas_call | solution.py:429
  1134.4 17.2 %collective-permute-done.85 = bf16[256,2048]{1,0:T(8,128)(2,1)S(1)} collective-permute-done((bf16[256,2048]{1,0:T(8,128)(2,1)S(1)}, bf16[256,2048]{1,0:T(8,128)(2,1)S(1)}, u32[]{:S(2)}, u32[]{:S(2)}) %collective-permute-start.85) | collective-permute-done | bytes 1048608 | tf_op jit(solution)/shard_map/ppermute | solution.py:756
  1180.1 13.5 collective-permute-done.88
  1199.7 14.3 %project_back.7 = bf16[2,512,2048]{2,1,0:T(8,128)(2,1)} custom-call(s32[1]{0:T(128)} %bitcast.28.core_ref, bf16[4,1024,256]{2,1,0:T(8,128)(2,1)} %tie.19.r_ref, bf16[4,1024,256]{2,1,0:T(8,128)(2,1)} %get-tuple-element.75.k_ref.refs_1_, bf16[4,1024,256]{2,1,0:T(8,128)(2,1)} %get-tuple-element.76.v_ref.refs_2_, ...), custom_call_target="tpu_custom_call" | custom-call | flops 5249999872 | tf_op jit(solution)/shard_map/project_back/pallas_call | solution.py:429
  1221.0 25.5 %collective-permute-done.118 = bf16[1,224,512]{2,1,0:T(8,128)(2,1)S(1)} collective-permute-done((bf16[1,224,512]{2,1,0:T(8,128)(2,1)S(1)}, bf16[1,224,512]{2,1,0:T(8,128)(2,1)S(1)}, u32[]{:S(2)}, u32[]{:S(2)}) %collective-permute-start.118) | collective-permute-done | bytes 229408 | tf_op jit(solution)/shard_map/ppermute | solution.py:756
  1257.1 6.3 fusion.12
  1266.5 34.7 %collective-permute-done.121 = bf16[1,224,512]{2,1,0:T(8,128)(2,1)S(1)} collective-permute-done((bf16[1,224,512]{2,1,0:T(8,128)(2,1)}, bf16[1,224,512]{2,1,0:T(8,128)(2,1)S(1)}, u32[]{:S(2)}, u32[]{:S(2)}) %collective-permute-start.121) | collective-permute-done | bytes 229408 | tf_op jit(solution)/shard_map/ppermute | solution.py:756
  1322.1 6.8 add_convert_fusion
  1365.5 18.7 %reduce-scatter.14.cloned.1.call-done = bf16[1,512,512]{2,1,0:T(8,128)(2,1)} async-done(((bf16[4,512,512]{2,1,0:T(8,128)(2,1)}), bf16[1,512,512]{2,1,0:T(8,128)(2,1)}) %reduce-scatter.14.cloned.1.call-update) | async-done | bytes 524304 | tf_op jit(solution)/shard_map/reduce_scatter | solution.py:1207
  (857 shorter events, 552.8 us)
Async XLA Ops:
  7.2 180.7 %all-gather.13.cloned.1.call-start = ((), (), s32[]{:S(2)}) async-start(), calls=%async_computation.12 | async-start | bytes 5242880 | tf_op jit(solution)/shard_map/all_gather | solution.py:904
  33.7 308.2 %all-gather.9.cloned.1.call-start = ((), (), s32[]{:S(2)}) async-start(), calls=%async_computation.5 | async-start | bytes 4587520 | tf_op jit(solution)/shard_map/all_gather | solution.py:904
  48.7 293.2 %all-gather.15.cloned.1.call-start = ((), (), s32[]{:S(2)}) async-start(), calls=%async_computation.13 | async-start | bytes 8650752 | tf_op jit(solution)/shard_map/all_gather | solution.py:1045
  58.0 62.4 %collective-permute-start.5 = (f32[64,64]{1,0:T(8,128)S(1)}, f32[64,64]{1,0:T(8,128)S(1)}, u32[]{:S(2)}, u32[]{:S(2)}) collective-permute-start(f32[64,64]{1,0:T(8,128)S(1)} %get-tuple-element.295), channel_id=1, source_target_pairs={{0,24},{8,16},{16,8},{24,0},{1,25},{9,17},{17,9},{25,1},{2,26},{10... | collective-permute-start | bytes 49160 | tf_op jit(solution)/shard_map/ppermute | solution.py:764
  60.5 314.1 %all-gather.11.cloned.1.call-start = ((), (), s32[]{:S(2)}) async-start(), calls=%async_computation.6 | async-start | bytes 4587520 | tf_op jit(solution)/shard_map/all_gather | solution.py:904
  63.5 58.5 %collective-permute-start.4 = (f32[64,64]{1,0:T(8,128)S(1)}, f32[64,64]{1,0:T(8,128)S(1)}, u32[]{:S(2)}, u32[]{:S(2)}) collective-permute-start(f32[64,64]{1,0:T(8,128)S(1)} %get-tuple-element.296), channel_id=1, source_target_pairs={{0,16},{16,0},{1,17},{17,1},{2,18},{18,2},{3,19},{19,3},{4,20},{20... | collective-permute-start | bytes 49160 | tf_op jit(solution)/shard_map/ppermute | solution.py:756
  68.0 60.2 %collective-permute-start.15 = (bf16[512,2048]{1,0:T(8,128)(2,1)S(1)}, bf16[512,2048]{1,0:T(8,128)(2,1)}, u32[]{:S(2)}, u32[]{:S(2)}) collective-permute-start(bf16[512,2048]{1,0:T(8,128)(2,1)S(1)} %copy-done.17), channel_id=1, source_target_pairs={{0,16},{16,0},{1,17},{17,1},{2,18},{18,2},{3,19},{19,3},{4,20},{20... | collective-permute-start | bytes 6291464 | tf_op jit(solution)/shard_map/ppermute | solution.py:756
  69.5 60.3 %collective-permute-start.13 = (bf16[512,2048]{1,0:T(8,128)(2,1)S(1)}, bf16[512,2048]{1,0:T(8,128)(2,1)}, u32[]{:S(2)}, u32[]{:S(2)}) collective-permute-start(bf16[512,2048]{1,0:T(8,128)(2,1)S(1)} %copy-done.17), channel_id=1, source_target_pairs={{0,8},{8,0},{1,9},{9,1},{2,10},{10,2},{3,11},{11,3},{4,12},{12,4},... | collective-permute-start | bytes 6291464 | tf_op jit(solution)/shard_map/ppermute | solution.py:756
  72.6 43.6 %collective-permute-start.23 = (bf16[1,2048]{1,0:T(2,128)(2,1)S(1)}, bf16[1,2048]{1,0:T(2,128)(2,1)S(1)}, u32[]{:S(2)}, u32[]{:S(2)}) collective-permute-start(bf16[1,2048]{1,0:T(2,128)(2,1)S(1)} %fusion.75), channel_id=1, source_target_pairs={{0,16},{16,0},{1,17},{17,1},{2,18},{18,2},{3,19},{19,3},{4,20},{20... | collective-permute-start | bytes 12296 | tf_op jit(solution)/shard_map/ppermute | solution.py:756
  120.4 35.8 %collective-permute-start.40 = (bf16[1,224,512]{2,1,0:T(8,128)(2,1)S(1)}, bf16[1,224,512]{2,1,0:T(8,128)(2,1)S(1)}, u32[]{:S(2)}, u32[]{:S(2)}) collective-permute-start(bf16[1,224,512]{2,1,0:T(8,128)(2,1)S(1)} %get-tuple-element.236), channel_id=1, source_target_pairs={{0,16},{16,0},{1,17},{17,1},{2,18},{18,2},{3,19},{19,3},{4,20},{20... | collective-permute-start | bytes 688136 | tf_op jit(solution)/shard_map/ppermute | solution.py:756
  262.0 279.7 %all-gather.17.cloned.1.call-start = ((), (), s32[]{:S(2)}) async-start(), calls=%async_computation.14 | async-start | bytes 8650752 | tf_op jit(solution)/shard_map/all_gather | solution.py:1046
  333.5 645.5 %reduce-scatter.6.cloned.1.call-start = ((), (), s32[]{:S(2)}) async-start(), calls=%async_computation.7 | async-start | bytes 4587520 | tf_op jit(solution)/shard_map/reduce_scatter | solution.py:911
  367.2 68.1 %collective-permute-start.43 = (bf16[512,2048]{1,0:T(8,128)(2,1)S(1)}, bf16[512,2048]{1,0:T(8,128)(2,1)}, u32[]{:S(2)}, u32[]{:S(2)}) collective-permute-start(bf16[512,2048]{1,0:T(8,128)(2,1)S(1)} %get-tuple-element.169), channel_id=1, source_target_pairs={{0,16},{16,0},{1,17},{17,1},{2,18},{18,2},{3,19},{19,3},{4,20},{20... | collective-permute-start | bytes 6291464 | tf_op jit(solution)/shard_map/ppermute | solution.py:756
  368.6 63.7 %collective-permute-start.36 = (bf16[512,2048]{1,0:T(8,128)(2,1)S(1)}, bf16[512,2048]{1,0:T(8,128)(2,1)}, u32[]{:S(2)}, u32[]{:S(2)}) collective-permute-start(bf16[512,2048]{1,0:T(8,128)(2,1)S(1)} %get-tuple-element.169), channel_id=1, source_target_pairs={{0,8},{8,0},{1,9},{9,1},{2,10},{10,2},{3,11},{11,3},{4,12},{12,4},... | collective-permute-start | bytes 6291464 | tf_op jit(solution)/shard_map/ppermute | solution.py:756
  370.1 73.6 %collective-permute-start.46 = (bf16[512,2048]{1,0:T(8,128)(2,1)S(1)}, bf16[512,2048]{1,0:T(8,128)(2,1)}, u32[]{:S(2)}, u32[]{:S(2)}) collective-permute-start(bf16[512,2048]{1,0:T(8,128)(2,1)S(1)} %get-tuple-element.169), channel_id=1, source_target_pairs={{0,1},{1,0},{2,3},{3,2},{4,5},{5,4},{6,7},{7,6},{8,9},{9,8},{10,11... | collective-permute-start | bytes 6291464 | tf_op jit(solution)/shard_map/ppermute | solution.py:756
  503.3 26.4 %collective-permute-start.49 = (bf16[256,2048]{1,0:T(8,128)(2,1)S(1)}, bf16[256,2048]{1,0:T(8,128)(2,1)S(1)}, u32[]{:S(2)}, u32[]{:S(2)}) collective-permute-start(bf16[256,2048]{1,0:T(8,128)(2,1)S(1)} %get-tuple-element.190), channel_id=1, source_target_pairs={{0,16},{16,0},{1,17},{17,1},{2,18},{18,2},{3,19},{19,3},{4,20},{20... | collective-permute-start | bytes 3145736 | tf_op jit(solution)/shard_map/ppermute | solution.py:756
  528.2 47.4 %collective-permute-start.54 = (bf16[512,2048]{1,0:T(8,128)(2,1)}, bf16[512,2048]{1,0:T(8,128)(2,1)S(1)}, u32[]{:S(2)}, u32[]{:S(2)}) collective-permute-start(bf16[512,2048]{1,0:T(8,128)(2,1)} %pad_maximum_fusion.11), channel_id=1, source_target_pairs={{0,16},{16,0},{1,17},{17,1},{2,18},{18,2},{3,19},{19,3},{4,20},{20... | collective-permute-start | bytes 6291464 | tf_op jit(solution)/shard_map/ppermute | solution.py:756
  531.5 47.3 %collective-permute-start.53 = (bf16[512,2048]{1,0:T(8,128)(2,1)}, bf16[512,2048]{1,0:T(8,128)(2,1)}, u32[]{:S(2)}, u32[]{:S(2)}) collective-permute-start(bf16[512,2048]{1,0:T(8,128)(2,1)} %pad_maximum_fusion.10), channel_id=1, source_target_pairs={{0,8},{8,0},{1,9},{9,1},{2,10},{10,2},{3,11},{11,3},{4,12},{12,4},... | collective-permute-start | bytes 6291464 | tf_op jit(solution)/shard_map/ppermute | solution.py:756
  584.7 46.0 %collective-permute-start.56 = (bf16[512,2048]{1,0:T(8,128)(2,1)S(1)}, bf16[512,2048]{1,0:T(8,128)(2,1)S(1)}, u32[]{:S(2)}, u32[]{:S(2)}) collective-permute-start(bf16[512,2048]{1,0:T(8,128)(2,1)S(1)} %get-tuple-element.167), channel_id=1, source_target_pairs={{0,8},{8,0},{1,9},{9,1},{2,10},{10,2},{3,11},{11,3},{4,12},{12,4},... | collective-permute-start | bytes 6291464 | tf_op jit(solution)/shard_map/ppermute | solution.py:756
  586.4 46.8 %collective-permute-start.60 = (bf16[512,2048]{1,0:T(8,128)(2,1)S(1)}, bf16[512,2048]{1,0:T(8,128)(2,1)S(1)}, u32[]{:S(2)}, u32[]{:S(2)}) collective-permute-start(bf16[512,2048]{1,0:T(8,128)(2,1)S(1)} %get-tuple-element.167), channel_id=1, source_target_pairs={{0,16},{16,0},{1,17},{17,1},{2,18},{18,2},{3,19},{19,3},{4,20},{20... | collective-permute-start | bytes 6291464 | tf_op jit(solution)/shard_map/ppermute | solution.py:756
  586.8 47.8 %collective-permute-start.55 = (bf16[512,2048]{1,0:T(8,128)(2,1)S(1)}, bf16[512,2048]{1,0:T(8,128)(2,1)}, u32[]{:S(2)}, u32[]{:S(2)}) collective-permute-start(bf16[512,2048]{1,0:T(8,128)(2,1)S(1)} %get-tuple-element.167), channel_id=1, source_target_pairs={{0,1},{1,0},{2,3},{3,2},{4,5},{5,4},{6,7},{7,6},{8,9},{9,8},{10,11... | collective-permute-start | bytes 6291464 | tf_op jit(solution)/shard_map/ppermute | solution.py:756
  709.8 25.6 %collective-permute-start.67 = (bf16[256,2048]{1,0:T(8,128)(2,1)S(1)}, bf16[256,2048]{1,0:T(8,128)(2,1)S(1)}, u32[]{:S(2)}, u32[]{:S(2)}) collective-permute-start(bf16[256,2048]{1,0:T(8,128)(2,1)S(1)} %get-tuple-element.189), channel_id=1, source_target_pairs={{0,8},{8,0},{1,9},{9,1},{2,10},{10,2},{3,11},{11,3},{4,12},{12,4},... | collective-permute-start | bytes 3145736 | tf_op jit(solution)/shard_map/ppermute | solution.py:756
  746.5 63.3 %collective-permute-start.68 = (bf16[512,2048]{1,0:T(8,128)(2,1)}, bf16[512,2048]{1,0:T(8,128)(2,1)}, u32[]{:S(2)}, u32[]{:S(2)}) collective-permute-start(bf16[512,2048]{1,0:T(8,128)(2,1)} %slice.1150), channel_id=1, source_target_pairs={{0,1},{1,0},{2,3},{3,2},{4,5},{5,4},{6,7},{7,6},{8,9},{9,8},{10,11... | collective-permute-start | bytes 6291464 | tf_op jit(solution)/shard_map/ppermute | solution.py:756
  756.8 56.2 %collective-permute-start.70 = (bf16[512,2048]{1,0:T(8,128)(2,1)}, bf16[512,2048]{1,0:T(8,128)(2,1)S(1)}, u32[]{:S(2)}, u32[]{:S(2)}) collective-permute-start(bf16[512,2048]{1,0:T(8,128)(2,1)} %pad_maximum_fusion.14), channel_id=1, source_target_pairs={{0,16},{16,0},{1,17},{17,1},{2,18},{18,2},{3,19},{19,3},{4,20},{20... | collective-permute-start | bytes 6291464 | tf_op jit(solution)/shard_map/ppermute | solution.py:756
  758.5 54.5 %collective-permute-start.69 = (bf16[512,2048]{1,0:T(8,128)(2,1)}, bf16[512,2048]{1,0:T(8,128)(2,1)}, u32[]{:S(2)}, u32[]{:S(2)}) collective-permute-start(bf16[512,2048]{1,0:T(8,128)(2,1)} %pad_maximum_fusion.13), channel_id=1, source_target_pairs={{0,8},{8,0},{1,9},{9,1},{2,10},{10,2},{3,11},{11,3},{4,12},{12,4},... | collective-permute-start | bytes 6291464 | tf_op jit(solution)/shard_map/ppermute | solution.py:756
  847.6 276.4 %reduce-scatter.10.cloned.1.call-start = ((), (), s32[]{:S(2)}) async-start(), calls=%async_computation.9 | async-start | bytes 1310720 | tf_op jit(solution)/shard_map/reduce_scatter | solution.py:911
  899.6 39.5 %collective-permute-start.76 = (bf16[4,64,256]{2,1,0:T(8,128)(2,1)S(1)}, bf16[4,64,256]{2,1,0:T(8,128)(2,1)S(1)}, u32[]{:S(2)}, u32[]{:S(2)}) collective-permute-start(bf16[4,64,256]{2,1,0:T(8,128)(2,1)S(1)} %get-tuple-element.153), channel_id=1, source_target_pairs={{2,0},{4,2},{6,4},{0,6},{3,1},{5,3},{7,5},{1,7},{10,8},{12,10},{14... | collective-permute-start | bytes 393224 | tf_op jit(solution)/shard_map/ppermute | solution.py:923
  900.1 39.0 %collective-permute-start.77 = (bf16[4,64,256]{2,1,0:T(8,128)(2,1)S(1)}, bf16[4,64,256]{2,1,0:T(8,128)(2,1)S(1)}, u32[]{:S(2)}, u32[]{:S(2)}) collective-permute-start(bf16[4,64,256]{2,1,0:T(8,128)(2,1)S(1)} %get-tuple-element.153), channel_id=1, source_target_pairs={{4,0},{6,2},{0,4},{2,6},{5,1},{7,3},{1,5},{3,7},{12,8},{14,10},{8,... | collective-permute-start | bytes 393224 | tf_op jit(solution)/shard_map/ppermute | solution.py:923
  902.2 36.9 %collective-permute-start.78 = (bf16[4,64,256]{2,1,0:T(8,128)(2,1)S(1)}, bf16[4,64,256]{2,1,0:T(8,128)(2,1)S(1)}, u32[]{:S(2)}, u32[]{:S(2)}) collective-permute-start(bf16[4,64,256]{2,1,0:T(8,128)(2,1)S(1)} %get-tuple-element.153), channel_id=1, source_target_pairs={{6,0},{0,2},{2,4},{4,6},{7,1},{1,3},{3,5},{5,7},{14,8},{8,10},{10,... | collective-permute-start | bytes 393224 | tf_op jit(solution)/shard_map/ppermute | solution.py:923
  996.5 42.3 %collective-permute-start.81 = (bf16[512,2048]{1,0:T(8,128)(2,1)}, bf16[512,2048]{1,0:T(8,128)(2,1)S(1)}, u32[]{:S(2)}, u32[]{:S(2)}) collective-permute-start(bf16[512,2048]{1,0:T(8,128)(2,1)} %slice_bitcast_fusion.8), channel_id=1, source_target_pairs={{0,1},{1,0},{2,3},{3,2},{4,5},{5,4},{6,7},{7,6},{8,9},{9,8},{10,11... | collective-permute-start | bytes 6291464 | tf_op jit(solution)/shard_map/ppermute | solution.py:756
  1015.0 202.2 %reduce-scatter.8.cloned.1.call-start = ((), (), s32[]{:S(2)}) async-start(), calls=%async_computation.8 | async-start | bytes 4587520 | tf_op jit(solution)/shard_map/reduce_scatter | solution.py:911
  1015.4 104.1 %collective-permute-start.87 = (bf16[1024,1024]{1,0:T(8,128)(2,1)}, bf16[1024,1024]{1,0:T(8,128)(2,1)}, u32[]{:S(2)}, u32[]{:S(2)}) collective-permute-start(bf16[1024,1024]{1,0:T(8,128)(2,1)} %slice_bitcast_fusion.2), channel_id=1, source_target_pairs={{0,1},{1,0},{2,3},{3,2},{4,5},{5,4},{6,7},{7,6},{8,9},{9,8},{10,11... | collective-permute-start | bytes 6291464 | tf_op jit(solution)/shard_map/ppermute | solution.py:756
  1099.4 28.6 %collective-permute-start.84 = (bf16[512,2048]{1,0:T(8,128)(2,1)}, bf16[512,2048]{1,0:T(8,128)(2,1)}, u32[]{:S(2)}, u32[]{:S(2)}) collective-permute-start(bf16[512,2048]{1,0:T(8,128)(2,1)} %slice_bitcast_fusion.4), channel_id=1, source_target_pairs={{0,1},{1,0},{2,3},{3,2},{4,5},{5,4},{6,7},{7,6},{8,9},{9,8},{10,11... | collective-permute-start | bytes 6291464 | tf_op jit(solution)/shard_map/ppermute | solution.py:756
  1126.2 221.7 %reduce-scatter.12.cloned.1.call-start = ((), (), s32[]{:S(2)}) async-start(), calls=%async_computation.10 | async-start | bytes 3932160 | tf_op jit(solution)/shard_map/reduce_scatter | solution.py:911
  1126.6 26.9 %collective-permute-start.83 = (bf16[256,2048]{1,0:T(8,128)(2,1)S(1)}, bf16[256,2048]{1,0:T(8,128)(2,1)S(1)}, u32[]{:S(2)}, u32[]{:S(2)}) collective-permute-start(bf16[256,2048]{1,0:T(8,128)(2,1)S(1)} %get-tuple-element.174), channel_id=1, source_target_pairs={{0,16},{16,0},{1,17},{17,1},{2,18},{18,2},{3,19},{19,3},{4,20},{20... | collective-permute-start | bytes 3145736 | tf_op jit(solution)/shard_map/ppermute | solution.py:756
  1167.1 26.4 %collective-permute-start.88 = (bf16[512,1024]{1,0:T(8,128)(2,1)}, bf16[512,1024]{1,0:T(8,128)(2,1)}, u32[]{:S(2)}, u32[]{:S(2)}) collective-permute-start(bf16[512,1024]{1,0:T(8,128)(2,1)} %get-tuple-element.173), channel_id=1, source_target_pairs={{0,16},{16,0},{1,17},{17,1},{2,18},{18,2},{3,19},{19,3},{4,20},{20... | collective-permute-start | bytes 3145736 | tf_op jit(solution)/shard_map/ppermute | solution.py:756
  1169.3 27.3 %collective-permute-start.90 = (bf16[512,1024]{1,0:T(8,128)(2,1)S(1)}, bf16[512,1024]{1,0:T(8,128)(2,1)}, u32[]{:S(2)}, u32[]{:S(2)}) collective-permute-start(bf16[512,1024]{1,0:T(8,128)(2,1)S(1)} %get-tuple-element.172), channel_id=1, source_target_pairs={{0,8},{8,0},{1,9},{9,1},{2,10},{10,2},{3,11},{11,3},{4,12},{12,4},... | collective-permute-start | bytes 3145736 | tf_op jit(solution)/shard_map/ppermute | solution.py:756
  1171.9 81.6 %collective-permute-start.93 = (bf16[512,2048]{1,0:T(8,128)(2,1)}, bf16[512,2048]{1,0:T(8,128)(2,1)}, u32[]{:S(2)}, u32[]{:S(2)}) collective-permute-start(bf16[512,2048]{1,0:T(8,128)(2,1)} %pad_maximum_fusion.17.refs_2_), channel_id=1, source_target_pairs={{0,16},{16,0},{1,17},{17,1},{2,18},{18,2},{3,19},{19,3},{4,20},{20... | collective-permute-start | bytes 6291464 | tf_op jit(solution)/shard_map/ppermute | solution.py:756
  1172.7 82.1 %collective-permute-start.92 = (bf16[512,2048]{1,0:T(8,128)(2,1)}, bf16[512,2048]{1,0:T(8,128)(2,1)}, u32[]{:S(2)}, u32[]{:S(2)}) collective-permute-start(bf16[512,2048]{1,0:T(8,128)(2,1)} %pad_maximum_fusion.16.refs_1_), channel_id=1, source_target_pairs={{0,8},{8,0},{1,9},{9,1},{2,10},{10,2},{3,11},{11,3},{4,12},{12,4},... | collective-permute-start | bytes 6291464 | tf_op jit(solution)/shard_map/ppermute | solution.py:756
  1217.1 39.6 %collective-permute-start.91 = (bf16[512,2048]{1,0:T(8,128)(2,1)}, bf16[512,2048]{1,0:T(8,128)(2,1)}, u32[]{:S(2)}, u32[]{:S(2)}) collective-permute-start(bf16[512,2048]{1,0:T(8,128)(2,1)} %slice_bitcast_fusion), channel_id=1, source_target_pairs={{0,1},{1,0},{2,3},{3,2},{4,5},{5,4},{6,7},{7,6},{8,9},{9,8},{10,11... | collective-permute-start | bytes 6291464 | tf_op jit(solution)/shard_map/ppermute | solution.py:756
  1217.2 167.0 %reduce-scatter.14.cloned.1.call-start = ((), (), s32[]{:S(2)}) async-start(), calls=%async_computation.11 | async-start | bytes 2621440 | tf_op jit(solution)/shard_map/reduce_scatter | solution.py:1207
  1218.9 27.6 %collective-permute-start.118 = (bf16[1,224,512]{2,1,0:T(8,128)(2,1)S(1)}, bf16[1,224,512]{2,1,0:T(8,128)(2,1)S(1)}, u32[]{:S(2)}, u32[]{:S(2)}) collective-permute-start(bf16[1,224,512]{2,1,0:T(8,128)(2,1)S(1)} %get-tuple-element.226), channel_id=1, source_target_pairs={{0,16},{16,0},{1,17},{17,1},{2,18},{18,2},{3,19},{19,3},{4,20},{20... | collective-permute-start | bytes 688136 | tf_op jit(solution)/shard_map/ppermute | solution.py:756
  1220.8 26.9 %collective-permute-start.117 = (bf16[1,224,512]{2,1,0:T(8,128)(2,1)S(1)}, bf16[1,224,512]{2,1,0:T(8,128)(2,1)S(1)}, u32[]{:S(2)}, u32[]{:S(2)}) collective-permute-start(bf16[1,224,512]{2,1,0:T(8,128)(2,1)S(1)} %get-tuple-element.227), channel_id=1, source_target_pairs={{0,24},{8,16},{16,8},{24,0},{1,25},{9,17},{17,9},{25,1},{2,26},{10... | collective-permute-start | bytes 688136 | tf_op jit(solution)/shard_map/ppermute | solution.py:764
  1247.7 74.3 %collective-permute-start.115 = (bf16[1024,1024]{1,0:T(8,128)(2,1)}, bf16[1024,1024]{1,0:T(8,128)(2,1)}, u32[]{:S(2)}, u32[]{:S(2)}) collective-permute-start(bf16[1024,1024]{1,0:T(8,128)(2,1)} %pad_maximum_fusion.19.refs_4_), channel_id=1, source_target_pairs={{0,16},{16,0},{1,17},{17,1},{2,18},{18,2},{3,19},{19,3},{4,20},{20... | collective-permute-start | bytes 6291464 | tf_op jit(solution)/shard_map/ppermute | solution.py:756
  1252.5 69.5 %collective-permute-start.114 = (bf16[1024,1024]{1,0:T(8,128)(2,1)}, bf16[1024,1024]{1,0:T(8,128)(2,1)}, u32[]{:S(2)}, u32[]{:S(2)}) collective-permute-start(bf16[1024,1024]{1,0:T(8,128)(2,1)} %pad_maximum_fusion.18.refs_3_), channel_id=1, source_target_pairs={{0,8},{8,0},{1,9},{9,1},{2,10},{10,2},{3,11},{11,3},{4,12},{12,4},... | collective-permute-start | bytes 6291464 | tf_op jit(solution)/shard_map/ppermute | solution.py:756
  1253.5 47.7 %collective-permute-start.121 = (bf16[1,224,512]{2,1,0:T(8,128)(2,1)}, bf16[1,224,512]{2,1,0:T(8,128)(2,1)S(1)}, u32[]{:S(2)}, u32[]{:S(2)}) collective-permute-start(bf16[1,224,512]{2,1,0:T(8,128)(2,1)} %get-tuple-element.215), channel_id=1, source_target_pairs={{0,16},{16,0},{1,17},{17,1},{2,18},{18,2},{3,19},{19,3},{4,20},{20... | collective-permute-start | bytes 688136 | tf_op jit(solution)/shard_map/ppermute | solution.py:756
  1254.8 51.0 %collective-permute-start.120 = (bf16[1,224,512]{2,1,0:T(8,128)(2,1)}, bf16[1,224,512]{2,1,0:T(8,128)(2,1)}, u32[]{:S(2)}, u32[]{:S(2)}) collective-permute-start(bf16[1,224,512]{2,1,0:T(8,128)(2,1)} %get-tuple-element.216), channel_id=1, source_target_pairs={{0,24},{8,16},{16,8},{24,0},{1,25},{9,17},{17,9},{25,1},{2,26},{10... | collective-permute-start | bytes 688136 | tf_op jit(solution)/shard_map/ppermute | solution.py:764
  1256.7 51.3 %collective-permute-start.119 = (bf16[1,224,512]{2,1,0:T(8,128)(2,1)}, bf16[1,224,512]{2,1,0:T(8,128)(2,1)}, u32[]{:S(2)}, u32[]{:S(2)}) collective-permute-start(bf16[1,224,512]{2,1,0:T(8,128)(2,1)} %get-tuple-element.214), channel_id=1, source_target_pairs={{0,8},{8,0},{1,9},{9,1},{2,10},{10,2},{3,11},{11,3},{4,12},{12,4},... | collective-permute-start | bytes 688136 | tf_op jit(solution)/shard_map/ppermute | solution.py:756
  (207 other events, 2192.9 us)
Sparse Core Ops, SparseCore 0:
  33.8 82.3 all-gather.12
  117.8 78.5 all-gather.8
  199.4 84.9 all-gather.14
  286.3 69.6 all-gather.10
  358.9 95.0 all-gather.16
  847.7 74.2 reduce-scatter.5
  1015.1 28.0 reduce-scatter.9
  1126.3 65.5 reduce-scatter.7
  1217.3 57.9 reduce-scatter.11
  1341.2 42.9 reduce-scatter.13
